TPU v7x, 32 devices: a whole 2x2x4 slice. The times are simulated.
32 devices in a mesh: wide: 8 (over y, x, core), narrow: 4 (over z).
Axes of the slice: x: 2, y: 2, z: 4, core: 2. Of those that a mesh axis runs over, the one named last changes fastest.
Arguments:
- hidden_in: bfloat16 [2, 32, 512, 768], P(None, ('wide', 'narrow')), may hold values from -6 to 6
- cotangent: bfloat16 [2, 32, 512, 768], P(None, ('wide', 'narrow')), may hold values from -6 to 6
- seq_lengths: int32 [2, 32], P(None, ('wide', 'narrow')), may hold values from 64 to 512, as said below
- query_weight: bfloat16 [768, 768], P(('wide', 'narrow')), may hold values from -0.21875 to 0.21875
- query_bias: bfloat16 [768], P(('wide', 'narrow')), may hold values from -3 to 3
- key_weight: bfloat16 [768, 768], P(('wide', 'narrow')), may hold values from -0.21875 to 0.21875
- key_bias: bfloat16 [768], P(('wide', 'narrow')), may hold values from -3 to 3
- value_weight: bfloat16 [768, 768], P(('wide', 'narrow')), may hold values from -0.21875 to 0.21875
- value_bias: bfloat16 [768], P(('wide', 'narrow')), may hold values from -3 to 3
- out_weight: bfloat16 [768, 768], P(('wide', 'narrow')), may hold values from -0.875 to 0.875
- out_bias: bfloat16 [768], P(('wide', 'narrow')), may hold values from -3 to 3
- first_gain: bfloat16 [768], P(('wide', 'narrow')), may hold values from 0.5 to 1.5
- first_shift: bfloat16 [768], P(('wide', 'narrow')), may hold values from -3 to 3
- up_weight: bfloat16 [768, 3072], P(('wide', 'narrow')), may hold values from -0.21875 to 0.21875
- up_bias: bfloat16 [3072], P(('wide', 'narrow')), may hold values from -3 to 3
- down_weight: bfloat16 [3072, 768], P(('wide', 'narrow')), may hold values from -0.109375 to 0.109375
- down_bias: bfloat16 [768], P(('wide', 'narrow')), may hold values from -3 to 3
- second_gain: bfloat16 [768], P(('wide', 'narrow')), may hold values from 0.5 to 1.5
- second_shift: bfloat16 [768], P(('wide', 'narrow')), may hold values from -3 to 3
- rel_table: bfloat16 [512, 768], P(None, ('wide', 'narrow')), may hold values from -6 to 6
Outputs:
- hidden_out: bfloat16 [2, 32, 512, 768], P(None, ('wide', 'narrow'))
- grad_hidden_in: float32 [2, 32, 512, 768], P(None, ('wide', 'narrow'))
- grad_query_weight: float32 [768, 768], P(('wide', 'narrow'))
- grad_query_bias: float32 [768], P(('wide', 'narrow'))
- grad_key_weight: float32 [768, 768], P(('wide', 'narrow'))
- grad_key_bias: float32 [768], P(('wide', 'narrow'))
- grad_value_weight: float32 [768, 768], P(('wide', 'narrow'))
- grad_value_bias: float32 [768], P(('wide', 'narrow'))
- grad_out_weight: float32 [768, 768], P(('wide', 'narrow'))
- grad_out_bias: float32 [768], P(('wide', 'narrow'))
- grad_first_gain: float32 [768], P(('wide', 'narrow'))
- grad_first_shift: float32 [768], P(('wide', 'narrow'))
- grad_up_weight: float32 [768, 3072], P(('wide', 'narrow'))
- grad_up_bias: float32 [3072], P(('wide', 'narrow'))
- grad_down_weight: float32 [3072, 768], P(('wide', 'narrow'))
- grad_down_bias: float32 [768], P(('wide', 'narrow'))
- grad_second_gain: float32 [768], P(('wide', 'narrow'))
- grad_second_shift: float32 [768], P(('wide', 'narrow'))
- grad_rel_table: float32 [512, 768], P(None, ('wide', 'narrow'))
Inputs may be any that keep to these rules, and one draw needn't show every extreme that they name: `seq_lengths`: each sequence's live length; key slots at or past it are padding.
All inputs are finite; a program needn't handle non-finite values.
Results may differ from a plain program's by a relative error of at most 0.04.
Values may be sent and summed in bfloat16 or wider, within the bound.
No kernel may reach another device: no remote copies, remote signals or barrier semaphores. Data moves between devices by JAX's collectives and lax.ppermute only.
A program may use at most 256 MiB of HBM per device.

v0:
```python
import functools
import math

import jax
import jax.numpy as jnp
from jax import lax
from jax.experimental import pallas as pl
from jax.experimental.pallas import tpu as pltpu
from jax.sharding import PartitionSpec as P

D = 768
HEADS = 12
HEAD = 64
SEQ = 512
MICRO = 2
PAIR = 2 * HEAD
PAIRS = HEADS // 2
CHUNK = 128
VECTORS = 256
SCALE = 1.0 / math.sqrt(3 * HEAD)
AXES = ("wide", "narrow")
norm_epsilon = 1e-06
bf16 = jnp.bfloat16
f32 = jnp.float32


def dot_nt(left, right):
    return lax.dot_general(left, right, (((1,), (1,)), ((), ())), preferred_element_type=f32)


def dot_nn(left, right):
    return lax.dot_general(left, right, (((1,), (0,)), ((), ())), preferred_element_type=f32)


def dot_tn(left, right):
    return lax.dot_general(left, right, (((0,), (0,)), ((), ())), preferred_element_type=f32)


def reverse_rows(flip, block):
    half = SEQ // 2
    return jnp.concatenate(
        [dot_nn(flip, block[half:]).astype(bf16), dot_nn(flip, block[:half]).astype(bf16)], axis=0
    )


def flip_matrix():
    half = SEQ // 2
    rows = lax.broadcasted_iota(jnp.int32, (half, half), 0)
    cols = lax.broadcasted_iota(jnp.int32, (half, half), 1)
    return jnp.where(rows + cols == half - 1, 1.0, 0.0).astype(bf16)


def skew(rows, base):
    return pltpu.roll(rows, base % SEQ, 1, stride=1, stride_axis=0)


def attend_kernel(len_ref, q_ref, k_ref, v_ref, pq_ref, pk_ref, ctx_ref, probs_ref, back_ref):
    length = len_ref[pl.program_id(1)]
    flip = flip_matrix()
    lane_pair = lax.broadcasted_iota(jnp.int32, (1, PAIR), 1)
    rows = lax.broadcasted_iota(jnp.int32, (CHUNK, SEQ), 0)
    cols = lax.broadcasted_iota(jnp.int32, (CHUNK, SEQ), 1)
    eye = jnp.where(
        lax.broadcasted_iota(jnp.int32, (CHUNK, CHUNK), 0)
        == lax.broadcasted_iota(jnp.int32, (CHUNK, CHUNK), 1),
        1.0,
        0.0,
    ).astype(bf16)
    key_valid = cols[:1] < length
    q_all, k_all, v_all = q_ref[...], k_ref[...], v_ref[...]
    pq_all = pq_ref[...]
    pk_flipped = reverse_rows(flip, pk_ref[...])
    for head in range(2):
        mine = (lane_pair >= head * HEAD) & (lane_pair < (head + 1) * HEAD)
        q_head = jnp.where(mine, q_all, jnp.zeros_like(q_all))
        k_head = jnp.where(mine, k_all, jnp.zeros_like(k_all))
        for c in range(SEQ // CHUNK):
            part = slice(c * CHUNK, (c + 1) * CHUNK)
            table = dot_nt(k_head[part], pq_all).astype(bf16)
            moved = skew(table, c * CHUNK + 256)
            place = cols - rows - c * CHUNK + 256
            moved = jnp.where(place < 0, table[:, :1], moved)
            moved = jnp.where(place > SEQ - 1, table[:, SEQ - 1 :], moved)
            back_ref[part, :] = moved
        for c in range(SEQ // CHUNK):
            part = slice(c * CHUNK, (c + 1) * CHUNK)
            raw = dot_nt(
                jnp.concatenate([q_head[part], eye], axis=1),
                jnp.concatenate([k_all, back_ref[:, part]], axis=1),
            )
            table = dot_nt(q_head[part], pk_flipped).astype(bf16)
            moved = skew(table, c * CHUNK - 255)
            place = cols - rows - c * CHUNK + 255
            moved = jnp.where(place < 0, table[:, :1], moved)
            moved = jnp.where(place > SEQ - 1, table[:, SEQ - 1 :], moved)
            scores = jnp.where(key_valid, (raw + moved.astype(f32)) * SCALE, -1000000000.0)
            row_max = jnp.max(scores, axis=1, keepdims=True)
            exp_scores = jnp.exp(scores - row_max)
            row_total = jnp.sum(exp_scores, axis=1, keepdims=True)
            probs = (exp_scores * (1.0 / row_total)).astype(bf16)
            context = dot_nn(probs, v_all).astype(bf16)
            if head == 0:
                ctx_ref[part, :] = context
            else:
                ctx_ref[part, :] = jnp.where(mine, context, ctx_ref[part, :])
            half = SEQ // 2
            probs_ref[0, head, part, :half] = dot_nn(probs[:, half:], flip).astype(bf16)
            probs_ref[0, head, part, half:] = dot_nn(probs[:, :half], flip).astype(bf16)


def attend(lengths, qkv, pos):
    qkv_block = lambda which: pl.BlockSpec((SEQ, PAIR), lambda p, s, n: (s, which * PAIRS + p))
    pos_block = lambda which: pl.BlockSpec((SEQ, PAIR), lambda p, s, n: (0, which * PAIRS + p))
    return pl.pallas_call(
        attend_kernel,
        grid_spec=pltpu.PrefetchScalarGridSpec(
            num_scalar_prefetch=1,
            grid=(PAIRS, MICRO),
            in_specs=[qkv_block(0), qkv_block(1), qkv_block(2), pos_block(0), pos_block(1)],
            out_specs=[
                pl.BlockSpec((SEQ, PAIR), lambda p, s, n: (s, p)),
                pl.BlockSpec((1, 2, SEQ, SEQ), lambda p, s, n: (s, p, 0, 0)),
            ],
            scratch_shapes=[pltpu.VMEM((SEQ, SEQ), bf16)],
        ),
        out_shape=[
            jax.ShapeDtypeStruct((MICRO * SEQ, D), bf16),
            jax.ShapeDtypeStruct((MICRO, HEADS, SEQ, SEQ), bf16),
        ],
        compiler_params=pltpu.CompilerParams(vmem_limit_bytes=40 * 2**20),
        cost_estimate=pl.CostEstimate(
            flops=24 * 8 * 2 * SEQ * SEQ * PAIR,
            bytes_accessed=20 * 2**20,
            transcendentals=24 * SEQ * SEQ,
        ),
        name="attend",
    )(lengths, qkv, qkv, qkv, pos, pos)


def fold_edges(moved, c, rows, cols):
    first = c * CHUNK
    place = rows + first
    inside = (cols >= place - 255) & (cols <= place + 256)
    kept = jnp.where(inside, moved, jnp.zeros_like(moved))
    outside = jnp.where(inside, jnp.zeros_like(moved), moved)
    half = SEQ // 2
    region = outside[:, half:] if first < half else outside[:, :half]
    edge_sum = jnp.sum(region.astype(f32), axis=1, keepdims=True)
    edge = 0 if first < half else SEQ - 1
    return jnp.where(cols == edge, kept.astype(f32) + edge_sum, kept.astype(f32)).astype(bf16)


def attend_back_kernel(
    q_ref, k_ref, v_ref, pq_ref, pk_ref, gc_ref, probs_ref,
    gq_ref, gk_ref, gv_ref, gpq_ref, gpk_ref,
    raw_ref, moved_ref, turned_ref, turned_moved_ref,
):
    flip = flip_matrix()
    lane_pair = lax.broadcasted_iota(jnp.int32, (1, PAIR), 1)
    rows = lax.broadcasted_iota(jnp.int32, (CHUNK, SEQ), 0)
    cols = lax.broadcasted_iota(jnp.int32, (CHUNK, SEQ), 1)
    q_all = q_ref[...]
    pq_all, pk_all = pq_ref[...], pk_ref[...]
    gc_all = gc_ref[...]
    k_flipped = reverse_rows(flip, k_ref[...])
    v_flipped = reverse_rows(flip, v_ref[...])
    both = lambda: jnp.zeros((SEQ, PAIR), bf16)
    gk_pair = gv_pair = gpq_pair = gpk_pair = None
    for head in range(2):
        mine = (lane_pair >= head * HEAD) & (lane_pair < (head + 1) * HEAD)
        gc_head = jnp.where(mine, gc_all, jnp.zeros_like(gc_all))
        for c in range(SEQ // CHUNK):
            part = slice(c * CHUNK, (c + 1) * CHUNK)
            probs = probs_ref[0, head, part, :].astype(f32)
            grad_probs = dot_nt(gc_head[part], v_flipped)
            inner = jnp.sum(probs * grad_probs, axis=1, keepdims=True)
            grad_raw = (probs * (grad_probs - inner) * SCALE).astype(bf16)
            raw_ref[part, :] = grad_raw
            moved_ref[part, :] = fold_edges(skew(grad_raw, c * CHUNK - 255), c, rows, cols)
            gq = (dot_nn(grad_raw, k_flipped) + dot_nn(moved_ref[part, :], pk_all)).astype(bf16)
            if head == 0:
                gq_ref[part, :] = gq
            else:
                gq_ref[part, :] = jnp.where(mine, gq, gq_ref[part, :])
        gk_parts = []
        for c in range(SEQ // CHUNK):
            part = slice(c * CHUNK, (c + 1) * CHUNK)
            turned = raw_ref[:, part].T
            turned_moved = fold_edges(skew(turned, c * CHUNK - 255), c, rows, cols)
            turned_moved_ref[part, :] = turned_moved
            gk_parts.append(
                (dot_nn(turned, q_all) + dot_nn(turned_moved, pq_all)).astype(bf16)
            )
        gk = jnp.concatenate(gk_parts, axis=0)
        gv = dot_tn(gc_all, probs_ref[0, head]).T.astype(bf16)
        gpk = dot_tn(q_all, moved_ref[...]).T
        gpq = dot_tn(k_flipped, turned_moved_ref[...]).T
        if head == 0:
            gk_pair, gv_pair, gpk_pair, gpq_pair = gk, gv, gpk, gpq
        else:
            gk_pair = jnp.where(mine, gk, gk_pair)
            gv_pair = jnp.where(mine, gv, gv_pair)
            gpk_pair = jnp.where(mine, gpk, gpk_pair)
            gpq_pair = jnp.where(mine, gpq, gpq_pair)
    gk_ref[...] = reverse_rows(flip, gk_pair)
    gv_ref[...] = reverse_rows(flip, gv_pair)

    @pl.when(pl.program_id(1) == 0)
    def first():
        gpk_ref[...] = gpk_pair
        gpq_ref[...] = gpq_pair

    @pl.when(pl.program_id(1) != 0)
    def later():
        gpk_ref[...] += gpk_pair
        gpq_ref[...] += gpq_pair


def attend_back(qkv, pos, grad_context, probs):
    qkv_block = lambda which: pl.BlockSpec((SEQ, PAIR), lambda p, s: (s, which * PAIRS + p))
    pos_block = lambda which: pl.BlockSpec((SEQ, PAIR), lambda p, s: (0, which * PAIRS + p))
    token_block = pl.BlockSpec((SEQ, PAIR), lambda p, s: (s, p))
    table_block = pl.BlockSpec((SEQ, PAIR), lambda p, s: (0, p))
    token_shape = jax.ShapeDtypeStruct((MICRO * SEQ, D), bf16)
    table_shape = jax.ShapeDtypeStruct((SEQ, D), f32)
    return pl.pallas_call(
        attend_back_kernel,
        grid=(PAIRS, MICRO),
        in_specs=[
            qkv_block(0), qkv_block(1), qkv_block(2), pos_block(0), pos_block(1), token_block,
            pl.BlockSpec((1, 2, SEQ, SEQ), lambda p, s: (s, p, 0, 0)),
        ],
        out_specs=[token_block, token_block, token_block, table_block, table_block],
        out_shape=[token_shape, token_shape, token_shape, table_shape, table_shape],
        scratch_shapes=[pltpu.VMEM((SEQ, SEQ), bf16)] * 4,
        compiler_params=pltpu.CompilerParams(vmem_limit_bytes=40 * 2**20),
        cost_estimate=pl.CostEstimate(
            flops=24 * 16 * 2 * SEQ * SEQ * PAIR, bytes_accessed=24 * 2**20, transcendentals=0
        ),
        name="attend_back",
    )(qkv, qkv, qkv, pos, pos, grad_context, probs)


def normalise(v):
    row_mean = jnp.mean(v, axis=-1, keepdims=True)
    centered = v - row_mean
    variance = jnp.mean(centered * centered, axis=-1, keepdims=True)
    rstd = lax.rsqrt(variance + norm_epsilon)
    return centered * rstd, rstd


def norm_back(normed, rstd, gain, grad):
    e = grad * gain
    grad_in = rstd * (
        e
        - jnp.mean(e, axis=-1, keepdims=True)
        - normed * jnp.mean(e * normed, axis=-1, keepdims=True)
    )
    return grad_in, jnp.sum(grad * normed, axis=0), jnp.sum(grad, axis=0)


def narrow_shifts(block, shift):
    size = lax.axis_size("narrow")
    return lax.ppermute(block, "narrow", [(i, (i + shift) % size) for i in range(size)])


def gather_rows(shard):
    size = lax.axis_size("narrow")
    me = lax.axis_index("narrow")
    rows, cols = shard.shape
    together = jnp.zeros((size * rows, cols), shard.dtype)
    for shift in range(size):
        block = narrow_shifts(shard, shift) if shift else shard
        owner = lax.rem(me - shift + size, size)
        together = lax.dynamic_update_slice(together, block, (owner * rows, 0))
    return lax.all_gather(together, "wide", axis=0, tiled=True)


def scatter_wide(full):
    return lax.psum_scatter(full, "wide", scatter_dimension=0, tiled=True)


def scatter_narrow(part):
    size = lax.axis_size("narrow")
    me = lax.axis_index("narrow")
    rows = part.shape[0] // size
    total = None
    for shift in range(size):
        target = lax.rem(me + shift, size)
        block = lax.dynamic_slice_in_dim(part, target * rows, rows, 0)
        block = (narrow_shifts(block, shift) if shift else block).astype(f32)
        total = block if total is None else total + block
    return total


def body(
    hidden_in, cotangent, seq_lengths,
    query_weight, query_bias, key_weight, key_bias, value_weight, value_bias,
    out_weight, out_bias, first_gain, first_shift, up_weight, up_bias,
    down_weight, down_bias, second_gain, second_shift, rel_table,
):
    tokens = MICRO * SEQ
    x = hidden_in.reshape(tokens, D)
    cot = cotangent.reshape(tokens, D).astype(f32)
    lengths = seq_lengths.reshape(MICRO)
    share = query_weight.shape[0]
    vectors = [
        query_bias, key_bias, value_bias, out_bias, first_gain, first_shift,
        down_bias, second_gain, second_shift,
    ]
    vectors = jnp.concatenate([jnp.stack(vectors), up_bias.reshape(4, share)], axis=0)
    vectors = jnp.pad(vectors, ((0, VECTORS - vectors.shape[0]), (0, 0)))
    first_pack = gather_rows(
        jnp.concatenate(
            [
                query_weight, key_weight, value_weight,
                jnp.concatenate([rel_table, vectors], axis=0).T,
            ],
            axis=1,
        )
    )
    second_pack = gather_rows(jnp.concatenate([out_weight, up_weight], axis=1))
    down_full = gather_rows(down_weight)
    qkv_weight = first_pack[:, : 3 * D]
    rel_turned = first_pack[:, 3 * D : 3 * D + SEQ]
    out_full = second_pack[:, :D]
    up_full = second_pack[:, D:]
    vector_rows = first_pack[:, 3 * D + SEQ :].T.astype(f32)
    qkv_bias = vector_rows[:3].reshape(3 * D)
    out_b, gain_1, shift_1, down_b, gain_2, shift_2 = (vector_rows[i] for i in range(3, 9))
    up_b = jnp.transpose(vector_rows[9:13].reshape(4, D // share, share), (1, 0, 2)).reshape(4 * D)

    qkv = (dot_nn(x, qkv_weight) + qkv_bias).astype(bf16)
    pos = (dot_tn(rel_turned, qkv_weight[:, : 2 * D]) + qkv_bias[: 2 * D]).astype(bf16)
    context, probs = attend(lengths, qkv, pos)

    first_in = x.astype(f32) + dot_nn(context, out_full) + out_b
    normed_1, rstd_1 = normalise(first_in)
    hidden = normed_1 * gain_1 + shift_1
    hidden_low = hidden.astype(bf16)
    upward = dot_nn(hidden_low, up_full) + up_b
    cdf = 0.5 * (1.0 + lax.erf(upward * math.sqrt(0.5)))
    activated_low = (upward * cdf).astype(bf16)
    slope = (cdf + upward * jnp.exp(-0.5 * upward * upward) * (1 / math.sqrt(2 * math.pi))).astype(
        bf16
    )
    second_in = hidden + dot_nn(activated_low, down_full) + down_b
    normed_2, rstd_2 = normalise(second_in)
    hidden_out = (normed_2 * gain_2 + shift_2).astype(bf16)

    grad_second, grad_gain_2, grad_shift_2 = norm_back(normed_2, rstd_2, gain_2, cot)
    grad_feed = grad_second.astype(bf16)
    grad_down_bias = jnp.sum(grad_feed.astype(f32), axis=0)
    grad_down = dot_tn(activated_low, grad_feed).astype(bf16)
    grad_up = (dot_nt(grad_feed, down_full) * slope.astype(f32)).astype(bf16)
    grad_up_bias = jnp.sum(grad_up.astype(f32), axis=0)
    grad_up_weight = dot_tn(hidden_low, grad_up).astype(bf16)
    grad_hidden = grad_second + dot_nt(grad_up, up_full)
    grad_first, grad_gain_1, grad_shift_1 = norm_back(normed_1, rstd_1, gain_1, grad_hidden)
    grad_branch = grad_first.astype(bf16)
    grad_out_bias = jnp.sum(grad_branch.astype(f32), axis=0)
    grad_out = dot_tn(context, grad_branch).astype(bf16)
    grad_context = dot_nt(grad_branch, out_full).astype(bf16)

    grad_second_pack = jnp.concatenate([grad_out, grad_up_weight], axis=1)
    down_part = scatter_wide(grad_down)
    grad_context, grad_second_pack, down_part = lax.optimization_barrier(
        (grad_context, grad_second_pack, down_part)
    )
    second_part = scatter_wide(grad_second_pack)

    gq, gk, gv, gpq, gpk = attend_back(qkv, pos, grad_context, probs)
    gpos = jnp.concatenate([gpq, gpk], axis=1).astype(bf16)
    gqkv = jnp.concatenate([gq, gk, gv], axis=1)
    grad_inputs = grad_first + dot_nt(gqkv, qkv_weight)
    grad_qkv = dot_tn(x, gqkv)
    grad_pos_weight = dot_nn(rel_turned, gpos)
    grad_qkv = jnp.concatenate(
        [grad_qkv[:, : 2 * D] + grad_pos_weight, grad_qkv[:, 2 * D :]], axis=1
    )
    qkv_bias_grad = jnp.sum(gqkv.astype(f32), axis=0)
    pos_bias_grad = jnp.sum(gpos.astype(f32), axis=0)
    grad_rel_turned = dot_nt(qkv_weight[:, : 2 * D], gpos)
    vector_grads = [
        qkv_bias_grad[:D] + pos_bias_grad[:D],
        qkv_bias_grad[D : 2 * D] + pos_bias_grad[D:],
        qkv_bias_grad[2 * D :],
        grad_out_bias, grad_gain_1, grad_shift_1, grad_down_bias, grad_gain_2, grad_shift_2,
    ]
    grad_up_bias = jnp.transpose(grad_up_bias.reshape(D // share, 4, share), (1, 0, 2))
    vector_grads = jnp.concatenate(
        [
            jnp.stack(vector_grads),
            grad_up_bias.reshape(4, D),
            jnp.zeros((VECTORS - 13, D), f32),
        ],
        axis=0,
    )
    vector_grads = lax.optimization_barrier(vector_grads.T.astype(bf16))
    last_pack = jnp.concatenate(
        [grad_qkv.astype(bf16), grad_rel_turned.astype(bf16), vector_grads], axis=1
    )
    last_pack, second_part = lax.optimization_barrier((last_pack, second_part))
    last_sum = scatter_narrow(scatter_wide(last_pack))
    down_sum = scatter_narrow(down_part)
    second_sum = scatter_narrow(second_part)
    turned = last_sum[:, 3 * D :].T
    vec = lambda i: turned[SEQ + i]
    return (
        hidden_out.reshape(hidden_in.shape),
        grad_inputs.reshape(hidden_in.shape),
        last_sum[:, :D], vec(0),
        last_sum[:, D : 2 * D], vec(1),
        last_sum[:, 2 * D : 3 * D], vec(2),
        second_sum[:, :D], vec(3), vec(4), vec(5),
        second_sum[:, D:],
        turned[SEQ + 9 : SEQ + 13].reshape(4 * share),
        down_sum, vec(6), vec(7), vec(8),
        turned[:SEQ],
    )


def solution(mesh):
    tokens = P(None, AXES, None, None)
    rows = P(AXES, None)
    vector = P(AXES)
    weights = (
        rows, vector, rows, vector, rows, vector, rows, vector, vector, vector,
        rows, vector, rows, vector, vector, vector, P(None, AXES),
    )
    return jax.shard_map(
        body,
        mesh=mesh,
        in_specs=(tokens, tokens, P(None, AXES)) + weights,
        out_specs=(tokens, tokens) + weights,
        check_vma=False,
    )
```

profile of v0, /device:TPU:9, one launch (start us, length us, event | category | flops | bytes accessed | tf_op | source)
XLA Modules:
  0.0 428.8 jit_solution(15305180767066369519)
XLA Ops:
  8.0 1.5 concatenate.32
  16.0 8.6 %collective-permute-done.1 = bf16[24,3072]{1,0:T(8,128)(2,1)S(1)} collective-permute-done((bf16[24,3072]{1,0:T(8,128)(2,1)S(1)}, bf16[24,3072]{1,0:T(8,128)(2,1)S(1)}, u32[]{:S(2)}, u32[]{:S(2)}) %collective-permute-start.1) | collective-permute-done | bytes 147488 | tf_op jit(solution)/shard_map/ppermute | solution.py:264
  24.6 2.8 collective-permute-done.2
  30.5 1.4 collective-permute-start.5
  31.9 3.8 collective-permute-done.3
  35.8 10.0 %collective-permute-done.4 = bf16[24,3840]{1,0:T(8,128)(2,1)S(1)} collective-permute-done((bf16[24,3840]{1,0:T(8,128)(2,1)S(1)}, bf16[24,3840]{1,0:T(8,128)(2,1)S(1)}, u32[]{:S(2)}, u32[]{:S(2)}) %collective-permute-start.4) | collective-permute-done | bytes 184352 | tf_op jit(solution)/shard_map/ppermute | solution.py:264
  45.8 1.6 collective-permute-done.5
  48.4 1.6 collective-permute-start.7
  50.0 1.4 collective-permute-start.8
  51.5 1.8 collective-permute-done.6
  53.3 7.6 %collective-permute-done.7 = bf16[96,768]{1,0:T(8,128)(2,1)S(1)} collective-permute-done((bf16[96,768]{1,0:T(8,128)(2,1)S(1)}, bf16[96,768]{1,0:T(8,128)(2,1)S(1)}, u32[]{:S(2)}, u32[]{:S(2)}) %collective-permute-start.7) | collective-permute-done | bytes 147488 | tf_op jit(solution)/shard_map/ppermute | solution.py:264
  60.9 2.9 collective-permute-done.8
  64.7 3.1 all-gather.4.cloned.1.call-done
  71.6 3.5 fusion.21.pq_ref.pk_ref
  75.2 4.2 fusion.5.q_ref.k_ref.v_ref
  79.4 65.1 %attend.1 = (bf16[1024,768]{1,0:T(8,128)(2,1)S(1)}, bf16[2,12,512,512]{3,2,1,0:T(8,128)(2,1)}) custom-call(s32[2]{0:T(128)S(1)} %bitcast.65, bf16[1024,2304]{1,0:T(8,128)(2,1)S(1)} %fusion.5.q_ref.k_ref.v_ref, bf16[1024,2304]{1,0:T(8,128)(2,1)S(1)} %fusion.5.q_ref.k_ref.v_ref, bf16[1024,2304]{1,0:T(8,128)(2,1)S(1)} %fusion.5.q_ref.k_ref.v_ref, ...), custom_call_target="tpu_custom_call" | custom-call | flops 12884901888 | bytes 20971520 | tf_op jit(solution)/shard_map/attend/pallas_call | solution.py:114
  144.5 2.1 copy-done.1
  146.7 3.5 fusion.54
  151.9 9.7 %multiply_convert_fusion.1 = (bf16[1024,3072]{1,0:T(8,128)(2,1)}, f32[1024,3072]{1,0:T(8,128)}) fusion(f32[3072]{0:T(1024)S(1)} %add.256, bf16[768,3840]{1,0:T(8,128)(2,1)S(1)} %bitcast.83, f32[1024,768]{1,0:T(8,128)S(1)} %get-tuple-element.201, f32[768]{0:T(1024)S(1)} %get-tuple-element.166, f32[768]{0:T(1024)S(1)} %get-tuple-element.167, ...), kind=kOutput, calls=%fused_computation.7 | convolution fusion | flops 4854644736 | bytes 26767360 | tf_op jit(solution)/shard_map/dot_general | solution.py:32
  161.6 9.5 %fusion.55 = (f32[1024]{0:T(1024)S(1)}, f32[1024,768]{1,0:T(8,128)S(1)}) fusion(f32[768]{0:T(1024)S(1)} %get-tuple-element.165, bf16[1024,3072]{1,0:T(8,128)(2,1)} %get-tuple-element.202, bf16[3072,768]{1,0:T(8,128)(2,1)} %all-gather.8.cloned.1.call-done, f32[768]{0:T(1024)S(1)} %get-tuple-element.166, f32[768]{0:T(1024)S(1)} %get-tuple-element.167, ...), kind=kOutput, calls=%fused_computation.140 | convolution fusion | flops 4837342208 | bytes 17323008 | tf_op jit(solution)/shard_map/dot_general | solution.py:32
  172.5 2.7 fusion.17
  176.5 1.7 copy-done.10
  178.2 7.1 %convolution_convert_fusion = bf16[3072,768]{1,0:T(8,128)(2,1)} fusion(bf16[1024,3072]{1,0:T(8,128)(2,1)S(1)} %bitcast.89, f32[1024,768]{1,0:T(8,128)S(1)} %get-tuple-element.179), kind=kOutput, calls=%fused_computation.13 | convolution fusion | flops 4834983936 | bytes 14155776 | tf_op jit(solution)/shard_map/dot_general | solution.py:36
  185.4 13.7 %fusion.56 = (bf16[3072]{0:T(1024)(128)(2,1)S(1)}, bf16[1024,3072]{1,0:T(8,128)(2,1)S(1)}) fusion(f32[1024,3072]{1,0:T(8,128)} %get-tuple-element.203, f32[3072]{0:T(1024)S(1)} %add.256, bf16[3072,768]{1,0:T(8,128)(2,1)} %all-gather.8.cloned.1.call-done, f32[1024,768]{1,0:T(8,128)} %copy-done.10), kind=kOutput, calls=%fused_computation.141 | convolution fusion | flops 4876661760 | bytes 26757120 | tf_op jit(solution)/shard_map/dot_general | solution.py:28
  199.1 10.7 %multiply_reduce_fusion = (bf16[768]{0:T(1024)(128)(2,1)S(1)}, f32[1024]{0:T(1024)S(1)}, f32[1024]{0:T(1024)S(1)}, bf16[768]{0:T(1024)(128)(2,1)S(1)}, f32[1024,768]{1,0:T(8,128)S(1)}) fusion(f32[1024,768]{1,0:T(8,128)S(1)} %copy-done.5, f32[1024]{0:T(1024)S(1)} %add_rsqrt_fusion.1, f32[1024]{0:T(1024)S(1)} %broadcast_multiply_fusion.4, ...), kind=kOutput, calls=%fused_computation.34 | convolution fusion | flops 4839698432 | bytes 20469760 | tf_op jit(solution)/shard_map/dot_general | solution.py:28
  211.0 1.6 copy-done.9
  212.6 2.5 convolution_convert_fusion.3
  215.1 2.4 copy.124
  217.5 3.8 convolution_convert_fusion.2.gc_ref
  221.3 8.9 %convolution_convert_fusion.1 = bf16[768,3072]{1,0:T(8,128)(2,1)S(1)} fusion(bf16[1024,3072]{1,0:T(8,128)(2,1)} %copy-done.22, f32[1024,768]{1,0:T(8,128)S(1)} %copy-done.6, f32[768]{0:T(1024)S(1)} %get-tuple-element.166, f32[768]{0:T(1024)S(1)} %get-tuple-element.167, f32[1024]{0:T(1024)S(1)} %add_rsqrt_fusion.1, f32[1024]{0:T(1024)S(1)} %broadcast_multiply_fusion.4), kind=kOutput, calls=%fused_computation.14 | convolution fusion | flops 4838129664 | bytes 14170112 | tf_op jit(solution)/shard_map/dot_general | solution.py:36
  230.2 2.9 pad_maximum_fusion
  233.0 5.9 %reduce-scatter.6.cloned.1.call-done = bf16[384,768]{1,0:T(8,128)(2,1)} async-done(((bf16[3072,768]{1,0:T(8,128)(2,1)}), bf16[384,768]{1,0:T(8,128)(2,1)}) %reduce-scatter.6.cloned.1.call-update) | async-done | bytes 589840 | tf_op jit(solution)/shard_map/reduce_scatter | solution.py:280
  239.0 1.7 reduce.5
  241.6 76.9 %attend_back.1 = (bf16[1024,768]{1,0:T(8,128)(2,1)S(1)}, bf16[1024,768]{1,0:T(8,128)(2,1)S(1)}, bf16[1024,768]{1,0:T(8,128)(2,1)S(1)}, f32[512,768]{1,0:T(8,128)S(1)}, f32[512,768]{1,0:T(8,128)S(1)}) custom-call(bf16[1024,2304]{1,0:T(8,128)(2,1)} %copy-done.1, bf16[1024,2304]{1,0:T(8,128)(2,1)} %copy-done.1, bf16[1024,2304]{1,0:T(8,128)(2,1)} %copy-done.1, ...), custom_call_target="tpu_custom_call" | custom-call | flops 25769803776 | bytes 25165824 | tf_op jit(solution)/shard_map/attend_back/pallas_call | solution.py:226
  320.2 3.9 convolution_bitcast_fusion
  325.0 2.1 copy-done.17
  329.1 2.5 concatenate.39
  331.6 3.2 fusion.32
  335.3 2.7 fusion.6
  338.1 2.7 pad_maximum_fusion.1
  340.8 6.6 %copy.138 = bf16[768,3072]{1,0:T(8,128)(2,1)} copy(bf16[768,3072]{0,1:T(8,128)(2,1)} %pad_maximum_fusion.1) | data formatting | bytes 9437184
  352.2 10.7 %fusion.29 = f32[1024,768]{1,0:T(8,128)} fusion(f32[1024,768]{1,0:T(8,128)} %copy-done.9, bf16[1024,2304]{1,0:T(8,128)(2,1)} %copy-done.7, bf16[768,3072]{1,0:T(8,128)(2,1)} %all-gather.4.cloned.1.call-done), kind=kOutput, calls=%fused_computation.57 | convolution fusion | flops 3624665088 | bytes 14548992 | tf_op jit(solution)/shard_map/dot_general | solution.py:28
  362.9 1.8 collective-permute-done.17
  365.6 1.5 collective-permute-start.13
  367.2 34.3 %reduce-scatter.10.cloned.1.call-done = bf16[96,3072]{1,0:T(8,128)(2,1)} async-done(((bf16[768,3072]{1,0:T(8,128)(2,1)}), bf16[96,3072]{1,0:T(8,128)(2,1)}) %reduce-scatter.10.cloned.1.call-update) | async-done | bytes 589840 | tf_op jit(solution)/shard_map/reduce_scatter | solution.py:280
  402.6 2.2 collective-permute-start.10
  407.7 7.0 %collective-permute-done.10 = bf16[24,3072]{1,0:T(8,128)(2,1)S(1)} collective-permute-done((bf16[24,3072]{1,0:T(8,128)(2,1)S(1)}, bf16[24,3072]{1,0:T(8,128)(2,1)S(1)}, u32[]{:S(2)}, u32[]{:S(2)}) %collective-permute-start.10) | collective-permute-done | bytes 147488 | tf_op jit(solution)/shard_map/ppermute | solution.py:264
  414.7 2.3 collective-permute-done.11
  (173 shorter events, 42.0 us)
Async XLA Ops:
  7.2 41.1 %copy-start.19 = (bf16[96,768]{1,0:T(8,128)(2,1)S(1)}, bf16[96,768]{1,0:T(8,128)(2,1)}, u32[]{:S(2)}) copy-start(bf16[96,768]{1,0:T(8,128)(2,1)} %param.35) | copy-start | bytes 442372
  7.2 60.6 %all-gather.4.cloned.1.call-start = ((), (), s32[]{:S(2)}) async-start(), calls=%async_computation.3 | async-start | bytes 5308416 | tf_op jit(solution)/shard_map/all_gather | solution.py:276
  11.2 4.8 %collective-permute-start = (bf16[24,3072]{1,0:T(8,128)(2,1)S(1)}, bf16[24,3072]{1,0:T(8,128)(2,1)S(1)}, u32[]{:S(2)}, u32[]{:S(2)}) collective-permute-start(bf16[24,3072]{1,0:T(8,128)(2,1)S(1)} %get-tuple-element.196), channel_id=1, source_target_pairs={{0,1},{1,2},{2,3},{3,0},{4,5},{5,6},{6,7},{7,4},{8,9},{9,10},{10,1... | collective-permute-start | bytes 442376 | tf_op jit(solution)/shard_map/ppermute | solution.py:264
  12.6 12.0 %collective-permute-start.1 = (bf16[24,3072]{1,0:T(8,128)(2,1)S(1)}, bf16[24,3072]{1,0:T(8,128)(2,1)S(1)}, u32[]{:S(2)}, u32[]{:S(2)}) collective-permute-start(bf16[24,3072]{1,0:T(8,128)(2,1)S(1)} %get-tuple-element.196), channel_id=1, source_target_pairs={{0,2},{1,3},{2,0},{3,1},{4,6},{5,7},{6,4},{7,5},{8,10},{9,11},{10,... | collective-permute-start | bytes 442376 | tf_op jit(solution)/shard_map/ppermute | solution.py:264
  13.7 13.7 %collective-permute-start.2 = (bf16[24,3072]{1,0:T(8,128)(2,1)S(1)}, bf16[24,3072]{1,0:T(8,128)(2,1)S(1)}, u32[]{:S(2)}, u32[]{:S(2)}) collective-permute-start(bf16[24,3072]{1,0:T(8,128)(2,1)S(1)} %get-tuple-element.196), channel_id=1, source_target_pairs={{0,3},{1,0},{2,1},{3,2},{4,7},{5,4},{6,5},{7,6},{8,11},{9,8},{10,9... | collective-permute-start | bytes 442376 | tf_op jit(solution)/shard_map/ppermute | solution.py:264
  28.2 118.4 %all-gather.6.cloned.1.call-start = ((), (), s32[]{:S(2)}) async-start(), calls=%async_computation.4 | async-start | bytes 6635520 | tf_op jit(solution)/shard_map/all_gather | solution.py:276
  30.0 5.8 %collective-permute-start.3 = (bf16[24,3840]{1,0:T(8,128)(2,1)S(1)}, bf16[24,3840]{1,0:T(8,128)(2,1)S(1)}, u32[]{:S(2)}, u32[]{:S(2)}) collective-permute-start(bf16[24,3840]{1,0:T(8,128)(2,1)S(1)} %constant_dynamic-update-slice_fusion), channel_id=1, source_target_pairs={{0,1},{1,2},{2,3},{3,0},{4,5},{5,6},{6,7},{7,4},{8,9},{9,10},{10,1... | collective-permute-start | bytes 552968 | tf_op jit(solution)/shard_map/ppermute | solution.py:264
  30.1 15.7 %collective-permute-start.4 = (bf16[24,3840]{1,0:T(8,128)(2,1)S(1)}, bf16[24,3840]{1,0:T(8,128)(2,1)S(1)}, u32[]{:S(2)}, u32[]{:S(2)}) collective-permute-start(bf16[24,3840]{1,0:T(8,128)(2,1)S(1)} %constant_dynamic-update-slice_fusion), channel_id=1, source_target_pairs={{0,2},{1,3},{2,0},{3,1},{4,6},{5,7},{6,4},{7,5},{8,10},{9,11},{10,... | collective-permute-start | bytes 552968 | tf_op jit(solution)/shard_map/ppermute | solution.py:264
  30.5 16.9 %collective-permute-start.5 = (bf16[24,3840]{1,0:T(8,128)(2,1)S(1)}, bf16[24,3840]{1,0:T(8,128)(2,1)S(1)}, u32[]{:S(2)}, u32[]{:S(2)}) collective-permute-start(bf16[24,3840]{1,0:T(8,128)(2,1)S(1)} %constant_dynamic-update-slice_fusion), channel_id=1, source_target_pairs={{0,3},{1,0},{2,1},{3,2},{4,7},{5,4},{6,5},{7,6},{8,11},{9,8},{10,9... | collective-permute-start | bytes 552968 | tf_op jit(solution)/shard_map/ppermute | solution.py:264
  48.2 113.4 %all-gather.8.cloned.1.call-start = ((), (), s32[]{:S(2)}) async-start(), calls=%async_computation.5 | async-start | bytes 5308416 | tf_op jit(solution)/shard_map/all_gather | solution.py:276
  48.3 5.0 %collective-permute-start.6 = (bf16[96,768]{1,0:T(8,128)(2,1)S(1)}, bf16[96,768]{1,0:T(8,128)(2,1)S(1)}, u32[]{:S(2)}, u32[]{:S(2)}) collective-permute-start(bf16[96,768]{1,0:T(8,128)(2,1)S(1)} %copy-done.19), channel_id=1, source_target_pairs={{0,1},{1,2},{2,3},{3,0},{4,5},{5,6},{6,7},{7,4},{8,9},{9,10},{10,1... | collective-permute-start | bytes 442376 | tf_op jit(solution)/shard_map/ppermute | solution.py:264
  48.4 12.5 %collective-permute-start.7 = (bf16[96,768]{1,0:T(8,128)(2,1)S(1)}, bf16[96,768]{1,0:T(8,128)(2,1)S(1)}, u32[]{:S(2)}, u32[]{:S(2)}) collective-permute-start(bf16[96,768]{1,0:T(8,128)(2,1)S(1)} %copy-done.19), channel_id=1, source_target_pairs={{0,2},{1,3},{2,0},{3,1},{4,6},{5,7},{6,4},{7,5},{8,10},{9,11},{10,... | collective-permute-start | bytes 442376 | tf_op jit(solution)/shard_map/ppermute | solution.py:264
  50.0 13.8 %collective-permute-start.8 = (bf16[96,768]{1,0:T(8,128)(2,1)S(1)}, bf16[96,768]{1,0:T(8,128)(2,1)S(1)}, u32[]{:S(2)}, u32[]{:S(2)}) collective-permute-start(bf16[96,768]{1,0:T(8,128)(2,1)S(1)} %copy-done.19), channel_id=1, source_target_pairs={{0,3},{1,0},{2,1},{3,2},{4,7},{5,4},{6,5},{7,6},{8,11},{9,8},{10,9... | collective-permute-start | bytes 442376 | tf_op jit(solution)/shard_map/ppermute | solution.py:264
  64.7 174.3 %reduce-scatter.6.cloned.1.call-start = ((), (), s32[]{:S(2)}) async-start(), calls=%async_computation.6 | async-start | bytes 5308416 | tf_op jit(solution)/shard_map/reduce_scatter | solution.py:280
  68.8 2.3 copy-start.2
  71.2 4.0 slice-start
  71.6 3.6 slice-start.1
  71.6 3.6 copy-start.20
  75.2 4.2 copy-start
  144.5 2.1 copy-start.1
  146.7 5.2 %slice-start.2 = ((s8[5898240]{0:T(1024)(128)(4,1)}), s8[4194304]{0:T(1024)(128)(4,1)S(1)}, s32[]{:S(2)}) async-start(s8[5898240]{0:T(1024)(128)(4,1)} %bitcast.82), calls=%async_computation.11 | async-start | bytes 8388608
  146.7 5.2 %slice-start.3 = ((s8[5898240]{0:T(1024)(128)(4,1)}), s8[1703936]{0:T(1024)(128)(4,1)S(1)}, s32[]{:S(2)}) async-start(s8[5898240]{0:T(1024)(128)(4,1)} %bitcast.82), calls=%async_computation.12 | async-start | bytes 3407872
  150.2 1.7 copy-start.4
  172.5 5.7 %slice-start.4 = ((s8[6291456]{0:T(1024)(128)(4,1)}), s8[4194304]{0:T(1024)(128)(4,1)S(1)}, s32[]{:S(2)}) async-start(s8[6291456]{0:T(1024)(128)(4,1)} %bitcast.88), calls=%async_computation.13 | async-start | bytes 8388608
  175.3 2.9 slice-start.5
  176.5 1.7 copy-start.10
  185.3 155.5 %reduce-scatter.8.cloned.1.call-start = ((), (), s32[]{:S(2)}) async-start(), calls=%async_computation.7 | async-start | bytes 6635520 | tf_op jit(solution)/shard_map/reduce_scatter | solution.py:280
  185.4 13.8 %copy-start.5 = (f32[1024,768]{1,0:T(8,128)S(1)}, f32[1024,768]{1,0:T(8,128)}, u32[]{:S(2)}) copy-start(f32[1024,768]{1,0:T(8,128)} %copy-done.4) | copy-start | bytes 9437188
  185.4 13.7 %copy-start.11 = (f32[1024,768]{1,0:T(8,128)S(1)}, f32[1024,768]{1,0:T(8,128)}, u32[]{:S(2)}) copy-start(f32[1024,768]{1,0:T(8,128)} %copy-done.10) | copy-start | bytes 9437188
  199.1 10.7 %copy-start.22 = (bf16[1024,3072]{1,0:T(8,128)(2,1)}, bf16[1024,3072]{1,0:T(8,128)(2,1)S(1)}, u32[]{:S(2)}) copy-start(bf16[1024,3072]{1,0:T(8,128)(2,1)S(1)} %get-tuple-element.208) | copy-start | bytes 18874372
  211.0 1.6 copy-start.9
  217.5 3.8 copy-start.6
  221.3 8.9 %copy-start.8 = (bf16[768,768]{1,0:T(8,128)(2,1)S(1)}, bf16[768,768]{1,0:T(8,128)(2,1)}, u32[]{:S(2)}) copy-start(bf16[768,768]{1,0:T(8,128)(2,1)} %copy.124) | copy-start | bytes 3538948
  239.0 162.5 %reduce-scatter.10.cloned.1.call-start = ((), (), s32[]{:S(2)}) async-start(), calls=%async_computation.8 | async-start | bytes 5308416 | tf_op jit(solution)/shard_map/reduce_scatter | solution.py:280
  318.8 1.4 copy-start.21
  320.2 4.0 copy-start.7
  324.1 2.9 copy-start.17
  331.6 3.7 copy-start.18
  348.5 14.4 %collective-permute-start.15 = (bf16[96,768]{1,0:T(8,128)(2,1)S(1)}, bf16[96,768]{1,0:T(8,128)(2,1)S(1)}, u32[]{:S(2)}, u32[]{:S(2)}) collective-permute-start(bf16[96,768]{1,0:T(8,128)(2,1)S(1)} %get-tuple-element.186), channel_id=1, source_target_pairs={{0,1},{1,2},{2,3},{3,0},{4,5},{5,6},{6,7},{7,4},{8,9},{9,10},{10,1... | collective-permute-start | bytes 442376 | tf_op jit(solution)/shard_map/ppermute | solution.py:264
  349.8 13.1 %collective-permute-start.16 = (bf16[96,768]{1,0:T(8,128)(2,1)S(1)}, bf16[96,768]{1,0:T(8,128)(2,1)S(1)}, u32[]{:S(2)}, u32[]{:S(2)}) collective-permute-start(bf16[96,768]{1,0:T(8,128)(2,1)S(1)} %get-tuple-element.188), channel_id=1, source_target_pairs={{0,2},{1,3},{2,0},{3,1},{4,6},{5,7},{6,4},{7,5},{8,10},{9,11},{10,... | collective-permute-start | bytes 442376 | tf_op jit(solution)/shard_map/ppermute | solution.py:264
  350.9 14.6 %copy-start.15 = (bf16[96,3840]{1,0:T(8,128)(2,1)S(1)}, bf16[96,3840]{1,0:T(8,128)(2,1)}, u32[]{:S(2)}) copy-start(bf16[96,3840]{1,0:T(8,128)(2,1)} %reduce-scatter.8.cloned.1.call-done) | copy-start | bytes 2211844
  350.9 13.8 %collective-permute-start.17 = (bf16[96,768]{1,0:T(8,128)(2,1)S(1)}, bf16[96,768]{1,0:T(8,128)(2,1)S(1)}, u32[]{:S(2)}, u32[]{:S(2)}) collective-permute-start(bf16[96,768]{1,0:T(8,128)(2,1)S(1)} %get-tuple-element.187), channel_id=1, source_target_pairs={{0,3},{1,0},{2,1},{3,2},{4,7},{5,4},{6,5},{7,6},{8,11},{9,8},{10,9... | collective-permute-start | bytes 442376 | tf_op jit(solution)/shard_map/ppermute | solution.py:264
  365.5 39.5 %collective-permute-start.12 = (bf16[24,3840]{1,0:T(8,128)(2,1)S(1)}, bf16[24,3840]{1,0:T(8,128)(2,1)S(1)}, u32[]{:S(2)}, u32[]{:S(2)}) collective-permute-start(bf16[24,3840]{1,0:T(8,128)(2,1)S(1)} %get-tuple-element.183), channel_id=1, source_target_pairs={{0,1},{1,2},{2,3},{3,0},{4,5},{5,6},{6,7},{7,4},{8,9},{9,10},{10,1... | collective-permute-start | bytes 552968 | tf_op jit(solution)/shard_map/ppermute | solution.py:264
  365.6 40.7 %collective-permute-start.13 = (bf16[24,3840]{1,0:T(8,128)(2,1)S(1)}, bf16[24,3840]{1,0:T(8,128)(2,1)S(1)}, u32[]{:S(2)}, u32[]{:S(2)}) collective-permute-start(bf16[24,3840]{1,0:T(8,128)(2,1)S(1)} %get-tuple-element.185), channel_id=1, source_target_pairs={{0,2},{1,3},{2,0},{3,1},{4,6},{5,7},{6,4},{7,5},{8,10},{9,11},{10,... | collective-permute-start | bytes 552968 | tf_op jit(solution)/shard_map/ppermute | solution.py:264
  367.0 39.2 %collective-permute-start.14 = (bf16[24,3840]{1,0:T(8,128)(2,1)S(1)}, bf16[24,3840]{1,0:T(8,128)(2,1)S(1)}, u32[]{:S(2)}, u32[]{:S(2)}) collective-permute-start(bf16[24,3840]{1,0:T(8,128)(2,1)S(1)} %get-tuple-element.184), channel_id=1, source_target_pairs={{0,3},{1,0},{2,1},{3,2},{4,7},{5,4},{6,5},{7,6},{8,11},{9,8},{10,9... | collective-permute-start | bytes 552968 | tf_op jit(solution)/shard_map/ppermute | solution.py:264
  402.6 12.1 %collective-permute-start.10 = (bf16[24,3072]{1,0:T(8,128)(2,1)S(1)}, bf16[24,3072]{1,0:T(8,128)(2,1)S(1)}, u32[]{:S(2)}, u32[]{:S(2)}) collective-permute-start(bf16[24,3072]{1,0:T(8,128)(2,1)S(1)} %get-tuple-element.190), channel_id=1, source_target_pairs={{0,2},{1,3},{2,0},{3,1},{4,6},{5,7},{6,4},{7,5},{8,10},{9,11},{10,... | collective-permute-start | bytes 442376 | tf_op jit(solution)/shard_map/ppermute | solution.py:264
  404.8 12.2 %collective-permute-start.11 = (bf16[24,3072]{1,0:T(8,128)(2,1)S(1)}, bf16[24,3072]{1,0:T(8,128)(2,1)S(1)}, u32[]{:S(2)}, u32[]{:S(2)}) collective-permute-start(bf16[24,3072]{1,0:T(8,128)(2,1)S(1)} %get-tuple-element.191), channel_id=1, source_target_pairs={{0,3},{1,0},{2,1},{3,2},{4,7},{5,4},{6,5},{7,6},{8,11},{9,8},{10,9... | collective-permute-start | bytes 442376 | tf_op jit(solution)/shard_map/ppermute | solution.py:264
  405.0 12.8 %collective-permute-start.9 = (bf16[24,3072]{1,0:T(8,128)(2,1)S(1)}, bf16[24,3072]{1,0:T(8,128)(2,1)S(1)}, u32[]{:S(2)}, u32[]{:S(2)}) collective-permute-start(bf16[24,3072]{1,0:T(8,128)(2,1)S(1)} %get-tuple-element.189), channel_id=1, source_target_pairs={{0,1},{1,2},{2,3},{3,0},{4,5},{5,6},{6,7},{7,4},{8,9},{9,10},{10,1... | collective-permute-start | bytes 442376 | tf_op jit(solution)/shard_map/ppermute | solution.py:264
  (5 other events, 5.0 us)
Sparse Core Ops, SparseCore 0:
  28.4 39.3 all-gather.3
  70.2 43.8 all-gather.5
  116.0 38.9 all-gather.7
  185.4 53.4 reduce-scatter.5
  242.7 59.5 reduce-scatter.7
  347.6 53.8 reduce-scatter.9
where the time goes:
time: 435 us; the launch traced here: 429 us
  Pallas kernels  142 us (33%)
  matrix products  97.8 us (22%)
  waiting for transfers between devices  95.2 us (22%)
  local copies, waits for them, and re-layouts  41.3 us (9%)
  other arithmetic  19.4 us (4%)
  starting transfers between devices  17.9 us (4%)
  between operations  15.1 us (3%)
    pallas_call x1, Pallas kernels, attend_back(): pl.pallas_call(attend_back_kernel, grid=(PAIRS, MICRO), in_specs=[qkv_blo...  76.9 us
    pallas_call x1, Pallas kernels, attend(): pl.pallas_call(attend_kernel, grid_spec=pltpu.PrefetchScalarGridSpec(num_...  65.1 us
    ppermute x18, waiting for transfers between devices, narrow_shifts(): lax.ppermute(block, 'narrow', [(i, (i + shift) % size) for i in range(siz...  51.9 us
    dot_general x5, matrix products, dot_nt(): lax.dot_general(left, right, (((1,), (1,)), ((), ())), preferred_element_...  42.1 us
    reduce_scatter x3, waiting for transfers between devices, scatter_wide(): return lax.psum_scatter(full, 'wide', scatter_dimension=0, tiled=True)  40.2 us
    dot_general x5, matrix products, dot_nn(): lax.dot_general(left, right, (((1,), (0,)), ((), ())), preferred_element_...  29.7 us
    dot_general x5, matrix products, dot_tn(): lax.dot_general(left, right, (((0,), (0,)), ((), ())), preferred_element_...  25.9 us
    unnamed x64, local copies, waits for them, and re-layouts  22.5 us
  transfers between devices with their start and end apart: 24, of which 16 were waited for; matrix products, arithmetic and copies ran while one was open for 25% of the time, Pallas kernels for 33%

commit v1 on v0

v1 whole, which is shorter than its diff:
```python
import functools
import math

import jax
import jax.numpy as jnp
from jax import lax
from jax.experimental import pallas as pl
from jax.experimental.pallas import tpu as pltpu
from jax.sharding import PartitionSpec as P

D = 768
HEADS = 12
HEAD = 64
SEQ = 512
MICRO = 2
PAIR = 2 * HEAD
PAIRS = HEADS // 2
CHUNK = 128
ROWS = 32
DELAYS = (0, 1)
LOG2E = 1.4426950408889634
VECTORS = 256
SCALE = 1.0 / math.sqrt(3 * HEAD)
AXES = ("wide", "narrow")
norm_epsilon = 1e-06
bf16 = jnp.bfloat16
f32 = jnp.float32


def dot_nt(left, right):
    return lax.dot_general(left, right, (((1,), (1,)), ((), ())), preferred_element_type=f32)


def dot_nn(left, right):
    return lax.dot_general(left, right, (((1,), (0,)), ((), ())), preferred_element_type=f32)


def dot_tn(left, right):
    return lax.dot_general(left, right, (((0,), (0,)), ((), ())), preferred_element_type=f32)


def reverse_rows(flip, block):
    half = SEQ // 2
    return jnp.concatenate(
        [dot_nn(flip, block[half:]).astype(bf16), dot_nn(flip, block[:half]).astype(bf16)], axis=0
    )


def flip_matrix():
    half = SEQ // 2
    rows = lax.broadcasted_iota(jnp.int32, (half, half), 0)
    cols = lax.broadcasted_iota(jnp.int32, (half, half), 1)
    return jnp.where(rows + cols == half - 1, 1.0, 0.0).astype(bf16)


def skew(rows, base):
    return pltpu.roll(rows, base % SEQ, 1, stride=1, stride_axis=0)


def lane_tiles(block):
    return [block[:, t * CHUNK : (t + 1) * CHUNK] for t in range(SEQ // CHUNK)]


def clip_edges(moved, table, c, below):
    tiles = lane_tiles(moved)
    left = jnp.broadcast_to(table[:, :1], (CHUNK, CHUNK))
    right = jnp.broadcast_to(table[:, SEQ - 1 :], (CHUNK, CHUNK))
    if c == 0:
        tiles[2], tiles[3] = jnp.where(below, tiles[2], right), right
    elif c == 1:
        tiles[3] = jnp.where(below, tiles[3], right)
    elif c == 2:
        tiles[0] = jnp.where(below, left, tiles[0])
    else:
        tiles[0], tiles[1] = left, jnp.where(below, left, tiles[1])
    return jnp.concatenate(tiles, axis=1)


def fold_edges(moved, c, below):
    tiles = lane_tiles(moved)
    part = (2, 3, 0, 1)[c]
    zero = jnp.zeros_like(tiles[part])
    upper = c < 2
    if upper:
        outside, tiles[part] = jnp.where(below, zero, tiles[part]), jnp.where(below, tiles[part], zero)
    else:
        outside, tiles[part] = jnp.where(below, tiles[part], zero), jnp.where(below, zero, tiles[part])
    outside = [outside]
    if c in (0, 3):
        whole = 3 if c == 0 else 0
        outside.append(tiles[whole])
        tiles[whole] = zero
    edge, lane = (0, 0) if upper else (3, CHUNK - 1)
    outside = jnp.concatenate(outside, axis=1)
    lanes = lax.broadcasted_iota(jnp.int32, (outside.shape[1], CHUNK), 1)
    to_lane = jnp.where(lanes == lane, 1.0, 0.0).astype(bf16)
    tiles[edge] = tiles[edge] + dot_nn(outside, to_lane).astype(bf16)
    return jnp.concatenate(tiles, axis=1)


def weave(first, second):
    waiting = {0: [], 1: []}

    def emit(which, piece):
        store = piece() if piece is not None else None
        if store is not None:
            waiting[which].append(store)
        keep = DELAYS[which] if piece is not None else 0
        while len(waiting[which]) > keep:
            waiting[which].pop(0)()

    total = max(len(first), len(second))
    done = [0, 0]
    for step in range(1, total + 1):
        for which, pieces in ((1, second), (0, first)):
            while done[which] * total < step * len(pieces):
                emit(which, pieces[done[which]])
                done[which] += 1
    for which in (1, 0):
        emit(which, None)


def storing(ref, where, value):
    def store():
        ref[where] = value

    return store


def attend_kernel(
    len_ref, q_ref, k_ref, v_ref, pq_ref, pk_ref, ctx_ref, wide_ref, probs_ref, scale_ref,
    kp_a, kp_b, qp_a, qp_b, raw_a, raw_b, back_a, back_b, low_a, low_b,
):
    kp, qp, raw, back, low = (kp_a, kp_b), (qp_a, qp_b), (raw_a, raw_b), (back_a, back_b), (low_a, low_b)
    flip = flip_matrix()
    half = SEQ // 2
    lane_pair = lax.broadcasted_iota(jnp.int32, (1, PAIR), 1)
    rows = lax.broadcasted_iota(jnp.int32, (CHUNK, CHUNK), 0)
    cols = lax.broadcasted_iota(jnp.int32, (CHUNK, CHUNK), 1)
    strictly_below, below = cols < rows, cols <= rows
    places = lax.broadcasted_iota(jnp.int32, (1, SEQ), 1)
    pq_all = pq_ref[...]
    pk_flipped = reverse_rows(flip, pk_ref[...])
    units = [(seq, head) for seq in range(MICRO) for head in range(2)]
    heads = [
        (lane_pair >= head * HEAD) & (lane_pair < (head + 1) * HEAD) for head in range(2)
    ]
    hidden_keys = [jnp.where(places < len_ref[seq], 0.0, -1e30) for seq in range(MICRO)]

    def products(u):
        seq, head = units[u]
        slot = u % 2
        tokens = slice(seq * SEQ, (seq + 1) * SEQ)
        pieces = []
        for part in (slice(0, half), slice(half, SEQ)):
            def key_places(part=part):
                k_all = k_ref[tokens, :]
                k_head = jnp.where(heads[head], k_all, jnp.zeros_like(k_all))
                return storing(kp[slot], (slice(None), part), dot_nt(k_head, pq_all[part]).astype(bf16))

            def query_places(part=part):
                q_all = q_ref[tokens, :]
                q_head = jnp.where(heads[head], q_all, jnp.zeros_like(q_all))
                return storing(qp[slot], (slice(None), part), dot_nt(q_head, pk_flipped[part]).astype(bf16))

            def content(part=part):
                q_all = q_ref[tokens, :]
                q_head = jnp.where(heads[head], q_all, jnp.zeros_like(q_all))
                keys = slice(seq * SEQ + part.start, seq * SEQ + part.stop)
                return storing(raw[slot], (slice(None), part), dot_nt(q_head, k_ref[keys, :]))

            pieces += [key_places, query_places, content]
        return pieces

    def softmax(u):
        seq, head = units[u]
        slot = u % 2
        pieces = []
        for c in range(SEQ // CHUNK):
            def turn(c=c):
                part = slice(c * CHUNK, (c + 1) * CHUNK)
                table = kp[slot][part, :]
                moved = clip_edges(skew(table, c * CHUNK + 256), table, c, strictly_below)
                return storing(back[slot], (slice(None), part), moved.T)

            pieces.append(turn)
        for c in range(SEQ // CHUNK):
            def shift(c=c):
                part = slice(c * CHUNK, (c + 1) * CHUNK)
                table = qp[slot][part, :]
                return storing(
                    qp[slot], (part, slice(None)),
                    clip_edges(skew(table, c * CHUNK - 255), table, c, below),
                )

            pieces.append(shift)
        pieces.append(None)

        def normal(here):
            scores = (
                raw[slot][here, :]
                + (qp[slot][here, :].astype(f32) + back[slot][here, :].astype(f32))
                + hidden_keys[seq]
            )
            row_max = jnp.max(scores, axis=1, keepdims=True)
            exp_scores = jnp.exp2((scores - row_max) * (SCALE * LOG2E))
            return storing(low[slot], (here, slice(None)), exp_scores.astype(bf16))

        for start in range(0, SEQ, ROWS):
            pieces.append(functools.partial(normal, slice(start, start + ROWS)))
        return pieces

    def results(u):
        seq, head = units[u]
        slot = u % 2
        tokens = slice(seq * SEQ, (seq + 1) * SEQ)

        def context():
            v_all = v_ref[tokens, :]
            both = dot_nn(low[slot][...], jnp.concatenate([v_all, jnp.ones_like(v_all)], axis=1))
            scale = 1.0 / both[:, PAIR:]
            scale_ref[seq, head] = scale
            ctx = both[:, :PAIR] * scale
            if head == 1:
                ctx = jnp.where(heads[head], ctx, wide_ref[tokens, :])
                ctx_ref[tokens, :] = ctx.astype(bf16)
            wide_ref[tokens, :] = ctx

        def left():
            probs_ref[seq, head, :, :half] = dot_nn(low[slot][:, half:], flip).astype(bf16)

        def right():
            probs_ref[seq, head, :, half:] = dot_nn(low[slot][:, :half], flip).astype(bf16)

        return [context, left, right]

    count = len(units)
    for step in range(count + 2):
        matrix = products(step) if step < count else []
        if step >= 2:
            matrix = results(step - 2) + matrix
        vector = softmax(step - 1) if 1 <= step <= count else []
        weave(matrix, vector)


def attend(lengths, qkv, pos):
    qkv_block = lambda which: pl.BlockSpec((MICRO * SEQ, PAIR), lambda p, n: (0, which * PAIRS + p))
    pos_block = lambda which: pl.BlockSpec((SEQ, PAIR), lambda p, n: (0, which * PAIRS + p))
    square = lambda kind: [pltpu.VMEM((SEQ, SEQ), kind)] * 2
    return pl.pallas_call(
        attend_kernel,
        grid_spec=pltpu.PrefetchScalarGridSpec(
            num_scalar_prefetch=1,
            grid=(PAIRS,),
            in_specs=[qkv_block(0), qkv_block(1), qkv_block(2), pos_block(0), pos_block(1)],
            out_specs=[
                pl.BlockSpec((MICRO * SEQ, PAIR), lambda p, n: (0, p)),
                pl.BlockSpec((MICRO * SEQ, PAIR), lambda p, n: (0, p)),
                pl.BlockSpec((MICRO, 2, SEQ, SEQ), lambda p, n: (0, p, 0, 0)),
                pl.BlockSpec((MICRO, 2, SEQ, CHUNK), lambda p, n: (0, p, 0, 0)),
            ],
            scratch_shapes=square(bf16) + square(bf16) + square(f32) + square(bf16) + square(bf16),
        ),
        out_shape=[
            jax.ShapeDtypeStruct((MICRO * SEQ, D), bf16),
            jax.ShapeDtypeStruct((MICRO * SEQ, D), f32),
            jax.ShapeDtypeStruct((MICRO, HEADS, SEQ, SEQ), bf16),
            jax.ShapeDtypeStruct((MICRO, HEADS, SEQ, CHUNK), f32),
        ],
        compiler_params=pltpu.CompilerParams(vmem_limit_bytes=40 * 2**20),
        cost_estimate=pl.CostEstimate(
            flops=24 * 8 * 2 * SEQ * SEQ * PAIR,
            bytes_accessed=20 * 2**20,
            transcendentals=24 * SEQ * SEQ,
        ),
        name="attend",
    )(lengths, qkv, qkv, qkv, pos, pos)


def attend_back_kernel(
    q_ref, k_ref, v_ref, pq_ref, pk_ref, gc_ref, ctx_ref, probs_ref, scale_ref,
    gq_ref, gk_ref, gv_ref, gpq_ref, gpk_ref,
    raw_a, raw_b, grad_a, grad_b, moved_a, moved_b, turned_a, turned_b,
    inner_a, inner_b, q_t, k_t, gc_t, pq_t, pk_t, k_rev, v_rev, gq_t, gk_t, gv_t,
):
    raw, grad, moved, turned = (raw_a, raw_b), (grad_a, grad_b), (moved_a, moved_b), (turned_a, turned_b)
    inner = (inner_a, inner_b)
    flip = flip_matrix()
    half = SEQ // 2
    lane_pair = lax.broadcasted_iota(jnp.int32, (1, PAIR), 1)
    rows = lax.broadcasted_iota(jnp.int32, (CHUNK, CHUNK), 0)
    cols = lax.broadcasted_iota(jnp.int32, (CHUNK, CHUNK), 1)
    below = cols <= rows
    units = [(seq, head) for seq in range(MICRO) for head in range(2)]
    heads = [
        (lane_pair >= head * HEAD) & (lane_pair < (head + 1) * HEAD) for head in range(2)
    ]
    tokens = [slice(seq * SEQ, (seq + 1) * SEQ) for seq in range(MICRO)]
    pq_t[...] = pq_ref[...].T
    pk_t[...] = pk_ref[...].T

    def prepare(seq):
        v_rev[seq] = reverse_rows(flip, v_ref[tokens[seq], :])
        k_flipped = reverse_rows(flip, k_ref[tokens[seq], :])
        k_t[seq] = k_flipped.T
        q_t[seq] = q_ref[tokens[seq], :].T
        scale = jnp.where(heads[0], scale_ref[seq, 0], scale_ref[seq, 1])
        gc_t[seq] = (gc_ref[tokens[seq], :].astype(f32) * scale).astype(bf16).T

    def grads(u):
        seq, head = units[u]
        slot = u % 2
        pieces = []

        def start():
            if head == 0:
                prepare(seq)
            product = gc_ref[tokens[seq], :].astype(f32) * ctx_ref[tokens[seq], :]
            product = jnp.where(heads[head], product, 0.0)
            inner[slot][...] = jnp.broadcast_to(
                jnp.sum(product, axis=1, keepdims=True), (SEQ, CHUNK)
            )

        pieces.append(start)
        for part in (slice(0, half), slice(half, SEQ)):
            def values(part=part):
                gc_all = gc_ref[tokens[seq], :]
                gc_head = jnp.where(heads[head], gc_all, jnp.zeros_like(gc_all))
                return storing(raw[slot], (slice(None), part), dot_nt(gc_head, v_rev[seq, part, :]))

            pieces.append(values)
        pieces.append(None)
        for c in range(SEQ // CHUNK):
            for r in range(0, CHUNK, ROWS):
                def softmax(here=slice(c * CHUNK + r, c * CHUNK + r + ROWS)):
                    low, scale = inner[slot][here, :], scale_ref[seq, head, here, :]
                    tiles = [
                        (
                            probs_ref[seq, head, here, t : t + CHUNK].astype(f32)
                            * ((raw[slot][here, t : t + CHUNK] - low) * scale)
                        ).astype(bf16)
                        for t in range(0, SEQ, CHUNK)
                    ]
                    return storing(grad[slot], (here, slice(None)), jnp.concatenate(tiles, axis=1))

                pieces.append(softmax)
        pieces.append(None)

        def shift(c):
            part = slice(c * CHUNK, (c + 1) * CHUNK)
            table = fold_edges(skew(grad[slot][part, :], c * CHUNK - 255), c, below)
            return storing(moved[slot], (part, slice(None)), table)

        def turn(c):
            part = slice(c * CHUNK, (c + 1) * CHUNK)
            table = fold_edges(skew(grad[slot][:, part].T, c * CHUNK - 255), c, below)
            return storing(turned[slot], (part, slice(None)), table)

        for c in range(SEQ // CHUNK):
            pieces += [functools.partial(turn, c), functools.partial(shift, c)]
        return pieces

    def results(u):
        seq, head = units[u]
        slot = u % 2
        mine = slice(head * HEAD, (head + 1) * HEAD)

        def values():
            gv_t[seq, mine, :] = dot_nn(gc_t[seq, mine, :], probs_ref[seq, head]).astype(bf16)

        def keys():
            total = dot_nn(q_t[seq, mine, :], grad[slot][...])
            total = total + dot_nt(pq_t[mine, :], turned[slot][...])
            gk_t[seq, mine, :] = (total * SCALE).astype(bf16)

        def queries():
            total = dot_nt(k_t[seq, mine, :], grad[slot][...])
            total = total + dot_nt(pk_t[mine, :], moved[slot][...])
            gq_t[seq, mine, :] = (total * SCALE).astype(bf16)

        def key_places():
            total = dot_nn(q_t[seq, mine, :], moved[slot][...]) * SCALE
            gpk_ref[mine, :] = total if seq == 0 else gpk_ref[mine, :] + total

        def query_places():
            total = dot_nn(k_t[seq, mine, :], turned[slot][...]) * SCALE
            gpq_ref[mine, :] = total if seq == 0 else gpq_ref[mine, :] + total

        def finish():
            gq_ref[tokens[seq], :] = gq_t[seq].T
            for kept, out in ((gk_t, gk_ref), (gv_t, gv_ref)):
                out[tokens[seq], :] = jnp.concatenate(
                    [
                        dot_nn(kept[seq, :, half:], flip).astype(bf16),
                        dot_nn(kept[seq, :, :half], flip).astype(bf16),
                    ],
                    axis=1,
                ).T

        pieces = [values, keys, queries, key_places, query_places]
        return pieces + [finish] if head == 1 else pieces

    count = len(units)
    for step in range(count + 1):
        matrix = results(step - 1) if step >= 1 else []
        vector = grads(step) if step < count else []
        weave(matrix, vector)


def attend_back(qkv, pos, grad_context, context_wide, probs, scale):
    qkv_block = lambda which: pl.BlockSpec((MICRO * SEQ, PAIR), lambda p: (0, which * PAIRS + p))
    pos_block = lambda which: pl.BlockSpec((SEQ, PAIR), lambda p: (0, which * PAIRS + p))
    token_block = pl.BlockSpec((MICRO * SEQ, PAIR), lambda p: (0, p))
    table_block = pl.BlockSpec((PAIR, SEQ), lambda p: (p, 0))
    token_shape = jax.ShapeDtypeStruct((MICRO * SEQ, D), bf16)
    table_shape = jax.ShapeDtypeStruct((D, SEQ), f32)
    square = lambda kind: [pltpu.VMEM((SEQ, SEQ), kind)] * 2
    wide = pltpu.VMEM((MICRO, PAIR, SEQ), bf16)
    tall = pltpu.VMEM((MICRO, SEQ, PAIR), bf16)
    return pl.pallas_call(
        attend_back_kernel,
        grid=(PAIRS,),
        in_specs=[
            qkv_block(0), qkv_block(1), qkv_block(2), pos_block(0), pos_block(1),
            token_block, token_block,
            pl.BlockSpec((MICRO, 2, SEQ, SEQ), lambda p: (0, p, 0, 0)),
            pl.BlockSpec((MICRO, 2, SEQ, CHUNK), lambda p: (0, p, 0, 0)),
        ],
        out_specs=[token_block, token_block, token_block, table_block, table_block],
        out_shape=[token_shape, token_shape, token_shape, table_shape, table_shape],
        scratch_shapes=square(f32) + square(bf16) * 3
        + [pltpu.VMEM((SEQ, CHUNK), f32)] * 2
        + [wide, wide, wide, pltpu.VMEM((PAIR, SEQ), bf16), pltpu.VMEM((PAIR, SEQ), bf16)]
        + [tall, tall, wide, wide, wide],
        compiler_params=pltpu.CompilerParams(vmem_limit_bytes=40 * 2**20),
        cost_estimate=pl.CostEstimate(
            flops=24 * 16 * 2 * SEQ * SEQ * PAIR, bytes_accessed=24 * 2**20, transcendentals=0
        ),
        name="attend_back",
    )(qkv, qkv, qkv, pos, pos, grad_context, context_wide, probs, scale)


def weigh_kernel(
    x_ref, gq_ref, gk_ref, gv_ref, rel_ref, gpq_ref, gpk_ref, wq_ref, wk_ref, vec_ref,
    first_ref, second_ref, x_turned, rel_sum, rows_ref,
):
    step = pl.program_id(0)
    width = gq_ref.shape[1]

    @pl.when(step == 0)
    def begin():
        x_turned[...] = x_ref[...].T
        rel_sum[...] = jnp.zeros_like(rel_sum)
        rows_ref[...] = jnp.zeros_like(rows_ref)
        rows_ref[8:24, :] = vec_ref[...]

    token_ones = jnp.ones((8, MICRO * SEQ), bf16)
    place_ones = jnp.ones((8, SEQ), bf16)
    here = pl.ds(pl.multiple_of(step * width, width), width)
    row = lax.broadcasted_iota(jnp.int32, (8, width), 0)
    biases = jnp.zeros((8, width), f32)
    tables = ((gq_ref, gpq_ref, wq_ref), (gk_ref, gpk_ref, wk_ref))
    for which, (grad_ref, table_ref, weight_ref) in enumerate(tables):
        grad = grad_ref[...]
        table = table_ref[...].astype(bf16)
        total = dot_nn(x_turned[...], grad) + dot_nt(rel_ref[...], table)
        first_ref[:, pl.ds(pl.multiple_of(which * D + step * width, width), width)] = total.astype(bf16)
        rel_sum[...] += dot_nn(weight_ref[...], table)
        bias = dot_nn(token_ones, grad) + dot_nt(place_ones, table)
        biases = jnp.where(row == which, bias, biases)
    grad = gv_ref[...]
    second_ref[:, here] = dot_nn(x_turned[...], grad).astype(bf16)
    rows_ref[:8, here] = jnp.where(row == 2, dot_nn(token_ones, grad), biases)

    @pl.when(step == pl.num_programs(0) - 1)
    def end():
        second_ref[:, D : D + SEQ] = rel_sum[...].astype(bf16)
        second_ref[:, D + SEQ :] = rows_ref[...].T.astype(bf16)


def weigh(x, gq, gk, gv, rel_turned, gpq, gpk, qkv_weight, vectors):
    steps = 3
    width = D // steps
    whole = lambda shape: pl.BlockSpec(shape, lambda p: (0, 0))
    columns = lambda rows, which=0: pl.BlockSpec((rows, width), lambda p: (0, which * steps + p))
    tokens = MICRO * SEQ
    return pl.pallas_call(
        weigh_kernel,
        grid=(steps,),
        in_specs=[
            whole((tokens, D)), columns(tokens), columns(tokens), columns(tokens),
            whole((D, SEQ)),
            pl.BlockSpec((width, SEQ), lambda p: (p, 0)), pl.BlockSpec((width, SEQ), lambda p: (p, 0)),
            columns(D), columns(D, 1), whole((16, D)),
        ],
        out_specs=[whole((D, 2 * D)), whole((D, D + SEQ + CHUNK))],
        out_shape=[
            jax.ShapeDtypeStruct((D, 2 * D), bf16),
            jax.ShapeDtypeStruct((D, D + SEQ + CHUNK), bf16),
        ],
        scratch_shapes=[
            pltpu.VMEM((D, tokens), bf16), pltpu.VMEM((D, SEQ), f32), pltpu.VMEM((CHUNK, D), f32),
        ],
        compiler_params=pltpu.CompilerParams(vmem_limit_bytes=40 * 2**20),
        cost_estimate=pl.CostEstimate(
            flops=2 * D * D * (3 * tokens + 4 * SEQ), bytes_accessed=20 * 2**20, transcendentals=0
        ),
        name="weigh",
    )(x, gq, gk, gv, rel_turned, gpq, gpk, qkv_weight, qkv_weight, vectors)


def normalise(v):
    row_mean = jnp.mean(v, axis=-1, keepdims=True)
    centered = v - row_mean
    variance = jnp.mean(centered * centered, axis=-1, keepdims=True)
    rstd = lax.rsqrt(variance + norm_epsilon)
    return centered * rstd, rstd


def norm_back(normed, rstd, gain, grad):
    e = grad * gain
    grad_in = rstd * (
        e
        - jnp.mean(e, axis=-1, keepdims=True)
        - normed * jnp.mean(e * normed, axis=-1, keepdims=True)
    )
    return grad_in, jnp.sum(grad * normed, axis=0), jnp.sum(grad, axis=0)


def narrow_shifts(block, shift):
    size = lax.axis_size("narrow")
    return lax.ppermute(block, "narrow", [(i, (i + shift) % size) for i in range(size)])


def gather_rows(shard):
    size = lax.axis_size("narrow")
    me = lax.axis_index("narrow")
    rows, cols = shard.shape
    together = jnp.zeros((size * rows, cols), shard.dtype)
    for shift in range(size):
        block = narrow_shifts(shard, shift) if shift else shard
        owner = lax.rem(me - shift + size, size)
        together = lax.dynamic_update_slice(together, block, (owner * rows, 0))
    return lax.all_gather(together, "wide", axis=0, tiled=True)


def scatter_wide(full):
    return lax.psum_scatter(full, "wide", scatter_dimension=0, tiled=True)


def scatter_narrow_start(part):
    size = lax.axis_size("narrow")
    me = lax.axis_index("narrow")
    rows = part.shape[-2] // size
    pieces = []
    for shift in range(size):
        target = lax.rem(me + shift, size)
        block = lax.dynamic_slice_in_dim(part, target * rows, rows, part.ndim - 2)
        pieces.append(narrow_shifts(block, shift) if shift else block)
    return pieces


def scatter_narrow(part):
    return sum(piece.astype(f32) for piece in scatter_narrow_start(part))


def swap(block, bit):
    size = lax.axis_size("wide")
    return lax.ppermute(block, "wide", [(i, i ^ (1 << bit)) for i in range(size)])


def my_bit(bit):
    return lax.rem(lax.axis_index("wide") // (1 << bit), 2)


def wide_bits():
    return (lax.axis_size("wide") - 1).bit_length()


def split_bits(full):
    bits = wide_bits()
    return full.reshape((2,) * bits + (full.shape[0] >> bits, full.shape[1]))


def halve(part, bit, left):
    axis, mine = left.index(bit), my_bit(bit)
    keep = lax.dynamic_index_in_dim(part, mine, axis, keepdims=False)
    send = lax.dynamic_index_in_dim(part, 1 - mine, axis, keepdims=False)
    left.remove(bit)
    return (keep.astype(f32) + swap(send, bit).astype(f32)).astype(bf16)


def all_bits():
    return list(range(wide_bits()))[::-1]


def body(
    hidden_in, cotangent, seq_lengths,
    query_weight, query_bias, key_weight, key_bias, value_weight, value_bias,
    out_weight, out_bias, first_gain, first_shift, up_weight, up_bias,
    down_weight, down_bias, second_gain, second_shift, rel_table,
):
    tokens = MICRO * SEQ
    x = hidden_in.reshape(tokens, D)
    cot = cotangent.reshape(tokens, D).astype(f32)
    lengths = seq_lengths.reshape(MICRO)
    share = query_weight.shape[0]
    vectors = [
        query_bias, key_bias, value_bias, out_bias, first_gain, first_shift,
        down_bias, second_gain, second_shift,
    ]
    vectors = jnp.concatenate([jnp.stack(vectors), up_bias.reshape(4, share)], axis=0)
    vectors = jnp.pad(vectors, ((0, VECTORS - vectors.shape[0]), (0, 0)))
    first_pack = gather_rows(
        jnp.concatenate(
            [
                query_weight, key_weight, value_weight,
                jnp.concatenate([rel_table, vectors], axis=0).T,
            ],
            axis=1,
        )
    )
    second_pack = gather_rows(jnp.concatenate([out_weight, up_weight], axis=1))
    down_full = gather_rows(down_weight)
    qkv_weight = first_pack[:, : 3 * D]
    rel_turned = first_pack[:, 3 * D : 3 * D + SEQ]
    out_full = second_pack[:, :D]
    up_full = second_pack[:, D:]
    vector_rows = first_pack[:, 3 * D + SEQ :].T.astype(f32)
    qkv_bias = vector_rows[:3].reshape(3 * D)
    out_b, gain_1, shift_1, down_b, gain_2, shift_2 = (vector_rows[i] for i in range(3, 9))
    up_b = jnp.transpose(vector_rows[9:13].reshape(4, D // share, share), (1, 0, 2)).reshape(4 * D)

    qkv = (dot_nn(x, qkv_weight) + qkv_bias).astype(bf16)
    pos = (dot_tn(rel_turned, qkv_weight[:, : 2 * D]) + qkv_bias[: 2 * D]).astype(bf16)
    context, context_wide, probs, probs_scale = attend(lengths, qkv, pos)

    first_in = x.astype(f32) + dot_nn(context, out_full) + out_b
    normed_1, rstd_1 = normalise(first_in)
    hidden = normed_1 * gain_1 + shift_1
    hidden_low = hidden.astype(bf16)
    upward = dot_nn(hidden_low, up_full) + up_b
    cdf = 0.5 * (1.0 + lax.erf(upward * math.sqrt(0.5)))
    activated_low = (upward * cdf).astype(bf16)
    slope = (cdf + upward * jnp.exp(-0.5 * upward * upward) * (1 / math.sqrt(2 * math.pi))).astype(
        bf16
    )
    second_in = hidden + dot_nn(activated_low, down_full) + down_b
    normed_2, rstd_2 = normalise(second_in)
    hidden_out = (normed_2 * gain_2 + shift_2).astype(bf16)

    grad_second, grad_gain_2, grad_shift_2 = norm_back(normed_2, rstd_2, gain_2, cot)
    grad_feed = grad_second.astype(bf16)
    grad_down_bias = jnp.sum(grad_feed.astype(f32), axis=0)
    grad_down = dot_tn(activated_low, grad_feed).astype(bf16)
    grad_up = (dot_nt(grad_feed, down_full) * slope.astype(f32)).astype(bf16)
    grad_up_bias = jnp.sum(grad_up.astype(f32), axis=0)
    grad_up_weight = dot_tn(hidden_low, grad_up).astype(bf16)
    grad_hidden = grad_second + dot_nt(grad_up, up_full)
    grad_first, grad_gain_1, grad_shift_1 = norm_back(normed_1, rstd_1, gain_1, grad_hidden)
    grad_branch = grad_first.astype(bf16)
    grad_out_bias = jnp.sum(grad_branch.astype(f32), axis=0)
    grad_out = dot_tn(context, grad_branch).astype(bf16)
    grad_context = dot_nt(grad_branch, out_full).astype(bf16)

    grad_second_pack = jnp.concatenate([grad_out, grad_up_weight], axis=1)
    down_part = scatter_wide(grad_down)
    grad_context, grad_second_pack, down_part = lax.optimization_barrier(
        (grad_context, grad_second_pack, down_part)
    )
    down_pieces = scatter_narrow_start(down_part)
    second_part = scatter_wide(grad_second_pack)

    gq, gk, gv, gpq, gpk = attend_back(
        qkv, pos, grad_context, context_wide, probs, probs_scale
    )
    grad_up_bias = jnp.transpose(grad_up_bias.reshape(D // share, 4, share), (1, 0, 2))
    vector_grads = jnp.concatenate(
        [
            jnp.stack(
                [
                    grad_out_bias, grad_gain_1, grad_shift_1,
                    grad_down_bias, grad_gain_2, grad_shift_2,
                ]
            ),
            grad_up_bias.reshape(4, D),
            jnp.zeros((6, D), f32),
        ],
        axis=0,
    )
    gq, down_pieces = lax.optimization_barrier((gq, down_pieces))
    down_sum = sum(piece.astype(f32) for piece in down_pieces)
    first_half, second_half = weigh(
        x, gq, gk, gv, rel_turned, gpq, gpk, qkv_weight, vector_grads
    )
    upper = all_bits()[:-1]
    halves = [
        [split_bits(first_half), all_bits(), [0] + upper],
        [split_bits(second_half), all_bits(), [0] + upper[::-1]],
    ]

    def halve_both():
        for entry in halves:
            entry[0] = halve(entry[0], entry[2].pop(0), entry[1])

    def together(*others):
        kept = lax.optimization_barrier((halves[0][0], halves[1][0]) + others)
        halves[0][0], halves[1][0] = kept[:2]
        return kept[2:]

    halve_both()
    gq, gk, gv, second_part = together(gq, gk, gv, second_part)
    second_pieces = scatter_narrow_start(second_part)
    grad_inputs = grad_first + dot_nt(jnp.concatenate([gq, gk, gv], axis=1), qkv_weight)
    halve_both()
    grad_inputs, *second_pieces = together(grad_inputs, *second_pieces)
    second_sum = sum(piece.astype(f32) for piece in second_pieces)
    while halves[0][2]:
        halve_both()
    last_sum = scatter_narrow(jnp.concatenate([halves[0][0], halves[1][0]], axis=1))
    turned = last_sum[:, 3 * D :].T
    vec = lambda i: turned[SEQ + i]
    return (
        hidden_out.reshape(hidden_in.shape),
        grad_inputs.reshape(hidden_in.shape),
        last_sum[:, :D], vec(0),
        last_sum[:, D : 2 * D], vec(1),
        last_sum[:, 2 * D : 3 * D], vec(2),
        second_sum[:, :D], vec(8), vec(9), vec(10),
        second_sum[:, D:],
        turned[SEQ + 14 : SEQ + 18].reshape(4 * share),
        down_sum, vec(11), vec(12), vec(13),
        turned[:SEQ],
    )


def solution(mesh):
    tokens = P(None, AXES, None, None)
    rows = P(AXES, None)
    vector = P(AXES)
    weights = (
        rows, vector, rows, vector, rows, vector, rows, vector, vector, vector,
        rows, vector, rows, vector, vector, vector, P(None, AXES),
    )
    return jax.shard_map(
        body,
        mesh=mesh,
        in_specs=(tokens, tokens, P(None, AXES)) + weights,
        out_specs=(tokens, tokens) + weights,
        check_vma=False,
    )
```

time: 435 us -> 374 us (0.86)
  Pallas kernels: 142 us -> 88.1 us
  matrix products: 97.8 us -> 85.9 us
  starting transfers between devices: 17.9 us -> 23.6 us
  local copies, waits for them, and re-layouts: 41.3 us -> 46.1 us
    reduce_scatter x3 -> x2, waiting for transfers between devices: 40.2 us -> 5.39 us  [scatter_wide(): return lax.psum_scatter(full, 'wide', scatter_dimension=0, tiled=True)]
    pallas_call x1 -> x2, Pallas kernels: 76.9 us -> 48.2 us  [the longest x1 36.5 us: attend_back(): pl.pallas_call(attend_back_kernel, grid=(PAIRS,), in_specs=[qkv_block(0),...]
    pallas_call x1, Pallas kernels: 65.1 us -> 39.9 us  [attend(): pl.pallas_call(attend_kernel, grid_spec=pltpu.PrefetchScalarGridSpec(num_...]
    all_gather x3, waiting for transfers between devices: 3.07 us -> 19.9 us  [gather_rows(): return lax.all_gather(together, 'wide', axis=0, tiled=True)]
    ppermute x0 -> x6, waiting for transfers between devices: none -> 10.2 us  [swap(): return lax.ppermute(block, 'wide', [(i, i ^ 1 << bit) for i in range(size)])]
    ppermute x0 -> x6, starting transfers between devices: none -> 5.93 us  [swap(): return lax.ppermute(block, 'wide', [(i, i ^ 1 << bit) for i in range(size)])]
    slice x4, local copies, waits for them, and re-layouts: 0.27 us -> 5.4 us  [the longest x1 4.07 us: body(): qkv_weight = first_pack[:, :3 * D]]
    dot_general x5 -> x4, matrix products: 42.1 us -> 37.5 us  [dot_nt(): lax.dot_general(left, right, (((1,), (1,)), ((), ())), preferred_element_...]
  transfers between devices with their start and end apart: 24 -> 29, of which waited for: 16 -> 21; matrix products, arithmetic and copies ran while one was open for 25% -> 27% of each run, Pallas kernels for 33% -> 24%
where the time goes in v1:
time: 374 us; the launch traced here: 368 us
  waiting for transfers between devices  91.8 us (25%)
  Pallas kernels  88.1 us (24%)
  matrix products  85.9 us (23%)
  local copies, waits for them, and re-layouts  46.1 us (12%)
  starting transfers between devices  23.6 us (6%)
  other arithmetic  17.6 us (5%)
  between operations  14.9 us (4%)
    ppermute x18, waiting for transfers between devices, narrow_shifts(): lax.ppermute(block, 'narrow', [(i, (i + shift) % size) for i in range(siz...  56.2 us
    pallas_call x1, Pallas kernels, attend(): pl.pallas_call(attend_kernel, grid_spec=pltpu.PrefetchScalarGridSpec(num_...  39.9 us
    dot_general x4, matrix products, dot_nt(): lax.dot_general(left, right, (((1,), (1,)), ((), ())), preferred_element_...  37.5 us
    pallas_call x1, Pallas kernels, attend_back(): pl.pallas_call(attend_back_kernel, grid=(PAIRS,), in_specs=[qkv_block(0),...  36.5 us
    dot_general x4, matrix products, dot_nn(): lax.dot_general(left, right, (((1,), (0,)), ((), ())), preferred_element_...  26.6 us
    dot_general x4, matrix products, dot_tn(): lax.dot_general(left, right, (((0,), (0,)), ((), ())), preferred_element_...  21.8 us
    all_gather x3, waiting for transfers between devices, gather_rows(): return lax.all_gather(together, 'wide', axis=0, tiled=True)  19.9 us
    unnamed x82, local copies, waits for them, and re-layouts  18.2 us
  transfers between devices with their start and end apart: 29, of which 21 were waited for; matrix products, arithmetic and copies ran while one was open for 27% of the time, Pallas kernels for 24%

profile of v1, /device:TPU:9, one launch (start us, length us, event | category | flops | bytes accessed | tf_op | source)
XLA Modules:
  0.0 368.0 jit_solution(15308191063083875133)
XLA Ops:
  21.4 8.6 %collective-permute-done.1 = bf16[24,3072]{1,0:T(8,128)(2,1)S(1)} collective-permute-done((bf16[24,3072]{1,0:T(8,128)(2,1)S(1)}, bf16[24,3072]{1,0:T(8,128)(2,1)S(1)}, u32[]{:S(2)}, u32[]{:S(2)}) %collective-permute-start.1) | collective-permute-done | bytes 147488 | tf_op jit(solution)/shard_map/ppermute | solution.py:532
  30.0 2.8 collective-permute-done.2
  37.3 3.8 %collective-permute-done.3 = bf16[24,3840]{1,0:T(8,128)(2,1)S(1)} collective-permute-done((bf16[24,3840]{1,0:T(8,128)(2,1)S(1)}, bf16[24,3840]{1,0:T(8,128)(2,1)S(1)}, u32[]{:S(2)}, u32[]{:S(2)}) %collective-permute-start.3) | collective-permute-done | bytes 184352 | tf_op jit(solution)/shard_map/ppermute | solution.py:532
  41.1 10.0 %collective-permute-done.4 = bf16[24,3840]{1,0:T(8,128)(2,1)S(1)} collective-permute-done((bf16[24,3840]{1,0:T(8,128)(2,1)S(1)}, bf16[24,3840]{1,0:T(8,128)(2,1)S(1)}, u32[]{:S(2)}, u32[]{:S(2)}) %collective-permute-start.4) | collective-permute-done | bytes 184352 | tf_op jit(solution)/shard_map/ppermute | solution.py:532
  51.1 1.6 collective-permute-done.5
  53.7 1.6 collective-permute-start.7
  56.8 1.8 collective-permute-done.6
  58.7 7.6 %collective-permute-done.7 = bf16[96,768]{1,0:T(8,128)(2,1)S(1)} collective-permute-done((bf16[96,768]{1,0:T(8,128)(2,1)S(1)}, bf16[96,768]{1,0:T(8,128)(2,1)S(1)}, u32[]{:S(2)}, u32[]{:S(2)}) %collective-permute-start.7) | collective-permute-done | bytes 147488 | tf_op jit(solution)/shard_map/ppermute | solution.py:532
  66.3 2.9 collective-permute-done.8
  70.1 3.1 all-gather.4.cloned.1.call-done
  77.3 3.5 fusion.23.pq_ref.pk_ref
  81.1 4.3 %fusion.5.q_ref.k_ref.v_ref = bf16[1024,2304]{1,0:T(8,128)(2,1)S(1)} fusion(bf16[1024,768]{1,0:T(8,128)(2,1)S(1)} %bitcast.94, f32[2304]{0:T(1024)S(1)} %add.285, bf16[768,3072]{1,0:T(8,128)(2,1)S(1)} %copy-done.19), kind=kOutput, calls=%fused_computation.14 | convolution fusion | flops 3628597248 | bytes 9842688 | tf_op jit(solution)/shard_map/dot_general | solution.py:35
  85.4 39.9 %attend.1 = (bf16[1024,768]{1,0:T(8,128)(2,1)S(1)}, f32[1024,768]{1,0:T(8,128)S(1)}, bf16[2,12,512,512]{3,2,1,0:T(8,128)(2,1)}, f32[2,12,512,128]{3,2,1,0:T(8,128)}) custom-call(s32[2]{0:T(128)S(1)} %bitcast.97, bf16[1024,2304]{1,0:T(8,128)(2,1)S(1)} %fusion.5.q_ref.k_ref.v_ref, bf16[1024,2304]{1,0:T(8,128)(2,1)S(1)} %fusion.5.q_ref.k_ref.v_ref, ...), custom_call_target="tpu_custom_call" | custom-call | flops 12884901888 | bytes 20971520 | tf_op jit(solution)/shard_map/attend/pallas_call | solution.py:250
  125.3 2.1 copy-done.11
  127.4 1.7 copy-done.12
  129.1 3.0 fusion.59
  133.8 9.8 %multiply_convert_fusion.1 = (bf16[1024,3072]{1,0:T(8,128)(2,1)}, f32[1024,3072]{1,0:T(8,128)}) fusion(f32[3072]{0:T(1024)S(1)} %add.299, bf16[768,3840]{1,0:T(8,128)(2,1)S(1)} %bitcast.116, f32[1024,768]{1,0:T(8,128)S(1)} %get-tuple-element.168, f32[768]{0:T(1024)S(1)} %get-tuple-element.132, f32[768]{0:T(1024)S(1)} %get-tuple-element.133, ...), kind=kOutput, calls=%fused_computation.8 | convolution fusion | flops 4854644736 | bytes 26767360 | tf_op jit(solution)/shard_map/dot_general | solution.py:35
  143.6 16.8 %all-gather.8.cloned.1.call-done = bf16[3072,768]{1,0:T(8,128)(2,1)} async-done(((bf16[384,768]{1,0:T(8,128)(2,1)}), bf16[3072,768]{1,0:T(8,128)(2,1)}) %all-gather.8.cloned.1.call-update) | async-done | bytes 4718608 | tf_op jit(solution)/shard_map/all_gather | solution.py:544
  160.4 9.5 %fusion.60 = (f32[1024]{0:T(1024)S(1)}, f32[1024,768]{1,0:T(8,128)S(1)}) fusion(f32[768]{0:T(1024)S(1)} %get-tuple-element.131, bf16[1024,3072]{1,0:T(8,128)(2,1)} %get-tuple-element.169, bf16[3072,768]{1,0:T(8,128)(2,1)} %all-gather.8.cloned.1.call-done, f32[768]{0:T(1024)S(1)} %get-tuple-element.132, f32[768]{0:T(1024)S(1)} %get-tuple-element.133, ...), kind=kOutput, calls=%fused_computation.158 | convolution fusion | flops 4837342208 | bytes 17323008 | tf_op jit(solution)/shard_map/dot_general | solution.py:35
  172.6 2.3 convert_reduce_fusion.2
  175.0 1.8 copy-done.22
  176.7 7.0 %convolution_convert_fusion = bf16[3072,768]{1,0:T(8,128)(2,1)} fusion(bf16[1024,3072]{1,0:T(8,128)(2,1)S(1)} %bitcast.119, f32[1024,768]{1,0:T(8,128)S(1)} %get-tuple-element.145), kind=kOutput, calls=%fused_computation.12 | convolution fusion | flops 4834983936 | bytes 14155776 | tf_op jit(solution)/shard_map/dot_general | solution.py:39
  183.9 13.8 %convert_reduce_fusion = (f32[3072]{0:T(1024)S(1)}, bf16[1024,3072]{1,0:T(8,128)(2,1)S(1)}) fusion(f32[1024,3072]{1,0:T(8,128)} %get-tuple-element.170, f32[3072]{0:T(1024)S(1)} %add.299, bf16[3072,768]{1,0:T(8,128)(2,1)} %all-gather.8.cloned.1.call-done, f32[1024,768]{1,0:T(8,128)} %copy-done.22), kind=kOutput, calls=%fused_computation.6 | convolution fusion | flops 4879807488 | bytes 26763264 | tf_op jit(solution)/shard_map/dot_general | solution.py:31
  197.7 10.7 %multiply_reduce_fusion = (f32[768]{0:T(1024)S(1)}, f32[1024]{0:T(1024)S(1)}, f32[1024]{0:T(1024)S(1)}, f32[768]{0:T(1024)S(1)}, f32[1024,768]{1,0:T(8,128)S(1)}) fusion(f32[1024,768]{1,0:T(8,128)S(1)} %copy-done.17, f32[1024]{0:T(1024)S(1)} %add_rsqrt_fusion.1, f32[1024]{0:T(1024)S(1)} %broadcast_multiply_fusion.4, f32[768]{0:T(1024)S(1)} %get-tuple-element.133, ...), kind=kOutput, calls=%fused_computation.38 | convolution fusion | flops 4839698432 | bytes 20472832 | tf_op jit(solution)/shard_map/dot_general | solution.py:31
  209.5 1.7 copy-done.24
  211.2 2.5 convolution_convert_fusion.3
  213.7 1.6 copy.71
  215.3 5.1 %convolution_convert_fusion.2.gc_ref = bf16[1024,768]{1,0:T(8,128)(2,1)} fusion(bf16[768,3840]{1,0:T(8,128)(2,1)} %all-gather.6.cloned.1.call-done, f32[1024,768]{1,0:T(8,128)} %copy-done.24), kind=kOutput, calls=%fused_computation.60 | convolution fusion | flops 1209532416 | bytes 5898240 | tf_op jit(solution)/shard_map/dot_general | solution.py:31
  220.3 8.8 %convolution_convert_fusion.1 = bf16[768,3072]{1,0:T(8,128)(2,1)S(1)} fusion(bf16[1024,3072]{1,0:T(8,128)(2,1)} %copy-done.35, f32[1024,768]{1,0:T(8,128)S(1)} %copy-done.18, f32[768]{0:T(1024)S(1)} %get-tuple-element.132, f32[768]{0:T(1024)S(1)} %get-tuple-element.133, f32[1024]{0:T(1024)S(1)} %add_rsqrt_fusion.1, f32[1024]{0:T(1024)S(1)} %broadcast_multiply_fusion.4), kind=kOutput, calls=%fused_computation.13 | convolution fusion | flops 4838129664 | bytes 14170112 | tf_op jit(solution)/shard_map/dot_general | solution.py:39
  229.1 2.9 pad_maximum_fusion
  232.0 5.4 %reduce-scatter.3.cloned.1.call-done = bf16[384,768]{1,0:T(8,128)(2,1)} async-done(((bf16[3072,768]{1,0:T(8,128)(2,1)}), bf16[384,768]{1,0:T(8,128)(2,1)}) %reduce-scatter.3.cloned.1.call-update) | async-done | bytes 589840 | tf_op jit(solution)/shard_map/reduce_scatter | solution.py:548
  237.5 4.1 %slice.131.wq_ref.wk_ref = bf16[768,2304]{1,0:T(8,128)(2,1)} slice(bf16[768,3072]{1,0:T(8,128)(2,1)} %all-gather.4.cloned.1.call-done), slice={[0:768], [0:2304]} | slice | bytes 7077888 | tf_op jit(solution)/shard_map/slice | solution.py:625
  243.3 2.2 collective-permute-start.10
  248.4 1.6 copy-done.4
  250.0 2.3 copy-done.13
  252.4 36.5 %attend_back.1 = (bf16[1024,768]{1,0:T(8,128)(2,1)S(1)}, bf16[1024,768]{1,0:T(8,128)(2,1)S(1)}, bf16[1024,768]{1,0:T(8,128)(2,1)S(1)}, f32[768,512]{1,0:T(8,128)S(1)}, f32[768,512]{1,0:T(8,128)S(1)}) custom-call(bf16[1024,2304]{1,0:T(8,128)(2,1)} %copy-done.11, bf16[1024,2304]{1,0:T(8,128)(2,1)} %copy-done.11, bf16[1024,2304]{1,0:T(8,128)(2,1)} %copy-done.11, ...), custom_call_target="tpu_custom_call" | custom-call | flops 25769803776 | bytes 25165824 | tf_op jit(solution)/shard_map/attend_back/pallas_call | solution.py:420
  289.0 11.7 %weigh.1 = (bf16[768,1536]{1,0:T(8,128)(2,1)}, bf16[768,1408]{1,0:T(8,128)(2,1)S(1)}) custom-call(bf16[1024,768]{1,0:T(8,128)(2,1)S(1)} %bitcast.96, bf16[1024,768]{1,0:T(8,128)(2,1)S(1)} %get-tuple-element.68.gq_ref, bf16[1024,768]{1,0:T(8,128)(2,1)S(1)} %get-tuple-element.69.gk_ref, bf16[1024,768]{1,0:T(8,128)(2,1)S(1)} %get-tuple-element.70.gv_ref, ...), custom_call_target="tpu_custom_call" | custom-call | flops 6039797760 | bytes 20971520 | tf_op jit(solution)/shard_map/weigh/pallas_call | solution.py:487
  301.1 1.7 collective-permute-start.13
  306.4 1.6 collective-permute-done.12
  307.9 2.9 fusion.26
  315.9 2.3 collective-permute-start.17
  319.5 7.9 %fusion.31 = f32[1024,768]{1,0:T(8,128)} fusion(f32[1024,768]{1,0:T(8,128)} %copy-done.24, bf16[1024,768]{1,0:T(8,128)(2,1)S(1)} %copy-done.10, bf16[1024,768]{1,0:T(8,128)(2,1)S(1)} %copy-done.8, bf16[1024,768]{1,0:T(8,128)(2,1)S(1)} %copy-done.6, bf16[768,3072]{1,0:T(8,128)(2,1)} %all-gather.4.cloned.1.call-done), kind=kOutput, calls=%fused_computation.59 | convolution fusion | flops 3638820864 | bytes 14548992 | tf_op jit(solution)/shard_map/dot_general | solution.py:31
  328.9 2.3 collective-permute-done.17
  331.1 4.1 %collective-permute-done.18 = bf16[24,3840]{1,0:T(8,128)(2,1)S(1)} collective-permute-done((bf16[24,3840]{1,0:T(8,128)(2,1)S(1)}, bf16[24,3840]{1,0:T(8,128)(2,1)S(1)}, u32[]{:S(2)}, u32[]{:S(2)}) %collective-permute-start.18) | collective-permute-done | bytes 184352 | tf_op jit(solution)/shard_map/ppermute | solution.py:532
  337.7 5.2 %collective-permute-done.20 = bf16[96,1408]{1,0:T(8,128)(2,1)S(1)} collective-permute-done((bf16[96,1408]{1,0:T(8,128)(2,1)S(1)}, bf16[96,1408]{1,0:T(8,128)(2,1)S(1)}, u32[]{:S(2)}, u32[]{:S(2)}) %collective-permute-start.20) | collective-permute-done | bytes 270368 | tf_op jit(solution)/shard_map/ppermute | solution.py:569
  342.9 2.3 collective-permute-done.19
  349.4 2.4 collective-permute-done.22
  351.7 6.6 %collective-permute-done.23 = bf16[24,2944]{1,0:T(8,128)(2,1)S(1)} collective-permute-done((bf16[24,2944]{1,0:T(8,128)(2,1)S(1)}, bf16[24,2944]{1,0:T(8,128)(2,1)S(1)}, u32[]{:S(2)}, u32[]{:S(2)}) %collective-permute-start.23) | collective-permute-done | bytes 141344 | tf_op jit(solution)/shard_map/ppermute | solution.py:532
  (210 shorter events, 57.7 us)
Async XLA Ops:
  7.2 46.5 %copy-start.34 = (bf16[96,768]{1,0:T(8,128)(2,1)S(1)}, bf16[96,768]{1,0:T(8,128)(2,1)}, u32[]{:S(2)}) copy-start(bf16[96,768]{1,0:T(8,128)(2,1)} %param.35) | copy-start | bytes 442372
  7.2 66.0 %all-gather.4.cloned.1.call-start = ((), (), s32[]{:S(2)}) async-start(), calls=%async_computation.2 | async-start | bytes 5308416 | tf_op jit(solution)/shard_map/all_gather | solution.py:544
  16.6 4.8 %collective-permute-start = (bf16[24,3072]{1,0:T(8,128)(2,1)S(1)}, bf16[24,3072]{1,0:T(8,128)(2,1)S(1)}, u32[]{:S(2)}, u32[]{:S(2)}) collective-permute-start(bf16[24,3072]{1,0:T(8,128)(2,1)S(1)} %get-tuple-element.165), channel_id=1, source_target_pairs={{0,1},{1,2},{2,3},{3,0},{4,5},{5,6},{6,7},{7,4},{8,9},{9,10},{10,1... | collective-permute-start | bytes 442376 | tf_op jit(solution)/shard_map/ppermute | solution.py:532
  17.9 12.0 %collective-permute-start.1 = (bf16[24,3072]{1,0:T(8,128)(2,1)S(1)}, bf16[24,3072]{1,0:T(8,128)(2,1)S(1)}, u32[]{:S(2)}, u32[]{:S(2)}) collective-permute-start(bf16[24,3072]{1,0:T(8,128)(2,1)S(1)} %get-tuple-element.165), channel_id=1, source_target_pairs={{0,2},{1,3},{2,0},{3,1},{4,6},{5,7},{6,4},{7,5},{8,10},{9,11},{10,... | collective-permute-start | bytes 442376 | tf_op jit(solution)/shard_map/ppermute | solution.py:532
  19.0 13.7 %collective-permute-start.2 = (bf16[24,3072]{1,0:T(8,128)(2,1)S(1)}, bf16[24,3072]{1,0:T(8,128)(2,1)S(1)}, u32[]{:S(2)}, u32[]{:S(2)}) collective-permute-start(bf16[24,3072]{1,0:T(8,128)(2,1)S(1)} %get-tuple-element.165), channel_id=1, source_target_pairs={{0,3},{1,0},{2,1},{3,2},{4,7},{5,4},{6,5},{7,6},{8,11},{9,8},{10,9... | collective-permute-start | bytes 442376 | tf_op jit(solution)/shard_map/ppermute | solution.py:532
  33.6 95.5 %all-gather.6.cloned.1.call-start = ((), (), s32[]{:S(2)}) async-start(), calls=%async_computation.3 | async-start | bytes 6635520 | tf_op jit(solution)/shard_map/all_gather | solution.py:544
  35.4 5.8 %collective-permute-start.3 = (bf16[24,3840]{1,0:T(8,128)(2,1)S(1)}, bf16[24,3840]{1,0:T(8,128)(2,1)S(1)}, u32[]{:S(2)}, u32[]{:S(2)}) collective-permute-start(bf16[24,3840]{1,0:T(8,128)(2,1)S(1)} %constant_dynamic-update-slice_fusion.12), channel_id=1, source_target_pairs={{0,1},{1,2},{2,3},{3,0},{4,5},{5,6},{6,7},{7,4},{8,9},{9,10},{10,1... | collective-permute-start | bytes 552968 | tf_op jit(solution)/shard_map/ppermute | solution.py:532
  35.4 15.7 %collective-permute-start.4 = (bf16[24,3840]{1,0:T(8,128)(2,1)S(1)}, bf16[24,3840]{1,0:T(8,128)(2,1)S(1)}, u32[]{:S(2)}, u32[]{:S(2)}) collective-permute-start(bf16[24,3840]{1,0:T(8,128)(2,1)S(1)} %constant_dynamic-update-slice_fusion.12), channel_id=1, source_target_pairs={{0,2},{1,3},{2,0},{3,1},{4,6},{5,7},{6,4},{7,5},{8,10},{9,11},{10,... | collective-permute-start | bytes 552968 | tf_op jit(solution)/shard_map/ppermute | solution.py:532
  35.8 16.9 %collective-permute-start.5 = (bf16[24,3840]{1,0:T(8,128)(2,1)S(1)}, bf16[24,3840]{1,0:T(8,128)(2,1)S(1)}, u32[]{:S(2)}, u32[]{:S(2)}) collective-permute-start(bf16[24,3840]{1,0:T(8,128)(2,1)S(1)} %constant_dynamic-update-slice_fusion.12), channel_id=1, source_target_pairs={{0,3},{1,0},{2,1},{3,2},{4,7},{5,4},{6,5},{7,6},{8,11},{9,8},{10,9... | collective-permute-start | bytes 552968 | tf_op jit(solution)/shard_map/ppermute | solution.py:532
  53.6 106.8 %all-gather.8.cloned.1.call-start = ((), (), s32[]{:S(2)}) async-start(), calls=%async_computation.4 | async-start | bytes 5308416 | tf_op jit(solution)/shard_map/all_gather | solution.py:544
  53.7 5.0 %collective-permute-start.6 = (bf16[96,768]{1,0:T(8,128)(2,1)S(1)}, bf16[96,768]{1,0:T(8,128)(2,1)S(1)}, u32[]{:S(2)}, u32[]{:S(2)}) collective-permute-start(bf16[96,768]{1,0:T(8,128)(2,1)S(1)} %copy-done.34), channel_id=1, source_target_pairs={{0,1},{1,2},{2,3},{3,0},{4,5},{5,6},{6,7},{7,4},{8,9},{9,10},{10,1... | collective-permute-start | bytes 442376 | tf_op jit(solution)/shard_map/ppermute | solution.py:532
  53.7 12.5 %collective-permute-start.7 = (bf16[96,768]{1,0:T(8,128)(2,1)S(1)}, bf16[96,768]{1,0:T(8,128)(2,1)S(1)}, u32[]{:S(2)}, u32[]{:S(2)}) collective-permute-start(bf16[96,768]{1,0:T(8,128)(2,1)S(1)} %copy-done.34), channel_id=1, source_target_pairs={{0,2},{1,3},{2,0},{3,1},{4,6},{5,7},{6,4},{7,5},{8,10},{9,11},{10,... | collective-permute-start | bytes 442376 | tf_op jit(solution)/shard_map/ppermute | solution.py:532
  55.3 13.8 %collective-permute-start.8 = (bf16[96,768]{1,0:T(8,128)(2,1)S(1)}, bf16[96,768]{1,0:T(8,128)(2,1)S(1)}, u32[]{:S(2)}, u32[]{:S(2)}) collective-permute-start(bf16[96,768]{1,0:T(8,128)(2,1)S(1)} %copy-done.34), channel_id=1, source_target_pairs={{0,3},{1,0},{2,1},{3,2},{4,7},{5,4},{6,5},{7,6},{8,11},{9,8},{10,9... | collective-permute-start | bytes 442376 | tf_op jit(solution)/shard_map/ppermute | solution.py:532
  70.0 167.4 %reduce-scatter.3.cloned.1.call-start = ((), (), s32[]{:S(2)}) async-start(), calls=%async_computation.5 | async-start | bytes 5308416 | tf_op jit(solution)/shard_map/reduce_scatter | solution.py:548
  171.4 5.4 %slice-start.2 = ((s8[6291456]{0:T(1024)(128)(4,1)}), s8[4194304]{0:T(1024)(128)(4,1)S(1)}, s32[]{:S(2)}) async-start(s8[6291456]{0:T(1024)(128)(4,1)} %bitcast.118), calls=%async_computation.9 | async-start | bytes 8388608
  183.8 127.1 %reduce-scatter.5.cloned.1.call-start = ((), (), s32[]{:S(2)}) async-start(), calls=%async_computation.6 | async-start | bytes 6635520 | tf_op jit(solution)/shard_map/reduce_scatter | solution.py:548
  183.8 13.9 %copy-start.17 = (f32[1024,768]{1,0:T(8,128)S(1)}, f32[1024,768]{1,0:T(8,128)}, u32[]{:S(2)}) copy-start(f32[1024,768]{1,0:T(8,128)} %copy-done.16) | copy-start | bytes 9437188
  183.8 13.9 %copy-start.23 = (f32[1024,768]{1,0:T(8,128)S(1)}, f32[1024,768]{1,0:T(8,128)}, u32[]{:S(2)}) copy-start(f32[1024,768]{1,0:T(8,128)} %copy-done.22) | copy-start | bytes 9437188
  197.7 10.7 %copy-start.35 = (bf16[1024,3072]{1,0:T(8,128)(2,1)}, bf16[1024,3072]{1,0:T(8,128)(2,1)S(1)}, u32[]{:S(2)}) copy-start(bf16[1024,3072]{1,0:T(8,128)(2,1)S(1)} %get-tuple-element.175) | copy-start | bytes 18874372
  215.3 5.1 %copy-start.18 = (f32[1024,768]{1,0:T(8,128)S(1)}, f32[1024,768]{1,0:T(8,128)}, u32[]{:S(2)}) copy-start(f32[1024,768]{1,0:T(8,128)} %copy-done.16) | copy-start | bytes 9437188
  237.5 5.7 %copy-start.29 = (bf16[384,768]{1,0:T(8,128)(2,1)S(1)}, bf16[384,768]{1,0:T(8,128)(2,1)}, u32[]{:S(2)}) copy-start(bf16[384,768]{1,0:T(8,128)(2,1)} %reduce-scatter.3.cloned.1.call-done) | copy-start | bytes 1769476
  243.3 45.6 %collective-permute-start.10 = (bf16[96,768]{1,0:T(8,128)(2,1)S(1)}, bf16[96,768]{1,0:T(8,128)(2,1)S(1)}, u32[]{:S(2)}, u32[]{:S(2)}) collective-permute-start(bf16[96,768]{1,0:T(8,128)(2,1)S(1)} %get-tuple-element.156), channel_id=1, source_target_pairs={{0,2},{1,3},{2,0},{3,1},{4,6},{5,7},{6,4},{7,5},{8,10},{9,11},{10,... | collective-permute-start | bytes 442376 | tf_op jit(solution)/shard_map/ppermute | solution.py:532
  245.5 43.4 %collective-permute-start.11 = (bf16[96,768]{1,0:T(8,128)(2,1)S(1)}, bf16[96,768]{1,0:T(8,128)(2,1)S(1)}, u32[]{:S(2)}, u32[]{:S(2)}) collective-permute-start(bf16[96,768]{1,0:T(8,128)(2,1)S(1)} %get-tuple-element.155), channel_id=1, source_target_pairs={{0,3},{1,0},{2,1},{3,2},{4,7},{5,4},{6,5},{7,6},{8,11},{9,8},{10,9... | collective-permute-start | bytes 442376 | tf_op jit(solution)/shard_map/ppermute | solution.py:532
  245.7 43.2 %collective-permute-start.9 = (bf16[96,768]{1,0:T(8,128)(2,1)S(1)}, bf16[96,768]{1,0:T(8,128)(2,1)S(1)}, u32[]{:S(2)}, u32[]{:S(2)}) collective-permute-start(bf16[96,768]{1,0:T(8,128)(2,1)S(1)} %get-tuple-element.157), channel_id=1, source_target_pairs={{0,1},{1,2},{2,3},{3,0},{4,5},{5,6},{6,7},{7,4},{8,9},{9,10},{10,1... | collective-permute-start | bytes 442376 | tf_op jit(solution)/shard_map/ppermute | solution.py:532
  288.9 11.8 %copy-start.5 = (bf16[1024,768]{1,0:T(8,128)(2,1)}, bf16[1024,768]{1,0:T(8,128)(2,1)S(1)}, u32[]{:S(2)}) copy-start(bf16[1024,768]{1,0:T(8,128)(2,1)S(1)} %get-tuple-element.68.gq_ref) | copy-start | bytes 4718596
  288.9 11.8 %copy-start.7 = (bf16[1024,768]{1,0:T(8,128)(2,1)}, bf16[1024,768]{1,0:T(8,128)(2,1)S(1)}, u32[]{:S(2)}) copy-start(bf16[1024,768]{1,0:T(8,128)(2,1)S(1)} %get-tuple-element.69.gk_ref) | copy-start | bytes 4718596
  288.9 11.8 %copy-start.9 = (bf16[1024,768]{1,0:T(8,128)(2,1)}, bf16[1024,768]{1,0:T(8,128)(2,1)S(1)}, u32[]{:S(2)}) copy-start(bf16[1024,768]{1,0:T(8,128)(2,1)S(1)} %get-tuple-element.70.gv_ref) | copy-start | bytes 4718596
  288.9 11.8 %copy-start.30 = (bf16[96,768]{1,0:T(8,128)(2,1)}, bf16[96,768]{1,0:T(8,128)(2,1)S(1)}, u32[]{:S(2)}) copy-start(bf16[96,768]{1,0:T(8,128)(2,1)S(1)} %collective-permute-done.11) | copy-start | bytes 442372
  288.9 11.8 %copy-start.32 = (bf16[96,768]{1,0:T(8,128)(2,1)}, bf16[96,768]{1,0:T(8,128)(2,1)S(1)}, u32[]{:S(2)}) copy-start(bf16[96,768]{1,0:T(8,128)(2,1)S(1)} %collective-permute-done.9) | copy-start | bytes 442372
  301.1 4.0 %collective-permute-start.13 = (bf16[2,2,96,1408]{3,2,0,1:T(8,128)(2,1)S(1)}, bf16[2,2,96,1408]{3,2,0,1:T(8,128)(2,1)S(1)}, u32[]{:S(2)}, u32[]{:S(2)}) collective-permute-start(bf16[2,2,96,1408]{3,2,0,1:T(8,128)(2,1)S(1)} %bitcast.102), channel_id=1, source_target_pairs={{0,4},{4,0},{8,12},{12,8},{16,20},{20,16},{24,28},{28,24},{1,5},{5... | collective-permute-start | bytes 3244040 | tf_op jit(solution)/shard_map/ppermute | solution.py:569
  303.9 4.0 %collective-permute-start.12 = (bf16[2,2,96,1536]{3,2,1,0:T(8,128)(2,1)}, bf16[2,2,96,1536]{3,2,1,0:T(8,128)(2,1)}, u32[]{:S(2)}, u32[]{:S(2)}) collective-permute-start(bf16[2,2,96,1536]{3,2,1,0:T(8,128)(2,1)} %dynamic-slice_bitcast_fusion), channel_id=1, source_target_pairs={{0,4},{4,0},{8,12},{12,8},{16,20},{20,16},{24,28},{28,24},{1,5},{5... | collective-permute-start | bytes 3538952 | tf_op jit(solution)/shard_map/ppermute | solution.py:569
  306.4 13.1 %copy-start.6 = (bf16[1024,768]{1,0:T(8,128)(2,1)S(1)}, bf16[1024,768]{1,0:T(8,128)(2,1)}, u32[]{:S(2)}) copy-start(bf16[1024,768]{1,0:T(8,128)(2,1)} %copy-done.5) | copy-start | bytes 4718596
  306.4 13.1 %copy-start.8 = (bf16[1024,768]{1,0:T(8,128)(2,1)S(1)}, bf16[1024,768]{1,0:T(8,128)(2,1)}, u32[]{:S(2)}) copy-start(bf16[1024,768]{1,0:T(8,128)(2,1)} %copy-done.7) | copy-start | bytes 4718596
  310.9 8.6 %copy-start.10 = (bf16[1024,768]{1,0:T(8,128)(2,1)S(1)}, bf16[1024,768]{1,0:T(8,128)(2,1)}, u32[]{:S(2)}) copy-start(bf16[1024,768]{1,0:T(8,128)(2,1)} %copy-done.9) | copy-start | bytes 4718596
  312.1 15.4 %collective-permute-start.15 = (bf16[2,96,1408]{2,1,0:T(8,128)(2,1)S(1)}, bf16[2,96,1408]{2,1,0:T(8,128)(2,1)S(1)}, u32[]{:S(2)}, u32[]{:S(2)}) collective-permute-start(bf16[2,96,1408]{2,1,0:T(8,128)(2,1)S(1)} %dynamic-slice_bitcast_fusion.2), channel_id=1, source_target_pairs={{0,8},{4,12},{8,0},{12,4},{16,24},{20,28},{24,16},{28,20},{1,9},{5... | collective-permute-start | bytes 1622024 | tf_op jit(solution)/shard_map/ppermute | solution.py:569
  314.4 14.3 %collective-permute-start.14 = (bf16[2,96,1536]{2,1,0:T(8,128)(2,1)S(1)}, bf16[2,96,1536]{2,1,0:T(8,128)(2,1)S(1)}, u32[]{:S(2)}, u32[]{:S(2)}) collective-permute-start(bf16[2,96,1536]{2,1,0:T(8,128)(2,1)S(1)} %dynamic-slice_bitcast_fusion.1), channel_id=1, source_target_pairs={{0,16},{4,20},{8,24},{12,28},{16,0},{20,4},{24,8},{28,12},{1,17},{... | collective-permute-start | bytes 1769480 | tf_op jit(solution)/shard_map/ppermute | solution.py:569
  315.9 13.0 %collective-permute-start.16 = (bf16[24,3840]{1,0:T(8,128)(2,1)S(1)}, bf16[24,3840]{1,0:T(8,128)(2,1)S(1)}, u32[]{:S(2)}, u32[]{:S(2)}) collective-permute-start(bf16[24,3840]{1,0:T(8,128)(2,1)S(1)} %get-tuple-element.153), channel_id=1, source_target_pairs={{0,1},{1,2},{2,3},{3,0},{4,5},{5,6},{6,7},{7,4},{8,9},{9,10},{10,1... | collective-permute-start | bytes 552968 | tf_op jit(solution)/shard_map/ppermute | solution.py:532
  315.9 15.2 %collective-permute-start.17 = (bf16[24,3840]{1,0:T(8,128)(2,1)S(1)}, bf16[24,3840]{1,0:T(8,128)(2,1)S(1)}, u32[]{:S(2)}, u32[]{:S(2)}) collective-permute-start(bf16[24,3840]{1,0:T(8,128)(2,1)S(1)} %get-tuple-element.152), channel_id=1, source_target_pairs={{0,2},{1,3},{2,0},{3,1},{4,6},{5,7},{6,4},{7,5},{8,10},{9,11},{10,... | collective-permute-start | bytes 552968 | tf_op jit(solution)/shard_map/ppermute | solution.py:532
  318.3 9.2 %copy-start.21 = (bf16[2,2,96,1408]{3,2,0,1:T(8,128)(2,1)S(1)}, bf16[2,2,96,1408]{3,2,0,1:T(8,128)(2,1)}, u32[]{:S(2)}) copy-start(bf16[2,2,96,1408]{3,2,0,1:T(8,128)(2,1)} %fusion.27) | copy-start | bytes 3244036
  318.3 10.4 %copy-start.20 = (bf16[2,2,96,1536]{3,2,1,0:T(8,128)(2,1)S(1)}, bf16[2,2,96,1536]{3,2,1,0:T(8,128)(2,1)}, u32[]{:S(2)}) copy-start(bf16[2,2,96,1536]{3,2,1,0:T(8,128)(2,1)} %fusion.26) | copy-start | bytes 3538948
  318.3 16.9 %collective-permute-start.18 = (bf16[24,3840]{1,0:T(8,128)(2,1)S(1)}, bf16[24,3840]{1,0:T(8,128)(2,1)S(1)}, u32[]{:S(2)}, u32[]{:S(2)}) collective-permute-start(bf16[24,3840]{1,0:T(8,128)(2,1)S(1)} %get-tuple-element.151), channel_id=1, source_target_pairs={{0,3},{1,0},{2,1},{3,2},{4,7},{5,4},{6,5},{7,6},{8,11},{9,8},{10,9... | collective-permute-start | bytes 552968 | tf_op jit(solution)/shard_map/ppermute | solution.py:532
  327.4 9.2 %copy-start.31 = (bf16[96,768]{1,0:T(8,128)(2,1)S(1)}, bf16[96,768]{1,0:T(8,128)(2,1)}, u32[]{:S(2)}) copy-start(bf16[96,768]{1,0:T(8,128)(2,1)} %copy-done.30) | copy-start | bytes 442372
  327.4 9.2 %copy-start.33 = (bf16[96,768]{1,0:T(8,128)(2,1)S(1)}, bf16[96,768]{1,0:T(8,128)(2,1)}, u32[]{:S(2)}) copy-start(bf16[96,768]{1,0:T(8,128)(2,1)} %copy-done.32) | copy-start | bytes 442372
  335.2 7.6 %collective-permute-start.20 = (bf16[96,1408]{1,0:T(8,128)(2,1)S(1)}, bf16[96,1408]{1,0:T(8,128)(2,1)S(1)}, u32[]{:S(2)}, u32[]{:S(2)}) collective-permute-start(bf16[96,1408]{1,0:T(8,128)(2,1)S(1)} %dynamic-slice_bitcast_fusion.4), channel_id=1, source_target_pairs={{0,16},{4,20},{8,24},{12,28},{16,0},{20,4},{24,8},{28,12},{1,17},{... | collective-permute-start | bytes 811016 | tf_op jit(solution)/shard_map/ppermute | solution.py:569
  337.4 7.8 %collective-permute-start.19 = (bf16[96,1536]{1,0:T(8,128)(2,1)S(1)}, bf16[96,1536]{1,0:T(8,128)(2,1)S(1)}, u32[]{:S(2)}, u32[]{:S(2)}) collective-permute-start(bf16[96,1536]{1,0:T(8,128)(2,1)S(1)} %dynamic-slice_bitcast_fusion.3), channel_id=1, source_target_pairs={{0,8},{4,12},{8,0},{12,4},{16,24},{20,28},{24,16},{28,20},{1,9},{5... | collective-permute-start | bytes 884744 | tf_op jit(solution)/shard_map/ppermute | solution.py:569
  345.4 4.0 %collective-permute-start.21 = (bf16[24,2944]{1,0:T(8,128)(2,1)S(1)}, bf16[24,2944]{1,0:T(8,128)(2,1)S(1)}, u32[]{:S(2)}, u32[]{:S(2)}) collective-permute-start(bf16[24,2944]{1,0:T(8,128)(2,1)S(1)} %get-tuple-element.159), channel_id=1, source_target_pairs={{0,1},{1,2},{2,3},{3,0},{4,5},{5,6},{6,7},{7,4},{8,9},{9,10},{10,1... | collective-permute-start | bytes 423944 | tf_op jit(solution)/shard_map/ppermute | solution.py:532
  345.5 6.3 %collective-permute-start.22 = (bf16[24,2944]{1,0:T(8,128)(2,1)S(1)}, bf16[24,2944]{1,0:T(8,128)(2,1)S(1)}, u32[]{:S(2)}, u32[]{:S(2)}) collective-permute-start(bf16[24,2944]{1,0:T(8,128)(2,1)S(1)} %get-tuple-element.160), channel_id=1, source_target_pairs={{0,2},{1,3},{2,0},{3,1},{4,6},{5,7},{6,4},{7,5},{8,10},{9,11},{10,... | collective-permute-start | bytes 423944 | tf_op jit(solution)/shard_map/ppermute | solution.py:532
  345.5 12.8 %collective-permute-start.23 = (bf16[24,2944]{1,0:T(8,128)(2,1)S(1)}, bf16[24,2944]{1,0:T(8,128)(2,1)S(1)}, u32[]{:S(2)}, u32[]{:S(2)}) collective-permute-start(bf16[24,2944]{1,0:T(8,128)(2,1)S(1)} %get-tuple-element.161), channel_id=1, source_target_pairs={{0,3},{1,0},{2,1},{3,2},{4,7},{5,4},{6,5},{7,6},{8,11},{9,8},{10,9... | collective-permute-start | bytes 423944 | tf_op jit(solution)/shard_map/ppermute | solution.py:532
  (21 other events, 52.3 us)
Sparse Core Ops, SparseCore 0:
  33.7 39.3 all-gather.3
  75.6 43.8 all-gather.5
  121.4 38.9 all-gather.7
  183.9 53.4 reduce-scatter.2
  241.1 59.6 reduce-scatter.4

commit v2 on v1

--- a/solution.py
+++ b/solution.py
@@ -19,7 +19,8 @@
 ROWS = 32
 DELAYS = (0, 1)
 LOG2E = 1.4426950408889634
-VECTORS = 256
+VECTORS = 128
+EARLY = 2
 SCALE = 1.0 / math.sqrt(3 * HEAD)
 AXES = ("wide", "narrow")
 norm_epsilon = 1e-06
@@ -278,11 +279,13 @@
 
 
 def attend_back_kernel(
-    q_ref, k_ref, v_ref, pq_ref, pk_ref, gc_ref, ctx_ref, probs_ref, scale_ref,
+    earlier, q_ref, k_ref, v_ref, pq_ref, pk_ref, gc_ref, ctx_ref, probs_ref, scale_ref, *refs
+):
+    (
     gq_ref, gk_ref, gv_ref, gpq_ref, gpk_ref,
     raw_a, raw_b, grad_a, grad_b, moved_a, moved_b, turned_a, turned_b,
     inner_a, inner_b, q_t, k_t, gc_t, pq_t, pk_t, k_rev, v_rev, gq_t, gk_t, gv_t,
-):
+    ) = refs[earlier:]
     raw, grad, moved, turned = (raw_a, raw_b), (grad_a, grad_b), (moved_a, moved_b), (turned_a, turned_b)
     inner = (inner_a, inner_b)
     flip = flip_matrix()
@@ -407,56 +410,70 @@
         weave(matrix, vector)
 
 
-def attend_back(qkv, pos, grad_context, context_wide, probs, scale):
-    qkv_block = lambda which: pl.BlockSpec((MICRO * SEQ, PAIR), lambda p: (0, which * PAIRS + p))
-    pos_block = lambda which: pl.BlockSpec((SEQ, PAIR), lambda p: (0, which * PAIRS + p))
-    token_block = pl.BlockSpec((MICRO * SEQ, PAIR), lambda p: (0, p))
-    table_block = pl.BlockSpec((PAIR, SEQ), lambda p: (p, 0))
+def attend_back(first, count, earlier, qkv, pos, grad_context, context_wide, probs, scale):
+    qkv_block = lambda which: pl.BlockSpec((MICRO * SEQ, PAIR), lambda p: (0, which * PAIRS + first + p))
+    pos_block = lambda which: pl.BlockSpec((SEQ, PAIR), lambda p: (0, which * PAIRS + first + p))
+    token_block = pl.BlockSpec((MICRO * SEQ, PAIR), lambda p: (0, first + p))
+    table_block = pl.BlockSpec((PAIR, SEQ), lambda p: (first + p, 0))
     token_shape = jax.ShapeDtypeStruct((MICRO * SEQ, D), bf16)
     table_shape = jax.ShapeDtypeStruct((D, SEQ), f32)
     square = lambda kind: [pltpu.VMEM((SEQ, SEQ), kind)] * 2
     wide = pltpu.VMEM((MICRO, PAIR, SEQ), bf16)
     tall = pltpu.VMEM((MICRO, SEQ, PAIR), bf16)
     return pl.pallas_call(
-        attend_back_kernel,
-        grid=(PAIRS,),
+        functools.partial(attend_back_kernel, len(earlier)),
+        grid=(count,),
+        input_output_aliases={9 + i: i for i in range(len(earlier))},
         in_specs=[
             qkv_block(0), qkv_block(1), qkv_block(2), pos_block(0), pos_block(1),
             token_block, token_block,
-            pl.BlockSpec((MICRO, 2, SEQ, SEQ), lambda p: (0, p, 0, 0)),
-            pl.BlockSpec((MICRO, 2, SEQ, CHUNK), lambda p: (0, p, 0, 0)),
-        ],
+            pl.BlockSpec((MICRO, 2, SEQ, SEQ), lambda p: (0, first + p, 0, 0)),
+            pl.BlockSpec((MICRO, 2, SEQ, CHUNK), lambda p: (0, first + p, 0, 0)),
+        ]
+        + [pl.BlockSpec(memory_space=pl.ANY)] * len(earlier),
         out_specs=[token_block, token_block, token_block, table_block, table_block],
         out_shape=[token_shape, token_shape, token_shape, table_shape, table_shape],
         scratch_shapes=square(f32) + square(bf16) * 3
         + [pltpu.VMEM((SEQ, CHUNK), f32)] * 2
         + [wide, wide, wide, pltpu.VMEM((PAIR, SEQ), bf16), pltpu.VMEM((PAIR, SEQ), bf16)]
         + [tall, tall, wide, wide, wide],
-        compiler_params=pltpu.CompilerParams(vmem_limit_bytes=40 * 2**20),
+        compiler_params=pltpu.CompilerParams(vmem_limit_bytes=56 * 2**20),
         cost_estimate=pl.CostEstimate(
-            flops=24 * 16 * 2 * SEQ * SEQ * PAIR, bytes_accessed=24 * 2**20, transcendentals=0
+            flops=count * 4 * 16 * 2 * SEQ * SEQ * PAIR, bytes_accessed=count * 4 * 2**20, transcendentals=0
         ),
         name="attend_back",
-    )(qkv, qkv, qkv, pos, pos, grad_context, context_wide, probs, scale)
+    )(qkv, qkv, qkv, pos, pos, grad_context, context_wide, probs, scale, *earlier)
 
 
 def weigh_kernel(
-    x_ref, gq_ref, gk_ref, gv_ref, rel_ref, gpq_ref, gpk_ref, wq_ref, wk_ref, vec_ref,
-    first_ref, second_ref, x_turned, rel_sum, rows_ref,
+    low_ref, x_ref, gq_ref, gk_ref, gv_ref, rel_ref, gpq_ref, gpk_ref, wq_ref, wk_ref,
+    vec_ref, up_bias_ref,
+    first_keep, first_send, second_keep, second_send, x_turned, rel_sum, rows_ref,
 ):
     step = pl.program_id(0)
     width = gq_ref.shape[1]
+    count, rows = first_keep.shape[0], first_keep.shape[1]
+
+    def put(keep, send, columns, value):
+        value = value.astype(bf16).reshape(count, 2, rows, value.shape[1])
+        lower, upper = value[:, 0], value[:, 1]
+        is_upper = low_ref[0] == 1
+        keep[:, :, columns] = jnp.where(is_upper, upper, lower)
+        send[:, :, columns] = jnp.where(is_upper, lower, upper)
+
+    def columns_at(start):
+        return pl.ds(pl.multiple_of(start, width), width)
 
     @pl.when(step == 0)
     def begin():
         x_turned[...] = x_ref[...].T
         rel_sum[...] = jnp.zeros_like(rel_sum)
         rows_ref[...] = jnp.zeros_like(rows_ref)
-        rows_ref[8:24, :] = vec_ref[...]
+        rows_ref[8:14, :] = vec_ref[...]
+        rows_ref[14:18, :] = up_bias_ref[...]
 
     token_ones = jnp.ones((8, MICRO * SEQ), bf16)
     place_ones = jnp.ones((8, SEQ), bf16)
-    here = pl.ds(pl.multiple_of(step * width, width), width)
     row = lax.broadcasted_iota(jnp.int32, (8, width), 0)
     biases = jnp.zeros((8, width), f32)
     tables = ((gq_ref, gpq_ref, wq_ref), (gk_ref, gpk_ref, wk_ref))
@@ -464,49 +481,107 @@
         grad = grad_ref[...]
         table = table_ref[...].astype(bf16)
         total = dot_nn(x_turned[...], grad) + dot_nt(rel_ref[...], table)
-        first_ref[:, pl.ds(pl.multiple_of(which * D + step * width, width), width)] = total.astype(bf16)
+        put(first_keep, first_send, columns_at(which * D + step * width), total)
         rel_sum[...] += dot_nn(weight_ref[...], table)
         bias = dot_nn(token_ones, grad) + dot_nt(place_ones, table)
         biases = jnp.where(row == which, bias, biases)
     grad = gv_ref[...]
-    second_ref[:, here] = dot_nn(x_turned[...], grad).astype(bf16)
-    rows_ref[:8, here] = jnp.where(row == 2, dot_nn(token_ones, grad), biases)
+    put(second_keep, second_send, columns_at(step * width), dot_nn(x_turned[...], grad))
+    rows_ref[:8, columns_at(step * width)] = jnp.where(row == 2, dot_nn(token_ones, grad), biases)
 
     @pl.when(step == pl.num_programs(0) - 1)
     def end():
-        second_ref[:, D : D + SEQ] = rel_sum[...].astype(bf16)
-        second_ref[:, D + SEQ :] = rows_ref[...].T.astype(bf16)
-
-
-def weigh(x, gq, gk, gv, rel_turned, gpq, gpk, qkv_weight, vectors):
+        put(second_keep, second_send, slice(D, D + SEQ), rel_sum[...])
+        put(second_keep, second_send, slice(D + SEQ, D + SEQ + CHUNK), rows_ref[...].T)
+
+
+def weigh(x, gq, gk, gv, gpq, gpk, first_pack, vectors):
     steps = 3
     width = D // steps
-    whole = lambda shape: pl.BlockSpec(shape, lambda p: (0, 0))
-    columns = lambda rows, which=0: pl.BlockSpec((rows, width), lambda p: (0, which * steps + p))
+    whole = lambda shape: pl.BlockSpec(shape, lambda p, n: (0,) * len(shape))
+    columns = lambda rows, skip=0: pl.BlockSpec((rows, width), lambda p, n: (0, skip // width + p))
     tokens = MICRO * SEQ
+    size = lax.axis_size("wide")
+    shapes = [(size // 2, D // size, cols) for cols in (2 * D, 2 * D, D + SEQ + CHUNK, D + SEQ + CHUNK)]
     return pl.pallas_call(
         weigh_kernel,
-        grid=(steps,),
-        in_specs=[
-            whole((tokens, D)), columns(tokens), columns(tokens), columns(tokens),
-            whole((D, SEQ)),
-            pl.BlockSpec((width, SEQ), lambda p: (p, 0)), pl.BlockSpec((width, SEQ), lambda p: (p, 0)),
-            columns(D), columns(D, 1), whole((16, D)),
-        ],
-        out_specs=[whole((D, 2 * D)), whole((D, D + SEQ + CHUNK))],
-        out_shape=[
-            jax.ShapeDtypeStruct((D, 2 * D), bf16),
-            jax.ShapeDtypeStruct((D, D + SEQ + CHUNK), bf16),
-        ],
-        scratch_shapes=[
-            pltpu.VMEM((D, tokens), bf16), pltpu.VMEM((D, SEQ), f32), pltpu.VMEM((CHUNK, D), f32),
-        ],
-        compiler_params=pltpu.CompilerParams(vmem_limit_bytes=40 * 2**20),
+        grid_spec=pltpu.PrefetchScalarGridSpec(
+            num_scalar_prefetch=1,
+            grid=(steps,),
+            in_specs=[
+                whole((tokens, D)), columns(tokens), columns(tokens), columns(tokens),
+                whole((D, SEQ)),
+                pl.BlockSpec((width, SEQ), lambda p, n: (p, 0)),
+                pl.BlockSpec((width, SEQ), lambda p, n: (p, 0)),
+                columns(D, SEQ), columns(D, SEQ + D),
+            ]
+            + [whole((6, D)), whole((4, D))],
+            out_specs=[whole(shape) for shape in shapes],
+            scratch_shapes=[
+                pltpu.VMEM((D, tokens), bf16), pltpu.VMEM((D, SEQ), f32), pltpu.VMEM((CHUNK, D), f32),
+            ],
+        ),
+        out_shape=[jax.ShapeDtypeStruct(shape, bf16) for shape in shapes],
+        compiler_params=pltpu.CompilerParams(vmem_limit_bytes=56 * 2**20),
         cost_estimate=pl.CostEstimate(
             flops=2 * D * D * (3 * tokens + 4 * SEQ), bytes_accessed=20 * 2**20, transcendentals=0
         ),
         name="weigh",
-    )(x, gq, gk, gv, rel_turned, gpq, gpk, qkv_weight, qkv_weight, vectors)
+    )(my_bit(0).reshape(1), x, gq, gk, gv, first_pack, gpq, gpk, first_pack, first_pack, *vectors)
+
+
+def feed_back_kernel(
+    grad_ref, hidden_ref, slope_ref, down_ref, up_ref,
+    grad_hidden_ref, grad_weight_ref, bias_ref, hidden_turned, grad_up,
+):
+    step = pl.program_id(0)
+
+    @pl.when(step == 0)
+    def begin():
+        hidden_turned[...] = hidden_ref[...].T
+        grad_hidden_ref[...] = jnp.zeros_like(grad_hidden_ref)
+
+    for seq in range(MICRO):
+        part = slice(seq * SEQ, (seq + 1) * SEQ)
+        grad_act = dot_nt(grad_ref[part, :], down_ref[...])
+        grad_up[part, :] = (grad_act * slope_ref[part, :].astype(f32)).astype(bf16)
+    for seq in range(MICRO):
+        part = slice(seq * SEQ, (seq + 1) * SEQ)
+        grad_hidden_ref[part, :] += dot_nt(grad_up[part, :], up_ref[...])
+    grad_weight_ref[...] = dot_nn(hidden_turned[...], grad_up[...]).astype(bf16)
+    bias_ref[...] = dot_nn(jnp.ones((8, MICRO * SEQ), bf16), grad_up[...])
+
+
+def feed_back(grad_feed, hidden_low, slope, down_full, second_pack):
+    tokens = MICRO * SEQ
+    blocks = slope.shape[1] // D
+    whole = lambda shape: pl.BlockSpec(shape, lambda f: (0, 0))
+    return pl.pallas_call(
+        feed_back_kernel,
+        grid=(blocks,),
+        in_specs=[
+            whole((tokens, D)), whole((tokens, D)),
+            pl.BlockSpec((tokens, D), lambda f: (0, f)),
+            pl.BlockSpec((D, D), lambda f: (f, 0)),
+            pl.BlockSpec((D, D), lambda f: (0, 1 + f)),
+        ],
+        out_specs=[
+            whole((tokens, D)),
+            pl.BlockSpec((D, D), lambda f: (0, 1 + f)),
+            pl.BlockSpec((8, D), lambda f: (0, f)),
+        ],
+        out_shape=[
+            jax.ShapeDtypeStruct((tokens, D), f32),
+            jax.ShapeDtypeStruct((D, (1 + blocks) * D), bf16),
+            jax.ShapeDtypeStruct((8, blocks * D), f32),
+        ],
+        scratch_shapes=[pltpu.VMEM((D, tokens), bf16), pltpu.VMEM((tokens, D), bf16)],
+        compiler_params=pltpu.CompilerParams(vmem_limit_bytes=56 * 2**20),
+        cost_estimate=pl.CostEstimate(
+            flops=6 * tokens * D * blocks * D, bytes_accessed=30 * 2**20, transcendentals=0
+        ),
+        name="feed_back",
+    )(grad_feed, hidden_low, slope, down_full, second_pack)
 
 
 def normalise(v):
@@ -517,6 +592,10 @@
     return centered * rstd, rstd
 
 
+def column_sums(values):
+    return jnp.sum(values, axis=0)
+
+
 def norm_back(normed, rstd, gain, grad):
     e = grad * gain
     grad_in = rstd * (
@@ -524,7 +603,7 @@
         - jnp.mean(e, axis=-1, keepdims=True)
         - normed * jnp.mean(e * normed, axis=-1, keepdims=True)
     )
-    return grad_in, jnp.sum(grad * normed, axis=0), jnp.sum(grad, axis=0)
+    return grad_in, column_sums(grad * normed), column_sums(grad)
 
 
 def narrow_shifts(block, shift):
@@ -582,12 +661,28 @@
     return full.reshape((2,) * bits + (full.shape[0] >> bits, full.shape[1]))
 
 
-def halve(part, bit, left):
+def add_low(first, second):
+    return (first.astype(f32) + second.astype(f32)).astype(bf16)
+
+
+def two_halves(part, bit, left):
     axis, mine = left.index(bit), my_bit(bit)
     keep = lax.dynamic_index_in_dim(part, mine, axis, keepdims=False)
     send = lax.dynamic_index_in_dim(part, 1 - mine, axis, keepdims=False)
     left.remove(bit)
-    return (keep.astype(f32) + swap(send, bit).astype(f32)).astype(bf16)
+    return keep, send
+
+
+def scatter_upper(part):
+    size = lax.axis_size("wide")
+    groups = [list(range(low, size, 2)) for low in range(2)]
+    part = part.reshape(-1, part.shape[-1])
+    return lax.psum_scatter(part, "wide", scatter_dimension=0, tiled=True, axis_index_groups=groups)
+
+
+def halve(part, bit, left):
+    keep, send = two_halves(part, bit, left)
+    return add_low(keep, swap(send, bit))
 
 
 def all_bits():
@@ -609,24 +704,23 @@
         query_bias, key_bias, value_bias, out_bias, first_gain, first_shift,
         down_bias, second_gain, second_shift,
     ]
-    vectors = jnp.concatenate([jnp.stack(vectors), up_bias.reshape(4, share)], axis=0)
-    vectors = jnp.pad(vectors, ((0, VECTORS - vectors.shape[0]), (0, 0)))
+    vectors += [up_bias[c * share : (c + 1) * share] for c in range(4)]
+    places = lax.broadcasted_iota(jnp.int32, (VECTORS, share), 0)
+    stacked = jnp.zeros((VECTORS, share), bf16)
+    for place, vector in enumerate(vectors):
+        stacked = jnp.where(places == place, vector[None, :], stacked)
     first_pack = gather_rows(
         jnp.concatenate(
-            [
-                query_weight, key_weight, value_weight,
-                jnp.concatenate([rel_table, vectors], axis=0).T,
-            ],
-            axis=1,
+            [rel_table.T, query_weight, key_weight, value_weight, stacked.T], axis=1
         )
     )
     second_pack = gather_rows(jnp.concatenate([out_weight, up_weight], axis=1))
     down_full = gather_rows(down_weight)
-    qkv_weight = first_pack[:, : 3 * D]
-    rel_turned = first_pack[:, 3 * D : 3 * D + SEQ]
+    qkv_weight = first_pack[:, SEQ : SEQ + 3 * D]
+    rel_turned = first_pack[:, :SEQ]
     out_full = second_pack[:, :D]
     up_full = second_pack[:, D:]
-    vector_rows = first_pack[:, 3 * D + SEQ :].T.astype(f32)
+    vector_rows = first_pack[:, SEQ + 3 * D :].T.astype(f32)
     qkv_bias = vector_rows[:3].reshape(3 * D)
     out_b, gain_1, shift_1, down_b, gain_2, shift_2 = (vector_rows[i] for i in range(3, 9))
     up_b = jnp.transpose(vector_rows[9:13].reshape(4, D // share, share), (1, 0, 2)).reshape(4 * D)
@@ -651,52 +745,45 @@
 
     grad_second, grad_gain_2, grad_shift_2 = norm_back(normed_2, rstd_2, gain_2, cot)
     grad_feed = grad_second.astype(bf16)
-    grad_down_bias = jnp.sum(grad_feed.astype(f32), axis=0)
+    grad_down_bias = column_sums(grad_feed.astype(f32))
     grad_down = dot_tn(activated_low, grad_feed).astype(bf16)
-    grad_up = (dot_nt(grad_feed, down_full) * slope.astype(f32)).astype(bf16)
-    grad_up_bias = jnp.sum(grad_up.astype(f32), axis=0)
-    grad_up_weight = dot_tn(hidden_low, grad_up).astype(bf16)
-    grad_hidden = grad_second + dot_nt(grad_up, up_full)
+    grad_hidden, grad_second_pack, grad_up_bias = feed_back(
+        grad_feed, hidden_low, slope, down_full, second_pack
+    )
+    grad_up_bias = grad_up_bias[0]
+    grad_hidden = grad_second + grad_hidden
     grad_first, grad_gain_1, grad_shift_1 = norm_back(normed_1, rstd_1, gain_1, grad_hidden)
     grad_branch = grad_first.astype(bf16)
-    grad_out_bias = jnp.sum(grad_branch.astype(f32), axis=0)
+    grad_out_bias = column_sums(grad_branch.astype(f32))
     grad_out = dot_tn(context, grad_branch).astype(bf16)
     grad_context = dot_nt(grad_branch, out_full).astype(bf16)
 
-    grad_second_pack = jnp.concatenate([grad_out, grad_up_weight], axis=1)
+    grad_second_pack = lax.dynamic_update_slice(grad_second_pack, grad_out, (0, 0))
     down_part = scatter_wide(grad_down)
-    grad_context, grad_second_pack, down_part = lax.optimization_barrier(
-        (grad_context, grad_second_pack, down_part)
-    )
+    keep, send = two_halves(split_bits(grad_second_pack), 0, all_bits())
+    came = swap(send, 0)
+    grad_context, keep, send = lax.optimization_barrier((grad_context, keep, send))
+    inputs = (qkv, pos, grad_context, context_wide, probs, probs_scale)
+    early = list(attend_back(0, EARLY, (), *inputs))
+    early[0], keep, came, down_part = lax.optimization_barrier((early[0], keep, came, down_part))
+    second_part = scatter_upper(add_low(keep, came))
     down_pieces = scatter_narrow_start(down_part)
-    second_part = scatter_wide(grad_second_pack)
-
-    gq, gk, gv, gpq, gpk = attend_back(
-        qkv, pos, grad_context, context_wide, probs, probs_scale
-    )
+    gq, gk, gv, gpq, gpk = attend_back(EARLY, PAIRS - EARLY, early, *inputs)
     grad_up_bias = jnp.transpose(grad_up_bias.reshape(D // share, 4, share), (1, 0, 2))
     vector_grads = jnp.concatenate(
-        [
-            jnp.stack(
-                [
-                    grad_out_bias, grad_gain_1, grad_shift_1,
-                    grad_down_bias, grad_gain_2, grad_shift_2,
-                ]
-            ),
-            grad_up_bias.reshape(4, D),
-            jnp.zeros((6, D), f32),
-        ],
-        axis=0,
-    )
+        [grad_out_bias, grad_gain_1, grad_shift_1, grad_down_bias, grad_gain_2, grad_shift_2]
+    )
+    vector_grads = (vector_grads.reshape(6, D), grad_up_bias.reshape(4, D))
     gq, down_pieces = lax.optimization_barrier((gq, down_pieces))
     down_sum = sum(piece.astype(f32) for piece in down_pieces)
-    first_half, second_half = weigh(
-        x, gq, gk, gv, rel_turned, gpq, gpk, qkv_weight, vector_grads
+    first_keep, first_send, second_keep, second_send = weigh(
+        x, gq, gk, gv, gpq, gpk, first_pack, vector_grads
     )
     upper = all_bits()[:-1]
+    sides = lambda part: part.reshape((2,) * len(upper) + part.shape[1:])
     halves = [
-        [split_bits(first_half), all_bits(), [0] + upper],
-        [split_bits(second_half), all_bits(), [0] + upper[::-1]],
+        [sides(add_low(first_keep, swap(first_send, 0))), all_bits()[:-1], list(upper)],
+        [sides(add_low(second_keep, swap(second_send, 0))), all_bits()[:-1], upper[::-1]],
     ]
 
     def halve_both():
@@ -708,7 +795,6 @@
         halves[0][0], halves[1][0] = kept[:2]
         return kept[2:]
 
-    halve_both()
     gq, gk, gv, second_part = together(gq, gk, gv, second_part)
     second_pieces = scatter_narrow_start(second_part)
     grad_inputs = grad_first + dot_nt(jnp.concatenate([gq, gk, gv], axis=1), qkv_weight)

time: 374 us -> 349 us (0.933)
  matrix products: 85.9 us -> 55.5 us
  Pallas kernels: 88.1 us -> 116 us
  local copies, waits for them, and re-layouts: 46.1 us -> 32.8 us
  waiting for transfers between devices: 91.8 us -> 79 us
  other arithmetic: 17.6 us -> 22.9 us
    pallas_call x2 -> x4, Pallas kernels: 48.2 us -> 75.8 us  [the longest x2 40 us: attend_back(): pl.pallas_call(functools.partial(attend_back_kernel, len(earlier)), grid=...]
    dot_general x4 -> x2, matrix products: 37.5 us -> 12.9 us  [dot_nt(): lax.dot_general(left, right, (((1,), (1,)), ((), ())), preferred_element_...]
    dot_general x4 -> x3, matrix products: 21.8 us -> 12.1 us  [dot_tn(): lax.dot_general(left, right, (((0,), (0,)), ((), ())), preferred_element_...]
    all_gather x3, waiting for transfers between devices: 19.9 us -> 12.6 us  [gather_rows(): return lax.all_gather(together, 'wide', axis=0, tiled=True)]
    another operation x15 -> x1, local copies, waits for them, and re-layouts: 6.75 us -> 0.12 us  [body(): grad_up_bias.reshape(D // share, 4, share)]
    reduce_sum x4 -> x5, other arithmetic: 5.44 us -> 10.5 us  [column_sums(): return jnp.sum(values, axis=0)]
    reduce_scatter x2 -> x1, waiting for transfers between devices: 5.39 us -> 0.47 us  [scatter_wide(): return lax.psum_scatter(full, 'wide', scatter_dimension=0, tiled=True)]
    dot_general x4, matrix products: 26.6 us -> 30.5 us  [dot_nn(): lax.dot_general(left, right, (((1,), (0,)), ((), ())), preferred_element_...]
  transfers between devices with their start and end apart: 29 -> 30, of which waited for: 21 -> 20; matrix products, arithmetic and copies ran while one was open for 27% -> 19% of each run, Pallas kernels for 24% -> 34%
where the time goes in v2:
time: 349 us; the launch traced here: 344 us
  Pallas kernels  116 us (33%)
  waiting for transfers between devices  79 us (23%)
  matrix products  55.5 us (16%)
  local copies, waits for them, and re-layouts  32.8 us (9%)
  other arithmetic  22.9 us (7%)
  starting transfers between devices  22.6 us (6%)
  between operations  15 us (4%)
    ppermute x18, waiting for transfers between devices, narrow_shifts(): lax.ppermute(block, 'narrow', [(i, (i + shift) % size) for i in range(siz...  56.6 us
    pallas_call x2, Pallas kernels, attend_back(): pl.pallas_call(functools.partial(attend_back_kernel, len(earlier)), grid=...  40 us
    pallas_call x1, Pallas kernels, attend(): pl.pallas_call(attend_kernel, grid_spec=pltpu.PrefetchScalarGridSpec(num_...  39.9 us
    dot_general x4, matrix products, dot_nn(): lax.dot_general(left, right, (((1,), (0,)), ((), ())), preferred_element_...  30.5 us
    pallas_call x1, Pallas kernels, feed_back(): pl.pallas_call(feed_back_kernel, grid=(blocks,), in_specs=[whole((tokens,...  22.3 us
    unnamed x79, local copies, waits for them, and re-layouts  19.4 us
    ppermute x18, starting transfers between devices, narrow_shifts(): lax.ppermute(block, 'narrow', [(i, (i + shift) % size) for i in range(siz...  17.3 us
    pallas_call x1, Pallas kernels, weigh(): pl.pallas_call(weigh_kernel, grid_spec=pltpu.PrefetchScalarGridSpec(num_s...  13.5 us
  transfers between devices with their start and end apart: 30, of which 20 were waited for; matrix products, arithmetic and copies ran while one was open for 19% of the time, Pallas kernels for 34%

profile of v2, /device:TPU:9, one launch (start us, length us, event | category | flops | bytes accessed | tf_op | source)
XLA Modules:
  0.0 343.5 jit_solution(14384904611653908822)
XLA Ops:
  12.2 1.3 collective-permute-start
  14.6 1.4 collective-permute-start.2
  16.8 8.2 %collective-permute-done.1 = bf16[24,2944]{1,0:T(8,128)(2,1)S(1)} collective-permute-done((bf16[24,2944]{1,0:T(8,128)(2,1)S(1)}, bf16[24,2944]{1,0:T(8,128)(2,1)S(1)}, u32[]{:S(2)}, u32[]{:S(2)}) %collective-permute-start.1) | collective-permute-done | bytes 141344 | tf_op jit(solution)/shard_map/ppermute | solution.py:611
  25.0 2.8 collective-permute-done.2
  30.8 1.4 collective-permute-start.5
  32.3 3.8 %collective-permute-done.3 = bf16[24,3840]{1,0:T(8,128)(2,1)S(1)} collective-permute-done((bf16[24,3840]{1,0:T(8,128)(2,1)S(1)}, bf16[24,3840]{1,0:T(8,128)(2,1)S(1)}, u32[]{:S(2)}, u32[]{:S(2)}) %collective-permute-start.3) | collective-permute-done | bytes 184352 | tf_op jit(solution)/shard_map/ppermute | solution.py:611
  36.2 10.0 %collective-permute-done.4 = bf16[24,3840]{1,0:T(8,128)(2,1)S(1)} collective-permute-done((bf16[24,3840]{1,0:T(8,128)(2,1)S(1)}, bf16[24,3840]{1,0:T(8,128)(2,1)S(1)}, u32[]{:S(2)}, u32[]{:S(2)}) %collective-permute-start.4) | collective-permute-done | bytes 184352 | tf_op jit(solution)/shard_map/ppermute | solution.py:611
  46.1 1.6 collective-permute-done.5
  48.8 1.6 collective-permute-start.7
  50.4 1.4 collective-permute-start.8
  51.8 1.8 collective-permute-done.6
  53.7 7.6 %collective-permute-done.7 = bf16[96,768]{1,0:T(8,128)(2,1)S(1)} collective-permute-done((bf16[96,768]{1,0:T(8,128)(2,1)S(1)}, bf16[96,768]{1,0:T(8,128)(2,1)S(1)}, u32[]{:S(2)}, u32[]{:S(2)}) %collective-permute-start.7) | collective-permute-done | bytes 147488 | tf_op jit(solution)/shard_map/ppermute | solution.py:611
  61.3 2.9 collective-permute-done.8
  65.1 2.3 all-gather.4.cloned.1.call-done.rel_ref.wq_ref.wk_ref
  69.2 1.3 slice_reduce_fusion.1
  71.3 3.7 %fusion.23.pq_ref.pk_ref = bf16[512,1536]{1,0:T(8,128)(2,1)S(1)} fusion(bf16[768,2944]{1,0:T(8,128)(2,1)} %all-gather.4.cloned.1.call-done.rel_ref.wq_ref.wk_ref, f32[1536]{0:T(1024)S(1)} %add.286), kind=kOutput, calls=%fused_computation.45 | convolution fusion | flops 1209532416 | bytes 4724736 | tf_op jit(solution)/shard_map/dot_general | solution.py:40
  75.1 4.3 %fusion.5.q_ref.k_ref.v_ref = bf16[1024,2304]{1,0:T(8,128)(2,1)S(1)} fusion(bf16[1024,768]{1,0:T(8,128)(2,1)S(1)} %bitcast.97, f32[2304]{0:T(1024)S(1)} %add.283, bf16[768,2944]{1,0:T(8,128)(2,1)S(1)} %bitcast.84), kind=kOutput, calls=%fused_computation.11 | convolution fusion | flops 3628597248 | bytes 9842688 | tf_op jit(solution)/shard_map/dot_general | solution.py:36
  79.4 39.9 %attend.1 = (bf16[1024,768]{1,0:T(8,128)(2,1)S(1)}, f32[1024,768]{1,0:T(8,128)S(1)}, bf16[2,12,512,512]{3,2,1,0:T(8,128)(2,1)}, f32[2,12,512,128]{3,2,1,0:T(8,128)}) custom-call(s32[2]{0:T(128)S(1)} %bitcast.82, bf16[1024,2304]{1,0:T(8,128)(2,1)S(1)} %fusion.5.q_ref.k_ref.v_ref, bf16[1024,2304]{1,0:T(8,128)(2,1)S(1)} %fusion.5.q_ref.k_ref.v_ref, ...), custom_call_target="tpu_custom_call" | custom-call | flops 12884901888 | bytes 20971520 | tf_op jit(solution)/shard_map/attend/pallas_call | solution.py:251
  119.3 2.1 copy-done
  121.4 1.7 copy-done.2
  123.1 3.5 %fusion.52 = (f32[1024]{0:T(1024)S(1)}, f32[1024,768]{1,0:T(8,128)S(1)}) fusion(f32[768]{0:T(1024)S(1)} %get-tuple-element.160, bf16[1024,768]{1,0:T(8,128)(2,1)S(1)} %get-tuple-element.64, bf16[768,3840]{1,0:T(8,128)(2,1)} %all-gather.6.cloned.1.call-done.up_ref, bf16[1024,768]{1,0:T(8,128)(2,1)} %bitcast.95), kind=kOutput, calls=%fused_computation.168 | convolution fusion | flops 1211104256 | bytes 7478272 | tf_op jit(solution)/shard_map/dot_general | solution.py:36
  131.0 13.2 %fusion.4 = (bf16[1024,3072]{1,0:T(8,128)(2,1)}, bf16[1024,3072]{1,0:T(8,128)(2,1)}) fusion(f32[3072]{0:T(1024)S(1)} %add.297, bf16[1024,768]{1,0:T(8,128)(2,1)S(1)} %fusion.24.hidden_ref, bf16[768,3840]{1,0:T(8,128)(2,1)S(1)} %copy-done.29), kind=kOutput, calls=%fused_computation.5 | convolution fusion | flops 4869586944 | bytes 18886656 | tf_op jit(solution)/shard_map/dot_general | solution.py:36
  144.2 10.4 %all-gather.8.cloned.1.call-done.down_ref = bf16[3072,768]{1,0:T(8,128)(2,1)} async-done(((bf16[384,768]{1,0:T(8,128)(2,1)}), bf16[3072,768]{1,0:T(8,128)(2,1)}) %all-gather.8.cloned.1.call-update) | async-done | bytes 4718608 | tf_op jit(solution)/shard_map/all_gather | solution.py:623
  154.6 9.5 %fusion.53 = (f32[1024]{0:T(1024)S(1)}, f32[1024,768]{1,0:T(8,128)S(1)}) fusion(f32[768]{0:T(1024)S(1)} %get-tuple-element.157, bf16[1024,3072]{1,0:T(8,128)(2,1)} %get-tuple-element.176, bf16[3072,768]{1,0:T(8,128)(2,1)} %all-gather.8.cloned.1.call-done.down_ref, f32[768]{0:T(1024)S(1)} %get-tuple-element.158, f32[768]{0:T(1024)S(1)} %get-tuple-element.159, ...), kind=kOutput, calls=%fused_computation.169 | convolution fusion | flops 4837342208 | bytes 17323008 | tf_op jit(solution)/shard_map/dot_general | solution.py:36
  168.3 7.0 %convolution_convert_fusion = bf16[3072,768]{1,0:T(8,128)(2,1)} fusion(bf16[1024,3072]{1,0:T(8,128)(2,1)S(1)} %bitcast.104, bf16[1024,768]{1,0:T(8,128)(2,1)S(1)} %get-tuple-element.171.grad_ref), kind=kOutput, calls=%fused_computation.10 | convolution fusion | flops 4834197504 | bytes 12582912 | tf_op jit(solution)/shard_map/dot_general | solution.py:40
  175.4 22.3 %feed_back.1 = (f32[1024,768]{1,0:T(8,128)}, bf16[768,3840]{1,0:T(8,128)(2,1)}, f32[8,3072]{1,0:T(8,128)}) custom-call(bf16[1024,768]{1,0:T(8,128)(2,1)} %copy-done.15, bf16[1024,768]{1,0:T(8,128)(2,1)} %copy-done.14, bf16[1024,3072]{1,0:T(8,128)(2,1)} %get-tuple-element.175.slope_ref, bf16[3072,768]{1,0:T(8,128)(2,1)} %all-gather.8.cloned.1.call-done.down_ref, ...), custom_call_target="tpu_custom_call" | custom-call | flops 14495514624 | bytes 31457280 | tf_op jit(solution)/shard_map/feed_back/pallas_call | solution.py:559
  197.7 6.2 %multiply_reduce_fusion = (f32[768]{0:T(1024)S(1)}, f32[1024]{0:T(1024)S(1)}, f32[1024]{0:T(1024)S(1)}, f32[768]{0:T(1024)S(1)}, f32[1024,768]{1,0:T(8,128)S(1)}, /*index=5*/bf16[1024,768]{1,0:T(8,128)(2,1)}) fusion(f32[1024,768]{1,0:T(8,128)S(1)} %copy-done.5, f32[1024]{0:T(1024)S(1)} %add_rsqrt_fusion.1, f32[1024]{0:T(1024)S(1)} %broadcast_multiply_fusion.4, ...), kind=kLoop, calls=%fused_computation.33 | loop fusion | flops 16511488 | bytes 15776768 | tf_op jit(solution)/shard_map/reduce_sum | solution.py:596
  205.1 2.8 copy-done.8
  207.8 1.4 fusion.31
  210.1 3.9 %convolution_convert_fusion.1.gc_ref = bf16[1024,768]{1,0:T(8,128)(2,1)} fusion(bf16[768,3840]{1,0:T(8,128)(2,1)} %all-gather.6.cloned.1.call-done.up_ref, f32[1024,768]{1,0:T(8,128)S(1)} %get-tuple-element.173), kind=kOutput, calls=%fused_computation.56 | convolution fusion | flops 1209532416 | bytes 5898240 | tf_op jit(solution)/shard_map/dot_general | solution.py:32
  214.0 14.5 %attend_back.2 = (bf16[1024,768]{1,0:T(8,128)(2,1)}, bf16[1024,768]{1,0:T(8,128)(2,1)}, bf16[1024,768]{1,0:T(8,128)(2,1)}, f32[768,512]{1,0:T(8,128)}, f32[768,512]{1,0:T(8,128)}) custom-call(bf16[1024,2304]{1,0:T(8,128)(2,1)} %copy-done, bf16[1024,2304]{1,0:T(8,128)(2,1)} %copy-done, bf16[1024,2304]{1,0:T(8,128)(2,1)} %copy-done, ...), custom_call_target="tpu_custom_call" | custom-call | flops 8589934592 | bytes 8388608 | tf_op jit(solution)/shard_map/attend_back/pallas_call | solution.py:423
  229.0 4.1 %add_convert_fusion.1 = bf16[2,2,96,3840]{3,2,1,0:T(8,128)(2,1)} fusion(bf16[2,2,96,3840]{3,2,1,0:T(8,128)(2,1)} %collective-permute-done.9, bf16[2,2,96,3840]{3,2,1,0:T(8,128)(2,1)S(1)} %get-tuple-element.90), kind=kLoop, calls=%fused_computation.9 | loop fusion | flops 5898240 | bytes 8847360 | tf_op jit(solution)/shard_map/convert_element_type | solution.py:665
  238.6 1.2 collective-permute-start.12
  239.9 25.5 %attend_back.3 = (bf16[1024,768]{1,0:T(8,128)(2,1)}, bf16[1024,768]{1,0:T(8,128)(2,1)}, bf16[1024,768]{1,0:T(8,128)(2,1)}, f32[768,512]{1,0:T(8,128)}, f32[768,512]{1,0:T(8,128)}) custom-call(bf16[1024,2304]{1,0:T(8,128)(2,1)} %copy-done, bf16[1024,2304]{1,0:T(8,128)(2,1)} %copy-done, ...), custom_call_target="tpu_custom_call", output_to_operand_aliasing={{0}: (9, {}), {1}: (10, {}), {2}: (11, {}), {3}: (12, {}), ... | custom-call | flops 17179869184 | bytes 16777216 | tf_op jit(solution)/shard_map/attend_back/pallas_call | solution.py:423
  265.5 13.5 %weigh.1 = (bf16[4,96,1536]{2,1,0:T(8,128)(2,1)}, bf16[4,96,1536]{2,1,0:T(8,128)(2,1)}, bf16[4,96,1408]{2,1,0:T(8,128)(2,1)}, bf16[4,96,1408]{2,1,0:T(8,128)(2,1)}) custom-call(s32[1]{0:T(128)} %bitcast.9.low_ref, bf16[1024,768]{1,0:T(8,128)(2,1)} %bitcast.96, bf16[1024,768]{1,0:T(8,128)(2,1)} %get-tuple-element.94.gq_ref, ...), custom_call_target="tpu_custom_call" | custom-call | flops 6039797760 | bytes 20971520 | tf_op jit(solution)/shard_map/weigh/pallas_call | solution.py:506
  279.0 1.4 collective-permute-start.14
  280.5 2.5 collective-permute-done.14
  284.0 1.8 add_convert_fusion.4
  286.8 1.5 add_convert_fusion.3
  292.1 2.5 collective-permute-start.18
  294.9 8.9 %fusion.26 = f32[1024,768]{1,0:T(8,128)} fusion(f32[1024,768]{1,0:T(8,128)S(1)} %copy-done.10, bf16[768,2944]{1,0:T(8,128)(2,1)} %all-gather.4.cloned.1.call-done.rel_ref.wq_ref.wk_ref, bf16[1024,768]{1,0:T(8,128)(2,1)} %get-tuple-element.96.gv_ref, bf16[1024,768]{1,0:T(8,128)(2,1)} %get-tuple-element.95.gk_ref, bf16[1024,768]{1,0:T(8,128)(2,1)} %get-tuple-element.94.gq_ref), kind=kOutput, calls=%fused_computation.55 | convolution fusion | flops 3638820864 | bytes 14548992 | tf_op jit(solution)/shard_map/dot_general | solution.py:32
  304.2 2.8 collective-permute-done.18
  307.0 3.4 collective-permute-done.19
  312.8 4.5 %collective-permute-done.21 = bf16[96,1408]{1,0:T(8,128)(2,1)S(1)} collective-permute-done((bf16[96,1408]{1,0:T(8,128)(2,1)S(1)}, bf16[96,1408]{1,0:T(8,128)(2,1)S(1)}, u32[]{:S(2)}, u32[]{:S(2)}) %collective-permute-start.21) | collective-permute-done | bytes 270368 | tf_op jit(solution)/shard_map/ppermute | solution.py:648
  317.4 2.1 collective-permute-done.20
  319.8 1.4 collective-permute-start.24
  323.7 2.8 collective-permute-done.23
  326.5 7.3 %collective-permute-done.24 = bf16[24,2944]{1,0:T(8,128)(2,1)S(1)} collective-permute-done((bf16[24,2944]{1,0:T(8,128)(2,1)S(1)}, bf16[24,2944]{1,0:T(8,128)(2,1)S(1)}, u32[]{:S(2)}, u32[]{:S(2)}) %collective-permute-start.24) | collective-permute-done | bytes 141344 | tf_op jit(solution)/shard_map/ppermute | solution.py:611
  (196 shorter events, 45.4 us)
Async XLA Ops:
  7.2 41.5 %copy-start.28 = (bf16[96,768]{1,0:T(8,128)(2,1)S(1)}, bf16[96,768]{1,0:T(8,128)(2,1)}, u32[]{:S(2)}) copy-start(bf16[96,768]{1,0:T(8,128)(2,1)} %param.35) | copy-start | bytes 442372
  7.2 60.2 %all-gather.4.cloned.1.call-start = ((), (), s32[]{:S(2)}) async-start(), calls=%async_computation.2 | async-start | bytes 5087232 | tf_op jit(solution)/shard_map/all_gather | solution.py:623
  12.2 4.6 %collective-permute-start = (bf16[24,2944]{1,0:T(8,128)(2,1)S(1)}, bf16[24,2944]{1,0:T(8,128)(2,1)S(1)}, u32[]{:S(2)}, u32[]{:S(2)}) collective-permute-start(bf16[24,2944]{1,0:T(8,128)(2,1)S(1)} %constant_dynamic-update-slice_fusion), channel_id=1, source_target_pairs={{0,1},{1,2},{2,3},{3,0},{4,5},{5,6},{6,7},{7,4},{8,9},{9,10},{10,1... | collective-permute-start | bytes 423944 | tf_op jit(solution)/shard_map/ppermute | solution.py:611
  13.5 11.5 %collective-permute-start.1 = (bf16[24,2944]{1,0:T(8,128)(2,1)S(1)}, bf16[24,2944]{1,0:T(8,128)(2,1)S(1)}, u32[]{:S(2)}, u32[]{:S(2)}) collective-permute-start(bf16[24,2944]{1,0:T(8,128)(2,1)S(1)} %constant_dynamic-update-slice_fusion), channel_id=1, source_target_pairs={{0,2},{1,3},{2,0},{3,1},{4,6},{5,7},{6,4},{7,5},{8,10},{9,11},{10,... | collective-permute-start | bytes 423944 | tf_op jit(solution)/shard_map/ppermute | solution.py:611
  14.6 13.2 %collective-permute-start.2 = (bf16[24,2944]{1,0:T(8,128)(2,1)S(1)}, bf16[24,2944]{1,0:T(8,128)(2,1)S(1)}, u32[]{:S(2)}, u32[]{:S(2)}) collective-permute-start(bf16[24,2944]{1,0:T(8,128)(2,1)S(1)} %constant_dynamic-update-slice_fusion), channel_id=1, source_target_pairs={{0,3},{1,0},{2,1},{3,2},{4,7},{5,4},{6,5},{7,6},{8,11},{9,8},{10,9... | collective-permute-start | bytes 423944 | tf_op jit(solution)/shard_map/ppermute | solution.py:611
  28.6 94.5 %all-gather.6.cloned.1.call-start = ((), (), s32[]{:S(2)}) async-start(), calls=%async_computation.3 | async-start | bytes 6635520 | tf_op jit(solution)/shard_map/all_gather | solution.py:623
  30.4 5.8 %collective-permute-start.3 = (bf16[24,3840]{1,0:T(8,128)(2,1)S(1)}, bf16[24,3840]{1,0:T(8,128)(2,1)S(1)}, u32[]{:S(2)}, u32[]{:S(2)}) collective-permute-start(bf16[24,3840]{1,0:T(8,128)(2,1)S(1)} %constant_dynamic-update-slice_fusion.4), channel_id=1, source_target_pairs={{0,1},{1,2},{2,3},{3,0},{4,5},{5,6},{6,7},{7,4},{8,9},{9,10},{10,1... | collective-permute-start | bytes 552968 | tf_op jit(solution)/shard_map/ppermute | solution.py:611
  30.4 15.7 %collective-permute-start.4 = (bf16[24,3840]{1,0:T(8,128)(2,1)S(1)}, bf16[24,3840]{1,0:T(8,128)(2,1)S(1)}, u32[]{:S(2)}, u32[]{:S(2)}) collective-permute-start(bf16[24,3840]{1,0:T(8,128)(2,1)S(1)} %constant_dynamic-update-slice_fusion.4), channel_id=1, source_target_pairs={{0,2},{1,3},{2,0},{3,1},{4,6},{5,7},{6,4},{7,5},{8,10},{9,11},{10,... | collective-permute-start | bytes 552968 | tf_op jit(solution)/shard_map/ppermute | solution.py:611
  30.8 16.9 %collective-permute-start.5 = (bf16[24,3840]{1,0:T(8,128)(2,1)S(1)}, bf16[24,3840]{1,0:T(8,128)(2,1)S(1)}, u32[]{:S(2)}, u32[]{:S(2)}) collective-permute-start(bf16[24,3840]{1,0:T(8,128)(2,1)S(1)} %constant_dynamic-update-slice_fusion.4), channel_id=1, source_target_pairs={{0,3},{1,0},{2,1},{3,2},{4,7},{5,4},{6,5},{7,6},{8,11},{9,8},{10,9... | collective-permute-start | bytes 552968 | tf_op jit(solution)/shard_map/ppermute | solution.py:611
  48.6 105.9 %all-gather.8.cloned.1.call-start = ((), (), s32[]{:S(2)}) async-start(), calls=%async_computation.4 | async-start | bytes 5308416 | tf_op jit(solution)/shard_map/all_gather | solution.py:623
  48.7 5.0 %collective-permute-start.6 = (bf16[96,768]{1,0:T(8,128)(2,1)S(1)}, bf16[96,768]{1,0:T(8,128)(2,1)S(1)}, u32[]{:S(2)}, u32[]{:S(2)}) collective-permute-start(bf16[96,768]{1,0:T(8,128)(2,1)S(1)} %copy-done.28), channel_id=1, source_target_pairs={{0,1},{1,2},{2,3},{3,0},{4,5},{5,6},{6,7},{7,4},{8,9},{9,10},{10,1... | collective-permute-start | bytes 442376 | tf_op jit(solution)/shard_map/ppermute | solution.py:611
  48.8 12.5 %collective-permute-start.7 = (bf16[96,768]{1,0:T(8,128)(2,1)S(1)}, bf16[96,768]{1,0:T(8,128)(2,1)S(1)}, u32[]{:S(2)}, u32[]{:S(2)}) collective-permute-start(bf16[96,768]{1,0:T(8,128)(2,1)S(1)} %copy-done.28), channel_id=1, source_target_pairs={{0,2},{1,3},{2,0},{3,1},{4,6},{5,7},{6,4},{7,5},{8,10},{9,11},{10,... | collective-permute-start | bytes 442376 | tf_op jit(solution)/shard_map/ppermute | solution.py:611
  50.4 13.8 %collective-permute-start.8 = (bf16[96,768]{1,0:T(8,128)(2,1)S(1)}, bf16[96,768]{1,0:T(8,128)(2,1)S(1)}, u32[]{:S(2)}, u32[]{:S(2)}) collective-permute-start(bf16[96,768]{1,0:T(8,128)(2,1)S(1)} %copy-done.28), channel_id=1, source_target_pairs={{0,3},{1,0},{2,1},{3,2},{4,7},{5,4},{6,5},{7,6},{8,11},{9,8},{10,9... | collective-permute-start | bytes 442376 | tf_op jit(solution)/shard_map/ppermute | solution.py:611
  53.7 16.9 %copy-start.7 = (bf16[2,1,512,768]{3,2,1,0:T(8,128)(2,1)S(1)}, bf16[2,1,512,768]{3,2,1,0:T(8,128)(2,1)}, u32[]{:S(2)}) copy-start(bf16[2,1,512,768]{3,2,1,0:T(8,128)(2,1)} %param.21) | copy-start | bytes 4718596
  65.0 163.9 %reduce-scatter.3.cloned.1.call-start = ((), (), s32[]{:S(2)}) async-start(), calls=%async_computation.5 | async-start | bytes 5308416 | tf_op jit(solution)/shard_map/reduce_scatter | solution.py:627
  70.5 4.5 %slice-start = ((s8[4521984]{0:T(1024)(128)(4,1)}), s8[4194304]{0:T(1024)(128)(4,1)S(1)}, s32[]{:S(2)}) async-start(s8[4521984]{0:T(1024)(128)(4,1)} %bitcast.83), calls=%async_computation.7 | async-start | bytes 8388608
  75.1 4.3 %copy-start.1 = (bf16[512,1536]{1,0:T(8,128)(2,1)}, bf16[512,1536]{1,0:T(8,128)(2,1)S(1)}, u32[]{:S(2)}) copy-start(bf16[512,1536]{1,0:T(8,128)(2,1)S(1)} %fusion.23.pq_ref.pk_ref) | copy-start | bytes 4718596
  75.1 4.3 %copy-start.3 = (s32[2,1]{0,1:T(1,128)S(1)}, s32[2,1]{0,1:T(1,128)}, u32[]{:S(2)}) copy-start(s32[2,1]{0,1:T(1,128)} %param.22) | copy-start | bytes 28
  126.6 4.4 %copy-start.29 = (bf16[768,3840]{1,0:T(8,128)(2,1)S(1)}, bf16[768,3840]{1,0:T(8,128)(2,1)}, u32[]{:S(2)}) copy-start(bf16[768,3840]{1,0:T(8,128)(2,1)} %all-gather.6.cloned.1.call-done.up_ref) | copy-start | bytes 17694724
  164.1 4.2 %slice-start.2 = ((s8[6291456]{0:T(1024)(128)(4,1)}), s8[4194304]{0:T(1024)(128)(4,1)S(1)}, s32[]{:S(2)}) async-start(s8[6291456]{0:T(1024)(128)(4,1)} %bitcast.103), calls=%async_computation.9 | async-start | bytes 8388608
  175.3 113.0 %reduce-scatter.5.cloned.1.call-start = ((), (), s32[]{:S(2)}) async-start(), calls=%async_computation.6 | async-start | bytes 3686400 | tf_op jit(solution)/shard_map/reduce_scatter | solution.py:680
  175.4 22.3 %copy-start.5 = (f32[1024,768]{1,0:T(8,128)S(1)}, f32[1024,768]{1,0:T(8,128)}, u32[]{:S(2)}) copy-start(f32[1024,768]{1,0:T(8,128)} %copy-done.4) | copy-start | bytes 9437188
  205.1 5.0 %copy-start.9 = (f32[1024,768]{1,0:T(8,128)}, f32[1024,768]{1,0:T(8,128)S(1)}, u32[]{:S(2)}) copy-start(f32[1024,768]{1,0:T(8,128)S(1)} %get-tuple-element.173) | copy-start | bytes 9437188
  209.7 18.8 %collective-permute-start.9 = (bf16[2,2,96,3840]{3,2,1,0:T(8,128)(2,1)S(1)}, bf16[2,2,96,3840]{3,2,1,0:T(8,128)(2,1)}, u32[]{:S(2)}, u32[]{:S(2)}) collective-permute-start(bf16[2,2,96,3840]{3,2,1,0:T(8,128)(2,1)S(1)} %get-tuple-element.177), channel_id=1, source_target_pairs={{0,4},{4,0},{8,12},{12,8},{16,20},{20,16},{24,28},{28,24},{1,5},{5... | collective-permute-start | bytes 8847368 | tf_op jit(solution)/shard_map/ppermute | solution.py:648
  236.3 29.1 %collective-permute-start.10 = (bf16[96,768]{1,0:T(8,128)(2,1)S(1)}, bf16[96,768]{1,0:T(8,128)(2,1)S(1)}, u32[]{:S(2)}, u32[]{:S(2)}) collective-permute-start(bf16[96,768]{1,0:T(8,128)(2,1)S(1)} %get-tuple-element.186), channel_id=1, source_target_pairs={{0,1},{1,2},{2,3},{3,0},{4,5},{5,6},{6,7},{7,4},{8,9},{9,10},{10,1... | collective-permute-start | bytes 442376 | tf_op jit(solution)/shard_map/ppermute | solution.py:611
  237.5 28.0 %collective-permute-start.11 = (bf16[96,768]{1,0:T(8,128)(2,1)S(1)}, bf16[96,768]{1,0:T(8,128)(2,1)S(1)}, u32[]{:S(2)}, u32[]{:S(2)}) collective-permute-start(bf16[96,768]{1,0:T(8,128)(2,1)S(1)} %get-tuple-element.185), channel_id=1, source_target_pairs={{0,2},{1,3},{2,0},{3,1},{4,6},{5,7},{6,4},{7,5},{8,10},{9,11},{10,... | collective-permute-start | bytes 442376 | tf_op jit(solution)/shard_map/ppermute | solution.py:611
  238.6 26.8 %collective-permute-start.12 = (bf16[96,768]{1,0:T(8,128)(2,1)S(1)}, bf16[96,768]{1,0:T(8,128)(2,1)S(1)}, u32[]{:S(2)}, u32[]{:S(2)}) collective-permute-start(bf16[96,768]{1,0:T(8,128)(2,1)S(1)} %get-tuple-element.184), channel_id=1, source_target_pairs={{0,3},{1,0},{2,1},{3,2},{4,7},{5,4},{6,5},{7,6},{8,11},{9,8},{10,9... | collective-permute-start | bytes 442376 | tf_op jit(solution)/shard_map/ppermute | solution.py:611
  265.4 13.5 %copy-start.22 = (bf16[96,768]{1,0:T(8,128)(2,1)}, bf16[96,768]{1,0:T(8,128)(2,1)S(1)}, u32[]{:S(2)}) copy-start(bf16[96,768]{1,0:T(8,128)(2,1)S(1)} %collective-permute-done.10) | copy-start | bytes 442372
  265.4 13.5 %copy-start.24 = (bf16[96,768]{1,0:T(8,128)(2,1)}, bf16[96,768]{1,0:T(8,128)(2,1)S(1)}, u32[]{:S(2)}) copy-start(bf16[96,768]{1,0:T(8,128)(2,1)S(1)} %collective-permute-done.11) | copy-start | bytes 442372
  265.5 13.5 %copy-start.26 = (bf16[96,768]{1,0:T(8,128)(2,1)}, bf16[96,768]{1,0:T(8,128)(2,1)S(1)}, u32[]{:S(2)}) copy-start(bf16[96,768]{1,0:T(8,128)(2,1)S(1)} %collective-permute-done.12) | copy-start | bytes 442372
  279.0 7.8 %copy-start.17 = (bf16[4,96,1536]{2,1,0:T(8,128)(2,1)S(1)}, bf16[4,96,1536]{2,1,0:T(8,128)(2,1)}, u32[]{:S(2)}) copy-start(bf16[4,96,1536]{2,1,0:T(8,128)(2,1)} %get-tuple-element.86) | copy-start | bytes 3538948
  279.0 4.0 %collective-permute-start.14 = (bf16[4,96,1408]{2,1,0:T(8,128)(2,1)}, bf16[4,96,1408]{2,1,0:T(8,128)(2,1)S(1)}, u32[]{:S(2)}, u32[]{:S(2)}) collective-permute-start(bf16[4,96,1408]{2,1,0:T(8,128)(2,1)} %get-tuple-element.89), channel_id=1, source_target_pairs={{0,4},{4,0},{8,12},{12,8},{16,20},{20,16},{24,28},{28,24},{1,5},{5... | collective-permute-start | bytes 3244040 | tf_op jit(solution)/shard_map/ppermute | solution.py:648
  280.4 5.3 %collective-permute-start.13 = (bf16[4,96,1536]{2,1,0:T(8,128)(2,1)}, bf16[4,96,1536]{2,1,0:T(8,128)(2,1)S(1)}, u32[]{:S(2)}, u32[]{:S(2)}) collective-permute-start(bf16[4,96,1536]{2,1,0:T(8,128)(2,1)} %get-tuple-element.87), channel_id=1, source_target_pairs={{0,4},{4,0},{8,12},{12,8},{16,20},{20,16},{24,28},{28,24},{1,5},{5... | collective-permute-start | bytes 3538952 | tf_op jit(solution)/shard_map/ppermute | solution.py:648
  288.4 6.5 %copy-start.10 = (f32[1024,768]{1,0:T(8,128)S(1)}, f32[1024,768]{1,0:T(8,128)}, u32[]{:S(2)}) copy-start(f32[1024,768]{1,0:T(8,128)} %copy-done.9) | copy-start | bytes 9437188
  288.4 15.4 %collective-permute-start.16 = (bf16[2,96,1408]{2,1,0:T(8,128)(2,1)S(1)}, bf16[2,96,1408]{2,1,0:T(8,128)(2,1)S(1)}, u32[]{:S(2)}, u32[]{:S(2)}) collective-permute-start(bf16[2,96,1408]{2,1,0:T(8,128)(2,1)S(1)} %dynamic-slice_bitcast_fusion.3), channel_id=1, source_target_pairs={{0,8},{4,12},{8,0},{12,4},{16,24},{20,28},{24,16},{28,20},{1,9},{5... | collective-permute-start | bytes 1622024 | tf_op jit(solution)/shard_map/ppermute | solution.py:648
  289.7 14.3 %collective-permute-start.15 = (bf16[2,96,1536]{2,1,0:T(8,128)(2,1)S(1)}, bf16[2,96,1536]{2,1,0:T(8,128)(2,1)S(1)}, u32[]{:S(2)}, u32[]{:S(2)}) collective-permute-start(bf16[2,96,1536]{2,1,0:T(8,128)(2,1)S(1)} %dynamic-slice_bitcast_fusion.2), channel_id=1, source_target_pairs={{0,16},{4,20},{8,24},{12,28},{16,0},{20,4},{24,8},{28,12},{1,17},{... | collective-permute-start | bytes 1769480 | tf_op jit(solution)/shard_map/ppermute | solution.py:648
  291.4 12.8 %collective-permute-start.17 = (bf16[24,3840]{1,0:T(8,128)(2,1)S(1)}, bf16[24,3840]{1,0:T(8,128)(2,1)S(1)}, u32[]{:S(2)}, u32[]{:S(2)}) collective-permute-start(bf16[24,3840]{1,0:T(8,128)(2,1)S(1)} %get-tuple-element.182), channel_id=1, source_target_pairs={{0,1},{1,2},{2,3},{3,0},{4,5},{5,6},{6,7},{7,4},{8,9},{9,10},{10,1... | collective-permute-start | bytes 552968 | tf_op jit(solution)/shard_map/ppermute | solution.py:611
  292.1 14.9 %collective-permute-start.18 = (bf16[24,3840]{1,0:T(8,128)(2,1)S(1)}, bf16[24,3840]{1,0:T(8,128)(2,1)S(1)}, u32[]{:S(2)}, u32[]{:S(2)}) collective-permute-start(bf16[24,3840]{1,0:T(8,128)(2,1)S(1)} %get-tuple-element.181), channel_id=1, source_target_pairs={{0,2},{1,3},{2,0},{3,1},{4,6},{5,7},{6,4},{7,5},{8,10},{9,11},{10,... | collective-permute-start | bytes 552968 | tf_op jit(solution)/shard_map/ppermute | solution.py:611
  294.6 15.8 %collective-permute-start.19 = (bf16[24,3840]{1,0:T(8,128)(2,1)S(1)}, bf16[24,3840]{1,0:T(8,128)(2,1)S(1)}, u32[]{:S(2)}, u32[]{:S(2)}) collective-permute-start(bf16[24,3840]{1,0:T(8,128)(2,1)S(1)} %get-tuple-element.180), channel_id=1, source_target_pairs={{0,3},{1,0},{2,1},{3,2},{4,7},{5,4},{6,5},{7,6},{8,11},{9,8},{10,9... | collective-permute-start | bytes 552968 | tf_op jit(solution)/shard_map/ppermute | solution.py:611
  303.8 7.7 %copy-start.20 = (bf16[96,768]{1,0:T(8,128)(2,1)S(1)}, bf16[96,768]{1,0:T(8,128)(2,1)}, u32[]{:S(2)}) copy-start(bf16[96,768]{1,0:T(8,128)(2,1)} %get-tuple-element.105) | copy-start | bytes 442372
  303.8 7.8 %copy-start.23 = (bf16[96,768]{1,0:T(8,128)(2,1)S(1)}, bf16[96,768]{1,0:T(8,128)(2,1)}, u32[]{:S(2)}) copy-start(bf16[96,768]{1,0:T(8,128)(2,1)} %copy-done.22) | copy-start | bytes 442372
  303.8 7.8 %copy-start.25 = (bf16[96,768]{1,0:T(8,128)(2,1)S(1)}, bf16[96,768]{1,0:T(8,128)(2,1)}, u32[]{:S(2)}) copy-start(bf16[96,768]{1,0:T(8,128)(2,1)} %copy-done.24) | copy-start | bytes 442372
  303.9 7.8 %copy-start.27 = (bf16[96,768]{1,0:T(8,128)(2,1)S(1)}, bf16[96,768]{1,0:T(8,128)(2,1)}, u32[]{:S(2)}) copy-start(bf16[96,768]{1,0:T(8,128)(2,1)} %copy-done.26) | copy-start | bytes 442372
  310.4 6.9 %collective-permute-start.21 = (bf16[96,1408]{1,0:T(8,128)(2,1)S(1)}, bf16[96,1408]{1,0:T(8,128)(2,1)S(1)}, u32[]{:S(2)}, u32[]{:S(2)}) collective-permute-start(bf16[96,1408]{1,0:T(8,128)(2,1)S(1)} %dynamic-slice_bitcast_fusion.5), channel_id=1, source_target_pairs={{0,16},{4,20},{8,24},{12,28},{16,0},{20,4},{24,8},{28,12},{1,17},{... | collective-permute-start | bytes 811016 | tf_op jit(solution)/shard_map/ppermute | solution.py:648
  312.4 7.1 %collective-permute-start.20 = (bf16[96,1536]{1,0:T(8,128)(2,1)S(1)}, bf16[96,1536]{1,0:T(8,128)(2,1)S(1)}, u32[]{:S(2)}, u32[]{:S(2)}) collective-permute-start(bf16[96,1536]{1,0:T(8,128)(2,1)S(1)} %dynamic-slice_bitcast_fusion.4), channel_id=1, source_target_pairs={{0,8},{4,12},{8,0},{12,4},{16,24},{20,28},{24,16},{28,20},{1,9},{5... | collective-permute-start | bytes 884744 | tf_op jit(solution)/shard_map/ppermute | solution.py:648
  319.7 4.0 %collective-permute-start.22 = (bf16[24,2944]{1,0:T(8,128)(2,1)S(1)}, bf16[24,2944]{1,0:T(8,128)(2,1)S(1)}, u32[]{:S(2)}, u32[]{:S(2)}) collective-permute-start(bf16[24,2944]{1,0:T(8,128)(2,1)S(1)} %get-tuple-element.188), channel_id=1, source_target_pairs={{0,1},{1,2},{2,3},{3,0},{4,5},{5,6},{6,7},{7,4},{8,9},{9,10},{10,1... | collective-permute-start | bytes 423944 | tf_op jit(solution)/shard_map/ppermute | solution.py:611
  319.7 6.7 %collective-permute-start.23 = (bf16[24,2944]{1,0:T(8,128)(2,1)S(1)}, bf16[24,2944]{1,0:T(8,128)(2,1)S(1)}, u32[]{:S(2)}, u32[]{:S(2)}) collective-permute-start(bf16[24,2944]{1,0:T(8,128)(2,1)S(1)} %get-tuple-element.189), channel_id=1, source_target_pairs={{0,2},{1,3},{2,0},{3,1},{4,6},{5,7},{6,4},{7,5},{8,10},{9,11},{10,... | collective-permute-start | bytes 423944 | tf_op jit(solution)/shard_map/ppermute | solution.py:611
  319.8 13.9 %collective-permute-start.24 = (bf16[24,2944]{1,0:T(8,128)(2,1)S(1)}, bf16[24,2944]{1,0:T(8,128)(2,1)S(1)}, u32[]{:S(2)}, u32[]{:S(2)}) collective-permute-start(bf16[24,2944]{1,0:T(8,128)(2,1)S(1)} %get-tuple-element.190), channel_id=1, source_target_pairs={{0,3},{1,0},{2,1},{3,2},{4,7},{5,4},{6,5},{7,6},{8,11},{9,8},{10,9... | collective-permute-start | bytes 423944 | tf_op jit(solution)/shard_map/ppermute | solution.py:611
  (16 other events, 31.7 us)
Sparse Core Ops, SparseCore 0:
  28.8 38.5 all-gather.3
  69.8 43.8 all-gather.5
  115.6 38.9 all-gather.7
  175.5 53.4 reduce-scatter.2
  233.2 42.2 reduce-scatter.4

commit v3 on v2

--- a/solution.py
+++ b/solution.py
@@ -779,6 +779,8 @@
     first_keep, first_send, second_keep, second_send = weigh(
         x, gq, gk, gv, gpq, gpk, first_pack, vector_grads
     )
+    first_keep, second_part = lax.optimization_barrier((first_keep, second_part))
+    second_pieces = scatter_narrow_start(second_part)
     upper = all_bits()[:-1]
     sides = lambda part: part.reshape((2,) * len(upper) + part.shape[1:])
     halves = [
@@ -795,8 +797,7 @@
         halves[0][0], halves[1][0] = kept[:2]
         return kept[2:]
 
-    gq, gk, gv, second_part = together(gq, gk, gv, second_part)
-    second_pieces = scatter_narrow_start(second_part)
+    gq, gk, gv = together(gq, gk, gv)
     grad_inputs = grad_first + dot_nt(jnp.concatenate([gq, gk, gv], axis=1), qkv_weight)
     halve_both()
     grad_inputs, *second_pieces = together(grad_inputs, *second_pieces)

time: 349 us -> 347 us (level)
    unnamed x79 -> x69, local copies, waits for them, and re-layouts: 19.4 us -> 18.4 us
  transfers between devices with their start and end apart: 30 -> 30, of which waited for: 20 -> 22; matrix products, arithmetic and copies ran while one was open for 19% -> 17% of each run, Pallas kernels for 34% -> 34%
where the time goes in v3:
time: 347 us; the launch traced here: 342 us
  Pallas kernels  116 us (33%)
  waiting for transfers between devices  81.9 us (24%)
  matrix products  54.1 us (16%)
  local copies, waits for them, and re-layouts  30 us (9%)
  other arithmetic  23.5 us (7%)
  starting transfers between devices  21.6 us (6%)
  between operations  15 us (4%)
    ppermute x18, waiting for transfers between devices, narrow_shifts(): lax.ppermute(block, 'narrow', [(i, (i + shift) % size) for i in range(siz...  56.2 us
    pallas_call x2, Pallas kernels, attend_back(): pl.pallas_call(functools.partial(attend_back_kernel, len(earlier)), grid=...  40.4 us
    pallas_call x1, Pallas kernels, attend(): pl.pallas_call(attend_kernel, grid_spec=pltpu.PrefetchScalarGridSpec(num_...  39.9 us
    dot_general x4, matrix products, dot_nn(): lax.dot_general(left, right, (((1,), (0,)), ((), ())), preferred_element_...  30.5 us
    pallas_call x1, Pallas kernels, feed_back(): pl.pallas_call(feed_back_kernel, grid=(blocks,), in_specs=[whole((tokens,...  22.3 us
    unnamed x69, local copies, waits for them, and re-layouts  18.4 us
    ppermute x18, starting transfers between devices, narrow_shifts(): lax.ppermute(block, 'narrow', [(i, (i + shift) % size) for i in range(siz...  17.1 us
    pallas_call x1, Pallas kernels, weigh(): pl.pallas_call(weigh_kernel, grid_spec=pltpu.PrefetchScalarGridSpec(num_s...  13.4 us
  transfers between devices with their start and end apart: 30, of which 22 were waited for; matrix products, arithmetic and copies ran while one was open for 17% of the time, Pallas kernels for 34%

profile of v3, /device:TPU:9, one launch (start us, length us, event | category | flops | bytes accessed | tf_op | source)
XLA Modules:
  0.0 342.0 jit_solution(18250107428456489384)
XLA Ops:
  12.2 1.3 collective-permute-start
  14.6 1.4 collective-permute-start.2
  16.8 8.2 %collective-permute-done.1 = bf16[24,2944]{1,0:T(8,128)(2,1)S(1)} collective-permute-done((bf16[24,2944]{1,0:T(8,128)(2,1)S(1)}, bf16[24,2944]{1,0:T(8,128)(2,1)S(1)}, u32[]{:S(2)}, u32[]{:S(2)}) %collective-permute-start.1) | collective-permute-done | bytes 141344 | tf_op jit(solution)/shard_map/ppermute | solution.py:611
  25.0 2.8 collective-permute-done.2
  30.8 1.4 collective-permute-start.5
  32.3 3.8 %collective-permute-done.3 = bf16[24,3840]{1,0:T(8,128)(2,1)S(1)} collective-permute-done((bf16[24,3840]{1,0:T(8,128)(2,1)S(1)}, bf16[24,3840]{1,0:T(8,128)(2,1)S(1)}, u32[]{:S(2)}, u32[]{:S(2)}) %collective-permute-start.3) | collective-permute-done | bytes 184352 | tf_op jit(solution)/shard_map/ppermute | solution.py:611
  36.2 10.0 %collective-permute-done.4 = bf16[24,3840]{1,0:T(8,128)(2,1)S(1)} collective-permute-done((bf16[24,3840]{1,0:T(8,128)(2,1)S(1)}, bf16[24,3840]{1,0:T(8,128)(2,1)S(1)}, u32[]{:S(2)}, u32[]{:S(2)}) %collective-permute-start.4) | collective-permute-done | bytes 184352 | tf_op jit(solution)/shard_map/ppermute | solution.py:611
  46.1 1.6 collective-permute-done.5
  48.8 1.6 collective-permute-start.7
  50.4 1.4 collective-permute-start.8
  51.8 1.8 collective-permute-done.6
  53.7 7.6 %collective-permute-done.7 = bf16[96,768]{1,0:T(8,128)(2,1)S(1)} collective-permute-done((bf16[96,768]{1,0:T(8,128)(2,1)S(1)}, bf16[96,768]{1,0:T(8,128)(2,1)S(1)}, u32[]{:S(2)}, u32[]{:S(2)}) %collective-permute-start.7) | collective-permute-done | bytes 147488 | tf_op jit(solution)/shard_map/ppermute | solution.py:611
  61.3 2.9 collective-permute-done.8
  65.1 2.3 all-gather.4.cloned.1.call-done.rel_ref.wq_ref.wk_ref
  69.2 1.3 slice_reduce_fusion.1
  71.3 3.7 %fusion.23.pq_ref.pk_ref = bf16[512,1536]{1,0:T(8,128)(2,1)S(1)} fusion(bf16[768,2944]{1,0:T(8,128)(2,1)} %all-gather.4.cloned.1.call-done.rel_ref.wq_ref.wk_ref, f32[1536]{0:T(1024)S(1)} %add.286), kind=kOutput, calls=%fused_computation.45 | convolution fusion | flops 1209532416 | bytes 4724736 | tf_op jit(solution)/shard_map/dot_general | solution.py:40
  75.1 4.3 %fusion.5.q_ref.k_ref.v_ref = bf16[1024,2304]{1,0:T(8,128)(2,1)S(1)} fusion(bf16[1024,768]{1,0:T(8,128)(2,1)S(1)} %bitcast.97, f32[2304]{0:T(1024)S(1)} %add.283, bf16[768,2944]{1,0:T(8,128)(2,1)S(1)} %bitcast.84), kind=kOutput, calls=%fused_computation.11 | convolution fusion | flops 3628597248 | bytes 9842688 | tf_op jit(solution)/shard_map/dot_general | solution.py:36
  79.4 39.9 %attend.1 = (bf16[1024,768]{1,0:T(8,128)(2,1)S(1)}, f32[1024,768]{1,0:T(8,128)S(1)}, bf16[2,12,512,512]{3,2,1,0:T(8,128)(2,1)}, f32[2,12,512,128]{3,2,1,0:T(8,128)}) custom-call(s32[2]{0:T(128)S(1)} %bitcast.82, bf16[1024,2304]{1,0:T(8,128)(2,1)S(1)} %fusion.5.q_ref.k_ref.v_ref, bf16[1024,2304]{1,0:T(8,128)(2,1)S(1)} %fusion.5.q_ref.k_ref.v_ref, ...), custom_call_target="tpu_custom_call" | custom-call | flops 12884901888 | bytes 20971520 | tf_op jit(solution)/shard_map/attend/pallas_call | solution.py:251
  119.3 2.1 copy-done
  121.4 1.7 copy-done.2
  123.1 3.5 %fusion.52 = (f32[1024]{0:T(1024)S(1)}, f32[1024,768]{1,0:T(8,128)S(1)}) fusion(f32[768]{0:T(1024)S(1)} %get-tuple-element.162, bf16[1024,768]{1,0:T(8,128)(2,1)S(1)} %get-tuple-element.65, bf16[768,3840]{1,0:T(8,128)(2,1)} %all-gather.6.cloned.1.call-done.up_ref, bf16[1024,768]{1,0:T(8,128)(2,1)} %bitcast.95), kind=kOutput, calls=%fused_computation.168 | convolution fusion | flops 1211104256 | bytes 7478272 | tf_op jit(solution)/shard_map/dot_general | solution.py:36
  131.0 13.2 %fusion.4 = (bf16[1024,3072]{1,0:T(8,128)(2,1)}, bf16[1024,3072]{1,0:T(8,128)(2,1)}) fusion(f32[3072]{0:T(1024)S(1)} %add.297, bf16[1024,768]{1,0:T(8,128)(2,1)S(1)} %fusion.24.hidden_ref, bf16[768,3840]{1,0:T(8,128)(2,1)S(1)} %copy-done.24), kind=kOutput, calls=%fused_computation.5 | convolution fusion | flops 4869586944 | bytes 18886656 | tf_op jit(solution)/shard_map/dot_general | solution.py:36
  144.2 10.3 %all-gather.8.cloned.1.call-done.down_ref = bf16[3072,768]{1,0:T(8,128)(2,1)} async-done(((bf16[384,768]{1,0:T(8,128)(2,1)}), bf16[3072,768]{1,0:T(8,128)(2,1)}) %all-gather.8.cloned.1.call-update) | async-done | bytes 4718608 | tf_op jit(solution)/shard_map/all_gather | solution.py:623
  154.6 9.5 %fusion.53 = (f32[1024]{0:T(1024)S(1)}, f32[1024,768]{1,0:T(8,128)S(1)}) fusion(f32[768]{0:T(1024)S(1)} %get-tuple-element.159, bf16[1024,3072]{1,0:T(8,128)(2,1)} %get-tuple-element.178, bf16[3072,768]{1,0:T(8,128)(2,1)} %all-gather.8.cloned.1.call-done.down_ref, f32[768]{0:T(1024)S(1)} %get-tuple-element.160, f32[768]{0:T(1024)S(1)} %get-tuple-element.161, ...), kind=kOutput, calls=%fused_computation.169 | convolution fusion | flops 4837342208 | bytes 17323008 | tf_op jit(solution)/shard_map/dot_general | solution.py:36
  168.3 7.0 %convolution_convert_fusion = bf16[3072,768]{1,0:T(8,128)(2,1)} fusion(bf16[1024,3072]{1,0:T(8,128)(2,1)S(1)} %bitcast.104, bf16[1024,768]{1,0:T(8,128)(2,1)S(1)} %get-tuple-element.173.grad_ref), kind=kOutput, calls=%fused_computation.10 | convolution fusion | flops 4834197504 | bytes 12582912 | tf_op jit(solution)/shard_map/dot_general | solution.py:40
  175.4 22.3 %feed_back.1 = (f32[1024,768]{1,0:T(8,128)}, bf16[768,3840]{1,0:T(8,128)(2,1)}, f32[8,3072]{1,0:T(8,128)}) custom-call(bf16[1024,768]{1,0:T(8,128)(2,1)} %copy-done.15, bf16[1024,768]{1,0:T(8,128)(2,1)} %copy-done.14, bf16[1024,3072]{1,0:T(8,128)(2,1)} %get-tuple-element.177.slope_ref, bf16[3072,768]{1,0:T(8,128)(2,1)} %all-gather.8.cloned.1.call-done.down_ref, ...), custom_call_target="tpu_custom_call" | custom-call | flops 14495514624 | bytes 31457280 | tf_op jit(solution)/shard_map/feed_back/pallas_call | solution.py:559
  197.8 6.2 %multiply_reduce_fusion = (f32[768]{0:T(1024)S(1)}, f32[1024]{0:T(1024)S(1)}, f32[1024]{0:T(1024)S(1)}, f32[768]{0:T(1024)S(1)}, f32[1024,768]{1,0:T(8,128)S(1)}, /*index=5*/bf16[1024,768]{1,0:T(8,128)(2,1)}) fusion(f32[1024,768]{1,0:T(8,128)S(1)} %copy-done.5, f32[1024]{0:T(1024)S(1)} %add_rsqrt_fusion.1, f32[1024]{0:T(1024)S(1)} %broadcast_multiply_fusion.4, ...), kind=kLoop, calls=%fused_computation.33 | loop fusion | flops 16511488 | bytes 15776768 | tf_op jit(solution)/shard_map/reduce_sum | solution.py:596
  205.1 2.8 copy-done.8
  207.8 1.4 fusion.31
  210.1 3.9 %convolution_convert_fusion.1.gc_ref = bf16[1024,768]{1,0:T(8,128)(2,1)} fusion(bf16[768,3840]{1,0:T(8,128)(2,1)} %all-gather.6.cloned.1.call-done.up_ref, f32[1024,768]{1,0:T(8,128)S(1)} %get-tuple-element.175), kind=kOutput, calls=%fused_computation.56 | convolution fusion | flops 1209532416 | bytes 5898240 | tf_op jit(solution)/shard_map/dot_general | solution.py:32
  214.0 14.4 %attend_back.2 = (bf16[1024,768]{1,0:T(8,128)(2,1)}, bf16[1024,768]{1,0:T(8,128)(2,1)}, bf16[1024,768]{1,0:T(8,128)(2,1)}, f32[768,512]{1,0:T(8,128)}, f32[768,512]{1,0:T(8,128)}) custom-call(bf16[1024,2304]{1,0:T(8,128)(2,1)} %copy-done, bf16[1024,2304]{1,0:T(8,128)(2,1)} %copy-done, bf16[1024,2304]{1,0:T(8,128)(2,1)} %copy-done, ...), custom_call_target="tpu_custom_call" | custom-call | flops 8589934592 | bytes 8388608 | tf_op jit(solution)/shard_map/attend_back/pallas_call | solution.py:423
  229.0 4.1 %add_convert_fusion.1 = bf16[2,2,96,3840]{3,2,1,0:T(8,128)(2,1)} fusion(bf16[2,2,96,3840]{3,2,1,0:T(8,128)(2,1)} %collective-permute-done.9, bf16[2,2,96,3840]{3,2,1,0:T(8,128)(2,1)S(1)} %get-tuple-element.88), kind=kLoop, calls=%fused_computation.9 | loop fusion | flops 5898240 | bytes 8847360 | tf_op jit(solution)/shard_map/convert_element_type | solution.py:665
  235.6 1.3 collective-permute-start.10
  238.0 1.2 collective-permute-start.12
  239.3 25.9 %attend_back.3 = (bf16[1024,768]{1,0:T(8,128)(2,1)}, bf16[1024,768]{1,0:T(8,128)(2,1)}, bf16[1024,768]{1,0:T(8,128)(2,1)}, f32[768,512]{1,0:T(8,128)}, f32[768,512]{1,0:T(8,128)}) custom-call(bf16[1024,2304]{1,0:T(8,128)(2,1)} %copy-done, bf16[1024,2304]{1,0:T(8,128)(2,1)} %copy-done, ...), custom_call_target="tpu_custom_call", output_to_operand_aliasing={{0}: (9, {}), {1}: (10, {}), {2}: (11, {}), {3}: (12, {}), ... | custom-call | flops 17179869184 | bytes 16777216 | tf_op jit(solution)/shard_map/attend_back/pallas_call | solution.py:423
  265.2 13.4 %weigh.1 = (bf16[4,96,1536]{2,1,0:T(8,128)(2,1)}, bf16[4,96,1536]{2,1,0:T(8,128)(2,1)}, bf16[4,96,1408]{2,1,0:T(8,128)(2,1)}, bf16[4,96,1408]{2,1,0:T(8,128)(2,1)}) custom-call(s32[1]{0:T(128)} %bitcast.9.low_ref, bf16[1024,768]{1,0:T(8,128)(2,1)} %bitcast.96, bf16[1024,768]{1,0:T(8,128)(2,1)} %get-tuple-element.96.gq_ref, ...), custom_call_target="tpu_custom_call" | custom-call | flops 6039797760 | bytes 20971520 | tf_op jit(solution)/shard_map/weigh/pallas_call | solution.py:506
  279.7 3.3 collective-permute-done.14
  284.0 1.9 add_convert_fusion.4
  286.1 2.1 add_convert_fusion.3
  290.7 2.4 collective-permute-start.18
  293.4 7.5 %fusion.26 = f32[1024,768]{1,0:T(8,128)} fusion(f32[1024,768]{1,0:T(8,128)S(1)} %copy-done.10, bf16[768,2944]{1,0:T(8,128)(2,1)} %all-gather.4.cloned.1.call-done.rel_ref.wq_ref.wk_ref, bf16[1024,768]{1,0:T(8,128)(2,1)S(1)} %copy-done.19, bf16[1024,768]{1,0:T(8,128)(2,1)S(1)} %copy-done.18, bf16[1024,768]{1,0:T(8,128)(2,1)S(1)} %copy-done.17), kind=kOutput, calls=%fused_computation.55 | convolution fusion | flops 3638820864 | bytes 14548992 | tf_op jit(solution)/shard_map/dot_general | solution.py:32
  301.9 1.8 collective-permute-done.15
  303.9 1.7 collective-permute-done.18
  305.6 4.1 %collective-permute-done.19 = bf16[24,3840]{1,0:T(8,128)(2,1)S(1)} collective-permute-done((bf16[24,3840]{1,0:T(8,128)(2,1)S(1)}, bf16[24,3840]{1,0:T(8,128)(2,1)S(1)}, u32[]{:S(2)}, u32[]{:S(2)}) %collective-permute-start.19) | collective-permute-done | bytes 184352 | tf_op jit(solution)/shard_map/ppermute | solution.py:611
  311.4 5.7 %collective-permute-done.21 = bf16[96,1408]{1,0:T(8,128)(2,1)S(1)} collective-permute-done((bf16[96,1408]{1,0:T(8,128)(2,1)S(1)}, bf16[96,1408]{1,0:T(8,128)(2,1)S(1)}, u32[]{:S(2)}, u32[]{:S(2)}) %collective-permute-start.21) | collective-permute-done | bytes 270368 | tf_op jit(solution)/shard_map/ppermute | solution.py:648
  318.3 1.4 collective-permute-start.24
  322.1 2.8 collective-permute-done.23
  325.0 7.3 %collective-permute-done.24 = bf16[24,2944]{1,0:T(8,128)(2,1)S(1)} collective-permute-done((bf16[24,2944]{1,0:T(8,128)(2,1)S(1)}, bf16[24,2944]{1,0:T(8,128)(2,1)S(1)}, u32[]{:S(2)}, u32[]{:S(2)}) %collective-permute-start.24) | collective-permute-done | bytes 141344 | tf_op jit(solution)/shard_map/ppermute | solution.py:611
  (186 shorter events, 43.6 us)
Async XLA Ops:
  7.2 41.5 %copy-start.23 = (bf16[96,768]{1,0:T(8,128)(2,1)S(1)}, bf16[96,768]{1,0:T(8,128)(2,1)}, u32[]{:S(2)}) copy-start(bf16[96,768]{1,0:T(8,128)(2,1)} %param.35) | copy-start | bytes 442372
  7.2 60.2 %all-gather.4.cloned.1.call-start = ((), (), s32[]{:S(2)}) async-start(), calls=%async_computation.2 | async-start | bytes 5087232 | tf_op jit(solution)/shard_map/all_gather | solution.py:623
  12.2 4.6 %collective-permute-start = (bf16[24,2944]{1,0:T(8,128)(2,1)S(1)}, bf16[24,2944]{1,0:T(8,128)(2,1)S(1)}, u32[]{:S(2)}, u32[]{:S(2)}) collective-permute-start(bf16[24,2944]{1,0:T(8,128)(2,1)S(1)} %constant_dynamic-update-slice_fusion), channel_id=1, source_target_pairs={{0,1},{1,2},{2,3},{3,0},{4,5},{5,6},{6,7},{7,4},{8,9},{9,10},{10,1... | collective-permute-start | bytes 423944 | tf_op jit(solution)/shard_map/ppermute | solution.py:611
  13.5 11.5 %collective-permute-start.1 = (bf16[24,2944]{1,0:T(8,128)(2,1)S(1)}, bf16[24,2944]{1,0:T(8,128)(2,1)S(1)}, u32[]{:S(2)}, u32[]{:S(2)}) collective-permute-start(bf16[24,2944]{1,0:T(8,128)(2,1)S(1)} %constant_dynamic-update-slice_fusion), channel_id=1, source_target_pairs={{0,2},{1,3},{2,0},{3,1},{4,6},{5,7},{6,4},{7,5},{8,10},{9,11},{10,... | collective-permute-start | bytes 423944 | tf_op jit(solution)/shard_map/ppermute | solution.py:611
  14.6 13.2 %collective-permute-start.2 = (bf16[24,2944]{1,0:T(8,128)(2,1)S(1)}, bf16[24,2944]{1,0:T(8,128)(2,1)S(1)}, u32[]{:S(2)}, u32[]{:S(2)}) collective-permute-start(bf16[24,2944]{1,0:T(8,128)(2,1)S(1)} %constant_dynamic-update-slice_fusion), channel_id=1, source_target_pairs={{0,3},{1,0},{2,1},{3,2},{4,7},{5,4},{6,5},{7,6},{8,11},{9,8},{10,9... | collective-permute-start | bytes 423944 | tf_op jit(solution)/shard_map/ppermute | solution.py:611
  28.6 94.5 %all-gather.6.cloned.1.call-start = ((), (), s32[]{:S(2)}) async-start(), calls=%async_computation.3 | async-start | bytes 6635520 | tf_op jit(solution)/shard_map/all_gather | solution.py:623
  30.4 5.8 %collective-permute-start.3 = (bf16[24,3840]{1,0:T(8,128)(2,1)S(1)}, bf16[24,3840]{1,0:T(8,128)(2,1)S(1)}, u32[]{:S(2)}, u32[]{:S(2)}) collective-permute-start(bf16[24,3840]{1,0:T(8,128)(2,1)S(1)} %constant_dynamic-update-slice_fusion.4), channel_id=1, source_target_pairs={{0,1},{1,2},{2,3},{3,0},{4,5},{5,6},{6,7},{7,4},{8,9},{9,10},{10,1... | collective-permute-start | bytes 552968 | tf_op jit(solution)/shard_map/ppermute | solution.py:611
  30.4 15.7 %collective-permute-start.4 = (bf16[24,3840]{1,0:T(8,128)(2,1)S(1)}, bf16[24,3840]{1,0:T(8,128)(2,1)S(1)}, u32[]{:S(2)}, u32[]{:S(2)}) collective-permute-start(bf16[24,3840]{1,0:T(8,128)(2,1)S(1)} %constant_dynamic-update-slice_fusion.4), channel_id=1, source_target_pairs={{0,2},{1,3},{2,0},{3,1},{4,6},{5,7},{6,4},{7,5},{8,10},{9,11},{10,... | collective-permute-start | bytes 552968 | tf_op jit(solution)/shard_map/ppermute | solution.py:611
  30.8 16.9 %collective-permute-start.5 = (bf16[24,3840]{1,0:T(8,128)(2,1)S(1)}, bf16[24,3840]{1,0:T(8,128)(2,1)S(1)}, u32[]{:S(2)}, u32[]{:S(2)}) collective-permute-start(bf16[24,3840]{1,0:T(8,128)(2,1)S(1)} %constant_dynamic-update-slice_fusion.4), channel_id=1, source_target_pairs={{0,3},{1,0},{2,1},{3,2},{4,7},{5,4},{6,5},{7,6},{8,11},{9,8},{10,9... | collective-permute-start | bytes 552968 | tf_op jit(solution)/shard_map/ppermute | solution.py:611
  48.6 106.0 %all-gather.8.cloned.1.call-start = ((), (), s32[]{:S(2)}) async-start(), calls=%async_computation.4 | async-start | bytes 5308416 | tf_op jit(solution)/shard_map/all_gather | solution.py:623
  48.7 5.0 %collective-permute-start.6 = (bf16[96,768]{1,0:T(8,128)(2,1)S(1)}, bf16[96,768]{1,0:T(8,128)(2,1)S(1)}, u32[]{:S(2)}, u32[]{:S(2)}) collective-permute-start(bf16[96,768]{1,0:T(8,128)(2,1)S(1)} %copy-done.23), channel_id=1, source_target_pairs={{0,1},{1,2},{2,3},{3,0},{4,5},{5,6},{6,7},{7,4},{8,9},{9,10},{10,1... | collective-permute-start | bytes 442376 | tf_op jit(solution)/shard_map/ppermute | solution.py:611
  48.8 12.5 %collective-permute-start.7 = (bf16[96,768]{1,0:T(8,128)(2,1)S(1)}, bf16[96,768]{1,0:T(8,128)(2,1)S(1)}, u32[]{:S(2)}, u32[]{:S(2)}) collective-permute-start(bf16[96,768]{1,0:T(8,128)(2,1)S(1)} %copy-done.23), channel_id=1, source_target_pairs={{0,2},{1,3},{2,0},{3,1},{4,6},{5,7},{6,4},{7,5},{8,10},{9,11},{10,... | collective-permute-start | bytes 442376 | tf_op jit(solution)/shard_map/ppermute | solution.py:611
  50.4 13.8 %collective-permute-start.8 = (bf16[96,768]{1,0:T(8,128)(2,1)S(1)}, bf16[96,768]{1,0:T(8,128)(2,1)S(1)}, u32[]{:S(2)}, u32[]{:S(2)}) collective-permute-start(bf16[96,768]{1,0:T(8,128)(2,1)S(1)} %copy-done.23), channel_id=1, source_target_pairs={{0,3},{1,0},{2,1},{3,2},{4,7},{5,4},{6,5},{7,6},{8,11},{9,8},{10,9... | collective-permute-start | bytes 442376 | tf_op jit(solution)/shard_map/ppermute | solution.py:611
  53.7 16.9 %copy-start.7 = (bf16[2,1,512,768]{3,2,1,0:T(8,128)(2,1)S(1)}, bf16[2,1,512,768]{3,2,1,0:T(8,128)(2,1)}, u32[]{:S(2)}) copy-start(bf16[2,1,512,768]{3,2,1,0:T(8,128)(2,1)} %param.21) | copy-start | bytes 4718596
  65.1 163.9 %reduce-scatter.3.cloned.1.call-start = ((), (), s32[]{:S(2)}) async-start(), calls=%async_computation.5 | async-start | bytes 5308416 | tf_op jit(solution)/shard_map/reduce_scatter | solution.py:627
  70.5 4.5 %slice-start = ((s8[4521984]{0:T(1024)(128)(4,1)}), s8[4194304]{0:T(1024)(128)(4,1)S(1)}, s32[]{:S(2)}) async-start(s8[4521984]{0:T(1024)(128)(4,1)} %bitcast.83), calls=%async_computation.7 | async-start | bytes 8388608
  71.3 3.8 %slice-start.1 = ((s8[4521984]{0:T(1024)(128)(4,1)}), s8[327680]{0:T(1024)(128)(4,1)S(1)}, s32[]{:S(2)}) async-start(s8[4521984]{0:T(1024)(128)(4,1)} %bitcast.83), calls=%async_computation.8 | async-start | bytes 655360
  71.3 3.8 %copy-start.16 = (bf16[2,1,512,768]{3,2,1,0:T(8,128)(2,1)S(1)}, bf16[2,1,512,768]{3,2,1,0:T(8,128)(2,1)}, u32[]{:S(2)}) copy-start(bf16[2,1,512,768]{3,2,1,0:T(8,128)(2,1)} %param.20) | copy-start | bytes 4718596
  75.1 4.3 %copy-start.1 = (bf16[512,1536]{1,0:T(8,128)(2,1)}, bf16[512,1536]{1,0:T(8,128)(2,1)S(1)}, u32[]{:S(2)}) copy-start(bf16[512,1536]{1,0:T(8,128)(2,1)S(1)} %fusion.23.pq_ref.pk_ref) | copy-start | bytes 4718596
  75.1 4.3 %copy-start.3 = (s32[2,1]{0,1:T(1,128)S(1)}, s32[2,1]{0,1:T(1,128)}, u32[]{:S(2)}) copy-start(s32[2,1]{0,1:T(1,128)} %param.22) | copy-start | bytes 28
  126.6 4.4 %copy-start.24 = (bf16[768,3840]{1,0:T(8,128)(2,1)S(1)}, bf16[768,3840]{1,0:T(8,128)(2,1)}, u32[]{:S(2)}) copy-start(bf16[768,3840]{1,0:T(8,128)(2,1)} %all-gather.6.cloned.1.call-done.up_ref) | copy-start | bytes 17694724
  164.1 4.2 %slice-start.2 = ((s8[6291456]{0:T(1024)(128)(4,1)}), s8[4194304]{0:T(1024)(128)(4,1)S(1)}, s32[]{:S(2)}) async-start(s8[6291456]{0:T(1024)(128)(4,1)} %bitcast.103), calls=%async_computation.9 | async-start | bytes 8388608
  164.7 3.6 %slice-start.3 = ((s8[6291456]{0:T(1024)(128)(4,1)}), s8[2097152]{0:T(1024)(128)(4,1)S(1)}, s32[]{:S(2)}) async-start(s8[6291456]{0:T(1024)(128)(4,1)} %bitcast.103), calls=%async_computation.10 | async-start | bytes 4194304
  175.3 110.7 %reduce-scatter.5.cloned.1.call-start = ((), (), s32[]{:S(2)}) async-start(), calls=%async_computation.6 | async-start | bytes 3686400 | tf_op jit(solution)/shard_map/reduce_scatter | solution.py:680
  175.4 22.4 %copy-start.5 = (f32[1024,768]{1,0:T(8,128)S(1)}, f32[1024,768]{1,0:T(8,128)}, u32[]{:S(2)}) copy-start(f32[1024,768]{1,0:T(8,128)} %copy-done.4) | copy-start | bytes 9437188
  204.0 3.9 %copy-start.8 = (bf16[768,3840]{1,0:T(8,128)(2,1)S(1)}, bf16[768,3840]{1,0:T(8,128)(2,1)}, u32[]{:S(2)}) copy-start(bf16[768,3840]{1,0:T(8,128)(2,1)} %get-tuple-element.67) | copy-start | bytes 17694724
  205.1 5.0 %copy-start.9 = (f32[1024,768]{1,0:T(8,128)}, f32[1024,768]{1,0:T(8,128)S(1)}, u32[]{:S(2)}) copy-start(f32[1024,768]{1,0:T(8,128)S(1)} %get-tuple-element.175) | copy-start | bytes 9437188
  209.7 18.8 %collective-permute-start.9 = (bf16[2,2,96,3840]{3,2,1,0:T(8,128)(2,1)S(1)}, bf16[2,2,96,3840]{3,2,1,0:T(8,128)(2,1)}, u32[]{:S(2)}, u32[]{:S(2)}) collective-permute-start(bf16[2,2,96,3840]{3,2,1,0:T(8,128)(2,1)S(1)} %get-tuple-element.179), channel_id=1, source_target_pairs={{0,4},{4,0},{8,12},{12,8},{16,20},{20,16},{24,28},{28,24},{1,5},{5... | collective-permute-start | bytes 8847368 | tf_op jit(solution)/shard_map/ppermute | solution.py:648
  235.6 29.6 %collective-permute-start.10 = (bf16[96,768]{1,0:T(8,128)(2,1)S(1)}, bf16[96,768]{1,0:T(8,128)(2,1)S(1)}, u32[]{:S(2)}, u32[]{:S(2)}) collective-permute-start(bf16[96,768]{1,0:T(8,128)(2,1)S(1)} %get-tuple-element.188), channel_id=1, source_target_pairs={{0,1},{1,2},{2,3},{3,0},{4,5},{5,6},{6,7},{7,4},{8,9},{9,10},{10,1... | collective-permute-start | bytes 442376 | tf_op jit(solution)/shard_map/ppermute | solution.py:611
  236.9 28.3 %collective-permute-start.11 = (bf16[96,768]{1,0:T(8,128)(2,1)S(1)}, bf16[96,768]{1,0:T(8,128)(2,1)S(1)}, u32[]{:S(2)}, u32[]{:S(2)}) collective-permute-start(bf16[96,768]{1,0:T(8,128)(2,1)S(1)} %get-tuple-element.187), channel_id=1, source_target_pairs={{0,2},{1,3},{2,0},{3,1},{4,6},{5,7},{6,4},{7,5},{8,10},{9,11},{10,... | collective-permute-start | bytes 442376 | tf_op jit(solution)/shard_map/ppermute | solution.py:611
  238.0 27.2 %collective-permute-start.12 = (bf16[96,768]{1,0:T(8,128)(2,1)S(1)}, bf16[96,768]{1,0:T(8,128)(2,1)S(1)}, u32[]{:S(2)}, u32[]{:S(2)}) collective-permute-start(bf16[96,768]{1,0:T(8,128)(2,1)S(1)} %get-tuple-element.186), channel_id=1, source_target_pairs={{0,3},{1,0},{2,1},{3,2},{4,7},{5,4},{6,5},{7,6},{8,11},{9,8},{10,9... | collective-permute-start | bytes 442376 | tf_op jit(solution)/shard_map/ppermute | solution.py:611
  278.6 4.4 %collective-permute-start.14 = (bf16[4,96,1408]{2,1,0:T(8,128)(2,1)}, bf16[4,96,1408]{2,1,0:T(8,128)(2,1)S(1)}, u32[]{:S(2)}, u32[]{:S(2)}) collective-permute-start(bf16[4,96,1408]{2,1,0:T(8,128)(2,1)} %get-tuple-element.93), channel_id=1, source_target_pairs={{0,4},{4,0},{8,12},{12,8},{16,20},{20,16},{24,28},{28,24},{1,5},{5... | collective-permute-start | bytes 3244040 | tf_op jit(solution)/shard_map/ppermute | solution.py:648
  279.7 6.4 %collective-permute-start.13 = (bf16[4,96,1536]{2,1,0:T(8,128)(2,1)}, bf16[4,96,1536]{2,1,0:T(8,128)(2,1)}, u32[]{:S(2)}, u32[]{:S(2)}) collective-permute-start(bf16[4,96,1536]{2,1,0:T(8,128)(2,1)} %get-tuple-element.91), channel_id=1, source_target_pairs={{0,4},{4,0},{8,12},{12,8},{16,20},{20,16},{24,28},{28,24},{1,5},{5... | collective-permute-start | bytes 3538952 | tf_op jit(solution)/shard_map/ppermute | solution.py:648
  284.0 9.4 %copy-start.19 = (bf16[1024,768]{1,0:T(8,128)(2,1)S(1)}, bf16[1024,768]{1,0:T(8,128)(2,1)}, u32[]{:S(2)}) copy-start(bf16[1024,768]{1,0:T(8,128)(2,1)} %get-tuple-element.98.gv_ref) | copy-start | bytes 4718596
  286.0 4.2 %copy-start.21 = (bf16[96,3840]{1,0:T(8,128)(2,1)S(1)}, bf16[96,3840]{1,0:T(8,128)(2,1)}, u32[]{:S(2)}) copy-start(bf16[96,3840]{1,0:T(8,128)(2,1)} %reduce-scatter.5.cloned.1.call-done) | copy-start | bytes 2211844
  286.0 7.4 %copy-start.10 = (f32[1024,768]{1,0:T(8,128)S(1)}, f32[1024,768]{1,0:T(8,128)}, u32[]{:S(2)}) copy-start(f32[1024,768]{1,0:T(8,128)} %copy-done.9) | copy-start | bytes 9437188
  286.0 7.4 %copy-start.17 = (bf16[1024,768]{1,0:T(8,128)(2,1)S(1)}, bf16[1024,768]{1,0:T(8,128)(2,1)}, u32[]{:S(2)}) copy-start(bf16[1024,768]{1,0:T(8,128)(2,1)} %get-tuple-element.96.gq_ref) | copy-start | bytes 4718596
  286.0 7.4 %copy-start.18 = (bf16[1024,768]{1,0:T(8,128)(2,1)S(1)}, bf16[1024,768]{1,0:T(8,128)(2,1)}, u32[]{:S(2)}) copy-start(bf16[1024,768]{1,0:T(8,128)(2,1)} %get-tuple-element.97.gk_ref) | copy-start | bytes 4718596
  288.2 13.6 %collective-permute-start.16 = (bf16[2,96,1408]{2,1,0:T(8,128)(2,1)S(1)}, bf16[2,96,1408]{2,1,0:T(8,128)(2,1)S(1)}, u32[]{:S(2)}, u32[]{:S(2)}) collective-permute-start(bf16[2,96,1408]{2,1,0:T(8,128)(2,1)S(1)} %dynamic-slice_bitcast_fusion.3), channel_id=1, source_target_pairs={{0,8},{4,12},{8,0},{12,4},{16,24},{20,28},{24,16},{28,20},{1,9},{5... | collective-permute-start | bytes 1622024 | tf_op jit(solution)/shard_map/ppermute | solution.py:648
  289.4 14.3 %collective-permute-start.15 = (bf16[2,96,1536]{2,1,0:T(8,128)(2,1)S(1)}, bf16[2,96,1536]{2,1,0:T(8,128)(2,1)S(1)}, u32[]{:S(2)}, u32[]{:S(2)}) collective-permute-start(bf16[2,96,1536]{2,1,0:T(8,128)(2,1)S(1)} %dynamic-slice_bitcast_fusion.2), channel_id=1, source_target_pairs={{0,16},{4,20},{8,24},{12,28},{16,0},{20,4},{24,8},{28,12},{1,17},{... | collective-permute-start | bytes 1769480 | tf_op jit(solution)/shard_map/ppermute | solution.py:648
  290.2 13.6 %collective-permute-start.17 = (bf16[24,3840]{1,0:T(8,128)(2,1)S(1)}, bf16[24,3840]{1,0:T(8,128)(2,1)S(1)}, u32[]{:S(2)}, u32[]{:S(2)}) collective-permute-start(bf16[24,3840]{1,0:T(8,128)(2,1)S(1)} %get-tuple-element.184), channel_id=1, source_target_pairs={{0,1},{1,2},{2,3},{3,0},{4,5},{5,6},{6,7},{7,4},{8,9},{9,10},{10,1... | collective-permute-start | bytes 552968 | tf_op jit(solution)/shard_map/ppermute | solution.py:611
  290.7 14.9 %collective-permute-start.18 = (bf16[24,3840]{1,0:T(8,128)(2,1)S(1)}, bf16[24,3840]{1,0:T(8,128)(2,1)S(1)}, u32[]{:S(2)}, u32[]{:S(2)}) collective-permute-start(bf16[24,3840]{1,0:T(8,128)(2,1)S(1)} %get-tuple-element.183), channel_id=1, source_target_pairs={{0,2},{1,3},{2,0},{3,1},{4,6},{5,7},{6,4},{7,5},{8,10},{9,11},{10,... | collective-permute-start | bytes 552968 | tf_op jit(solution)/shard_map/ppermute | solution.py:611
  293.2 16.5 %collective-permute-start.19 = (bf16[24,3840]{1,0:T(8,128)(2,1)S(1)}, bf16[24,3840]{1,0:T(8,128)(2,1)S(1)}, u32[]{:S(2)}, u32[]{:S(2)}) collective-permute-start(bf16[24,3840]{1,0:T(8,128)(2,1)S(1)} %get-tuple-element.182), channel_id=1, source_target_pairs={{0,3},{1,0},{2,1},{3,2},{4,7},{5,4},{6,5},{7,6},{8,11},{9,8},{10,9... | collective-permute-start | bytes 552968 | tf_op jit(solution)/shard_map/ppermute | solution.py:611
  309.7 7.3 %collective-permute-start.21 = (bf16[96,1408]{1,0:T(8,128)(2,1)S(1)}, bf16[96,1408]{1,0:T(8,128)(2,1)S(1)}, u32[]{:S(2)}, u32[]{:S(2)}) collective-permute-start(bf16[96,1408]{1,0:T(8,128)(2,1)S(1)} %dynamic-slice_bitcast_fusion.5), channel_id=1, source_target_pairs={{0,16},{4,20},{8,24},{12,28},{16,0},{20,4},{24,8},{28,12},{1,17},{... | collective-permute-start | bytes 811016 | tf_op jit(solution)/shard_map/ppermute | solution.py:648
  310.9 7.1 %collective-permute-start.20 = (bf16[96,1536]{1,0:T(8,128)(2,1)S(1)}, bf16[96,1536]{1,0:T(8,128)(2,1)S(1)}, u32[]{:S(2)}, u32[]{:S(2)}) collective-permute-start(bf16[96,1536]{1,0:T(8,128)(2,1)S(1)} %dynamic-slice_bitcast_fusion.4), channel_id=1, source_target_pairs={{0,8},{4,12},{8,0},{12,4},{16,24},{20,28},{24,16},{28,20},{1,9},{5... | collective-permute-start | bytes 884744 | tf_op jit(solution)/shard_map/ppermute | solution.py:648
  318.2 4.0 %collective-permute-start.22 = (bf16[24,2944]{1,0:T(8,128)(2,1)S(1)}, bf16[24,2944]{1,0:T(8,128)(2,1)S(1)}, u32[]{:S(2)}, u32[]{:S(2)}) collective-permute-start(bf16[24,2944]{1,0:T(8,128)(2,1)S(1)} %get-tuple-element.190), channel_id=1, source_target_pairs={{0,1},{1,2},{2,3},{3,0},{4,5},{5,6},{6,7},{7,4},{8,9},{9,10},{10,1... | collective-permute-start | bytes 423944 | tf_op jit(solution)/shard_map/ppermute | solution.py:611
  318.2 6.7 %collective-permute-start.23 = (bf16[24,2944]{1,0:T(8,128)(2,1)S(1)}, bf16[24,2944]{1,0:T(8,128)(2,1)S(1)}, u32[]{:S(2)}, u32[]{:S(2)}) collective-permute-start(bf16[24,2944]{1,0:T(8,128)(2,1)S(1)} %get-tuple-element.191), channel_id=1, source_target_pairs={{0,2},{1,3},{2,0},{3,1},{4,6},{5,7},{6,4},{7,5},{8,10},{9,11},{10,... | collective-permute-start | bytes 423944 | tf_op jit(solution)/shard_map/ppermute | solution.py:611
  318.3 13.9 %collective-permute-start.24 = (bf16[24,2944]{1,0:T(8,128)(2,1)S(1)}, bf16[24,2944]{1,0:T(8,128)(2,1)S(1)}, u32[]{:S(2)}, u32[]{:S(2)}) collective-permute-start(bf16[24,2944]{1,0:T(8,128)(2,1)S(1)} %get-tuple-element.192), channel_id=1, source_target_pairs={{0,3},{1,0},{2,1},{3,2},{4,7},{5,4},{6,5},{7,6},{8,11},{9,8},{10,9... | collective-permute-start | bytes 423944 | tf_op jit(solution)/shard_map/ppermute | solution.py:611
  (11 other events, 15.6 us)
Sparse Core Ops, SparseCore 0:
  28.8 38.5 all-gather.3
  69.8 43.8 all-gather.5
  115.6 38.9 all-gather.7
  175.4 53.4 reduce-scatter.2
  233.2 42.2 reduce-scatter.4

commit v4 on v3

--- a/solution.py
+++ b/solution.py
@@ -20,7 +20,7 @@
 DELAYS = (0, 1)
 LOG2E = 1.4426950408889634
 VECTORS = 128
-EARLY = 2
+EARLY = 3
 SCALE = 1.0 / math.sqrt(3 * HEAD)
 AXES = ("wide", "narrow")
 norm_epsilon = 1e-06

time: 347 us -> 344 us (level)
    unnamed x69 -> x83, local copies, waits for them, and re-layouts: 18.4 us -> 18.4 us
  transfers between devices with their start and end apart: 30 -> 30, of which waited for: 22 -> 21; matrix products, arithmetic and copies ran while one was open for 17% -> 18% of each run, Pallas kernels for 34% -> 34%
where the time goes in v4:
time: 344 us; the launch traced here: 339 us
  Pallas kernels  116 us (34%)
  waiting for transfers between devices  80.3 us (23%)
  matrix products  54.2 us (16%)
  local copies, waits for them, and re-layouts  30.7 us (9%)
  starting transfers between devices  21.7 us (6%)
  other arithmetic  21.6 us (6%)
  between operations  15 us (4%)
    ppermute x18, waiting for transfers between devices, narrow_shifts(): lax.ppermute(block, 'narrow', [(i, (i + shift) % size) for i in range(siz...  55.4 us
    pallas_call x1, Pallas kernels, attend(): pl.pallas_call(attend_kernel, grid_spec=pltpu.PrefetchScalarGridSpec(num_...  39.9 us
    pallas_call x2, Pallas kernels, attend_back(): pl.pallas_call(functools.partial(attend_back_kernel, len(earlier)), grid=...  39.9 us
    dot_general x4, matrix products, dot_nn(): lax.dot_general(left, right, (((1,), (0,)), ((), ())), preferred_element_...  30.4 us
    pallas_call x1, Pallas kernels, feed_back(): pl.pallas_call(feed_back_kernel, grid=(blocks,), in_specs=[whole((tokens,...  22.4 us
    unnamed x83, local copies, waits for them, and re-layouts  18.4 us
    ppermute x18, starting transfers between devices, narrow_shifts(): lax.ppermute(block, 'narrow', [(i, (i + shift) % size) for i in range(siz...  17 us
    pallas_call x1, Pallas kernels, weigh(): pl.pallas_call(weigh_kernel, grid_spec=pltpu.PrefetchScalarGridSpec(num_s...  13.5 us
  transfers between devices with their start and end apart: 30, of which 21 were waited for; matrix products, arithmetic and copies ran while one was open for 18% of the time, Pallas kernels for 34%

profile of v4, /device:TPU:9, one launch (start us, length us, event | category | flops | bytes accessed | tf_op | source)
XLA Modules:
  0.0 339.1 jit_solution(5713205766268308874)
XLA Ops:
  12.2 1.3 collective-permute-start
  14.6 1.4 collective-permute-start.2
  16.8 8.2 %collective-permute-done.1 = bf16[24,2944]{1,0:T(8,128)(2,1)S(1)} collective-permute-done((bf16[24,2944]{1,0:T(8,128)(2,1)S(1)}, bf16[24,2944]{1,0:T(8,128)(2,1)S(1)}, u32[]{:S(2)}, u32[]{:S(2)}) %collective-permute-start.1) | collective-permute-done | bytes 141344 | tf_op jit(solution)/shard_map/ppermute | solution.py:611
  25.0 2.8 collective-permute-done.2
  30.8 1.4 collective-permute-start.5
  32.3 3.8 %collective-permute-done.3 = bf16[24,3840]{1,0:T(8,128)(2,1)S(1)} collective-permute-done((bf16[24,3840]{1,0:T(8,128)(2,1)S(1)}, bf16[24,3840]{1,0:T(8,128)(2,1)S(1)}, u32[]{:S(2)}, u32[]{:S(2)}) %collective-permute-start.3) | collective-permute-done | bytes 184352 | tf_op jit(solution)/shard_map/ppermute | solution.py:611
  36.2 10.0 %collective-permute-done.4 = bf16[24,3840]{1,0:T(8,128)(2,1)S(1)} collective-permute-done((bf16[24,3840]{1,0:T(8,128)(2,1)S(1)}, bf16[24,3840]{1,0:T(8,128)(2,1)S(1)}, u32[]{:S(2)}, u32[]{:S(2)}) %collective-permute-start.4) | collective-permute-done | bytes 184352 | tf_op jit(solution)/shard_map/ppermute | solution.py:611
  46.1 1.6 collective-permute-done.5
  48.8 1.6 collective-permute-start.7
  50.4 1.4 collective-permute-start.8
  51.8 1.8 collective-permute-done.6
  53.7 7.6 %collective-permute-done.7 = bf16[96,768]{1,0:T(8,128)(2,1)S(1)} collective-permute-done((bf16[96,768]{1,0:T(8,128)(2,1)S(1)}, bf16[96,768]{1,0:T(8,128)(2,1)S(1)}, u32[]{:S(2)}, u32[]{:S(2)}) %collective-permute-start.7) | collective-permute-done | bytes 147488 | tf_op jit(solution)/shard_map/ppermute | solution.py:611
  61.3 2.9 collective-permute-done.8
  65.1 2.3 all-gather.4.cloned.1.call-done.rel_ref.wq_ref.wk_ref
  69.2 1.3 slice_reduce_fusion.1
  71.3 3.7 %fusion.23.pq_ref.pk_ref = bf16[512,1536]{1,0:T(8,128)(2,1)S(1)} fusion(bf16[768,2944]{1,0:T(8,128)(2,1)} %all-gather.4.cloned.1.call-done.rel_ref.wq_ref.wk_ref, f32[1536]{0:T(1024)S(1)} %add.286), kind=kOutput, calls=%fused_computation.45 | convolution fusion | flops 1209532416 | bytes 4724736 | tf_op jit(solution)/shard_map/dot_general | solution.py:40
  75.1 4.3 %fusion.5.q_ref.k_ref.v_ref = bf16[1024,2304]{1,0:T(8,128)(2,1)S(1)} fusion(bf16[1024,768]{1,0:T(8,128)(2,1)S(1)} %bitcast.97, f32[2304]{0:T(1024)S(1)} %add.283, bf16[768,2944]{1,0:T(8,128)(2,1)S(1)} %bitcast.84), kind=kOutput, calls=%fused_computation.11 | convolution fusion | flops 3628597248 | bytes 9842688 | tf_op jit(solution)/shard_map/dot_general | solution.py:36
  79.4 39.9 %attend.1 = (bf16[1024,768]{1,0:T(8,128)(2,1)S(1)}, f32[1024,768]{1,0:T(8,128)S(1)}, bf16[2,12,512,512]{3,2,1,0:T(8,128)(2,1)}, f32[2,12,512,128]{3,2,1,0:T(8,128)}) custom-call(s32[2]{0:T(128)S(1)} %bitcast.82, bf16[1024,2304]{1,0:T(8,128)(2,1)S(1)} %fusion.5.q_ref.k_ref.v_ref, bf16[1024,2304]{1,0:T(8,128)(2,1)S(1)} %fusion.5.q_ref.k_ref.v_ref, ...), custom_call_target="tpu_custom_call" | custom-call | flops 12884901888 | bytes 20971520 | tf_op jit(solution)/shard_map/attend/pallas_call | solution.py:251
  119.3 2.1 copy-done
  121.5 1.7 copy-done.2
  123.2 3.5 %fusion.52 = (f32[1024]{0:T(1024)S(1)}, f32[1024,768]{1,0:T(8,128)S(1)}) fusion(f32[768]{0:T(1024)S(1)} %get-tuple-element.162, bf16[1024,768]{1,0:T(8,128)(2,1)S(1)} %get-tuple-element.65, bf16[768,3840]{1,0:T(8,128)(2,1)} %all-gather.6.cloned.1.call-done.up_ref, bf16[1024,768]{1,0:T(8,128)(2,1)} %bitcast.95), kind=kOutput, calls=%fused_computation.168 | convolution fusion | flops 1211104256 | bytes 7478272 | tf_op jit(solution)/shard_map/dot_general | solution.py:36
  131.0 13.1 %fusion.4 = (bf16[1024,3072]{1,0:T(8,128)(2,1)}, bf16[1024,3072]{1,0:T(8,128)(2,1)}) fusion(f32[3072]{0:T(1024)S(1)} %add.297, bf16[1024,768]{1,0:T(8,128)(2,1)S(1)} %fusion.24.hidden_ref, bf16[768,3840]{1,0:T(8,128)(2,1)S(1)} %copy-done.31), kind=kOutput, calls=%fused_computation.5 | convolution fusion | flops 4869586944 | bytes 18886656 | tf_op jit(solution)/shard_map/dot_general | solution.py:36
  144.2 10.4 %all-gather.8.cloned.1.call-done.down_ref = bf16[3072,768]{1,0:T(8,128)(2,1)} async-done(((bf16[384,768]{1,0:T(8,128)(2,1)}), bf16[3072,768]{1,0:T(8,128)(2,1)}) %all-gather.8.cloned.1.call-update) | async-done | bytes 4718608 | tf_op jit(solution)/shard_map/all_gather | solution.py:623
  154.6 9.5 %fusion.53 = (f32[1024]{0:T(1024)S(1)}, f32[1024,768]{1,0:T(8,128)S(1)}) fusion(f32[768]{0:T(1024)S(1)} %get-tuple-element.159, bf16[1024,3072]{1,0:T(8,128)(2,1)} %get-tuple-element.178, bf16[3072,768]{1,0:T(8,128)(2,1)} %all-gather.8.cloned.1.call-done.down_ref, f32[768]{0:T(1024)S(1)} %get-tuple-element.160, f32[768]{0:T(1024)S(1)} %get-tuple-element.161, ...), kind=kOutput, calls=%fused_computation.169 | convolution fusion | flops 4837342208 | bytes 17323008 | tf_op jit(solution)/shard_map/dot_general | solution.py:36
  168.3 7.0 %convolution_convert_fusion = bf16[3072,768]{1,0:T(8,128)(2,1)} fusion(bf16[1024,3072]{1,0:T(8,128)(2,1)S(1)} %bitcast.104, bf16[1024,768]{1,0:T(8,128)(2,1)S(1)} %get-tuple-element.173.grad_ref), kind=kOutput, calls=%fused_computation.10 | convolution fusion | flops 4834197504 | bytes 12582912 | tf_op jit(solution)/shard_map/dot_general | solution.py:40
  175.4 22.4 %feed_back.1 = (f32[1024,768]{1,0:T(8,128)}, bf16[768,3840]{1,0:T(8,128)(2,1)}, f32[8,3072]{1,0:T(8,128)}) custom-call(bf16[1024,768]{1,0:T(8,128)(2,1)} %copy-done.17, bf16[1024,768]{1,0:T(8,128)(2,1)} %copy-done.16, bf16[1024,3072]{1,0:T(8,128)(2,1)} %get-tuple-element.177.slope_ref, bf16[3072,768]{1,0:T(8,128)(2,1)} %all-gather.8.cloned.1.call-done.down_ref, ...), custom_call_target="tpu_custom_call" | custom-call | flops 14495514624 | bytes 31457280 | tf_op jit(solution)/shard_map/feed_back/pallas_call | solution.py:559
  197.8 6.1 %multiply_reduce_fusion = (f32[768]{0:T(1024)S(1)}, f32[1024]{0:T(1024)S(1)}, f32[1024]{0:T(1024)S(1)}, f32[768]{0:T(1024)S(1)}, f32[1024,768]{1,0:T(8,128)S(1)}, /*index=5*/bf16[1024,768]{1,0:T(8,128)(2,1)}) fusion(f32[1024,768]{1,0:T(8,128)S(1)} %copy-done.5, f32[1024]{0:T(1024)S(1)} %add_rsqrt_fusion.1, f32[1024]{0:T(1024)S(1)} %broadcast_multiply_fusion.4, ...), kind=kLoop, calls=%fused_computation.33 | loop fusion | flops 16511488 | bytes 15776768 | tf_op jit(solution)/shard_map/reduce_sum | solution.py:596
  205.1 2.8 copy-done.11
  207.9 1.4 fusion.31
  210.1 3.9 %convolution_convert_fusion.1.gc_ref = bf16[1024,768]{1,0:T(8,128)(2,1)} fusion(bf16[768,3840]{1,0:T(8,128)(2,1)} %all-gather.6.cloned.1.call-done.up_ref, f32[1024,768]{1,0:T(8,128)S(1)} %get-tuple-element.175), kind=kOutput, calls=%fused_computation.56 | convolution fusion | flops 1209532416 | bytes 5898240 | tf_op jit(solution)/shard_map/dot_general | solution.py:32
  214.0 19.9 %attend_back.2 = (bf16[1024,768]{1,0:T(8,128)(2,1)}, bf16[1024,768]{1,0:T(8,128)(2,1)}, bf16[1024,768]{1,0:T(8,128)(2,1)}, f32[768,512]{1,0:T(8,128)}, f32[768,512]{1,0:T(8,128)}) custom-call(bf16[1024,2304]{1,0:T(8,128)(2,1)} %copy-done, bf16[1024,2304]{1,0:T(8,128)(2,1)} %copy-done, bf16[1024,2304]{1,0:T(8,128)(2,1)} %copy-done, ...), custom_call_target="tpu_custom_call" | custom-call | flops 12884901888 | bytes 12582912 | tf_op jit(solution)/shard_map/attend_back/pallas_call | solution.py:423
  233.9 4.1 %add_convert_fusion.1 = bf16[2,2,96,3840]{3,2,1,0:T(8,128)(2,1)} fusion(bf16[2,2,96,3840]{3,2,1,0:T(8,128)(2,1)} %collective-permute-done.9, bf16[2,2,96,3840]{3,2,1,0:T(8,128)(2,1)S(1)} %get-tuple-element.88), kind=kLoop, calls=%fused_computation.9 | loop fusion | flops 5898240 | bytes 8847360 | tf_op jit(solution)/shard_map/convert_element_type | solution.py:665
  243.4 1.5 collective-permute-start.12
  244.9 20.0 %attend_back.3 = (bf16[1024,768]{1,0:T(8,128)(2,1)}, bf16[1024,768]{1,0:T(8,128)(2,1)}, bf16[1024,768]{1,0:T(8,128)(2,1)}, f32[768,512]{1,0:T(8,128)}, f32[768,512]{1,0:T(8,128)}) custom-call(bf16[1024,2304]{1,0:T(8,128)(2,1)} %copy-done, bf16[1024,2304]{1,0:T(8,128)(2,1)} %copy-done, ...), custom_call_target="tpu_custom_call", output_to_operand_aliasing={{0}: (9, {}), {1}: (10, {}), {2}: (11, {}), {3}: (12, {}), ... | custom-call | flops 12884901888 | bytes 12582912 | tf_op jit(solution)/shard_map/attend_back/pallas_call | solution.py:423
  264.9 13.5 %weigh.1 = (bf16[4,96,1536]{2,1,0:T(8,128)(2,1)}, bf16[4,96,1536]{2,1,0:T(8,128)(2,1)}, bf16[4,96,1408]{2,1,0:T(8,128)(2,1)}, bf16[4,96,1408]{2,1,0:T(8,128)(2,1)}) custom-call(s32[1]{0:T(128)} %bitcast.9.low_ref, bf16[1024,768]{1,0:T(8,128)(2,1)} %bitcast.96, bf16[1024,768]{1,0:T(8,128)(2,1)} %get-tuple-element.96.gq_ref, ...), custom_call_target="tpu_custom_call" | custom-call | flops 6039797760 | bytes 20971520 | tf_op jit(solution)/shard_map/weigh/pallas_call | solution.py:506
  279.5 2.5 collective-permute-done.14
  283.0 1.8 add_convert_fusion.4
  287.4 2.6 collective-permute-start.18
  290.0 7.7 %fusion.26 = f32[1024,768]{1,0:T(8,128)} fusion(f32[1024,768]{1,0:T(8,128)} %copy-done.12, bf16[768,2944]{1,0:T(8,128)(2,1)} %all-gather.4.cloned.1.call-done.rel_ref.wq_ref.wk_ref, bf16[1024,768]{1,0:T(8,128)(2,1)S(1)} %copy-done.10, bf16[1024,768]{1,0:T(8,128)(2,1)S(1)} %copy-done.9, bf16[1024,768]{1,0:T(8,128)(2,1)S(1)} %copy-done.8), kind=kOutput, calls=%fused_computation.55 | convolution fusion | flops 3638820864 | bytes 14548992 | tf_op jit(solution)/shard_map/dot_general | solution.py:32
  298.9 1.9 collective-permute-done.15
  300.9 1.4 collective-permute-done.18
  302.4 3.6 %collective-permute-done.19 = bf16[24,3840]{1,0:T(8,128)(2,1)S(1)} collective-permute-done((bf16[24,3840]{1,0:T(8,128)(2,1)S(1)}, bf16[24,3840]{1,0:T(8,128)(2,1)S(1)}, u32[]{:S(2)}, u32[]{:S(2)}) %collective-permute-start.19) | collective-permute-done | bytes 184352 | tf_op jit(solution)/shard_map/ppermute | solution.py:611
  306.0 1.3 collective-permute-start.21
  308.3 4.7 %collective-permute-done.21 = bf16[96,1408]{1,0:T(8,128)(2,1)S(1)} collective-permute-done((bf16[96,1408]{1,0:T(8,128)(2,1)S(1)}, bf16[96,1408]{1,0:T(8,128)(2,1)S(1)}, u32[]{:S(2)}, u32[]{:S(2)}) %collective-permute-start.21) | collective-permute-done | bytes 270368 | tf_op jit(solution)/shard_map/ppermute | solution.py:648
  313.0 2.1 collective-permute-done.20
  315.4 1.4 collective-permute-start.24
  319.3 2.8 collective-permute-done.23
  322.1 7.3 %collective-permute-done.24 = bf16[24,2944]{1,0:T(8,128)(2,1)S(1)} collective-permute-done((bf16[24,2944]{1,0:T(8,128)(2,1)S(1)}, bf16[24,2944]{1,0:T(8,128)(2,1)S(1)}, u32[]{:S(2)}, u32[]{:S(2)}) %collective-permute-start.24) | collective-permute-done | bytes 141344 | tf_op jit(solution)/shard_map/ppermute | solution.py:611
  (200 shorter events, 43.1 us)
Async XLA Ops:
  7.2 41.5 %copy-start.30 = (bf16[96,768]{1,0:T(8,128)(2,1)S(1)}, bf16[96,768]{1,0:T(8,128)(2,1)}, u32[]{:S(2)}) copy-start(bf16[96,768]{1,0:T(8,128)(2,1)} %param.35) | copy-start | bytes 442372
  7.2 60.2 %all-gather.4.cloned.1.call-start = ((), (), s32[]{:S(2)}) async-start(), calls=%async_computation.2 | async-start | bytes 5087232 | tf_op jit(solution)/shard_map/all_gather | solution.py:623
  12.2 4.6 %collective-permute-start = (bf16[24,2944]{1,0:T(8,128)(2,1)S(1)}, bf16[24,2944]{1,0:T(8,128)(2,1)S(1)}, u32[]{:S(2)}, u32[]{:S(2)}) collective-permute-start(bf16[24,2944]{1,0:T(8,128)(2,1)S(1)} %constant_dynamic-update-slice_fusion), channel_id=1, source_target_pairs={{0,1},{1,2},{2,3},{3,0},{4,5},{5,6},{6,7},{7,4},{8,9},{9,10},{10,1... | collective-permute-start | bytes 423944 | tf_op jit(solution)/shard_map/ppermute | solution.py:611
  13.5 11.5 %collective-permute-start.1 = (bf16[24,2944]{1,0:T(8,128)(2,1)S(1)}, bf16[24,2944]{1,0:T(8,128)(2,1)S(1)}, u32[]{:S(2)}, u32[]{:S(2)}) collective-permute-start(bf16[24,2944]{1,0:T(8,128)(2,1)S(1)} %constant_dynamic-update-slice_fusion), channel_id=1, source_target_pairs={{0,2},{1,3},{2,0},{3,1},{4,6},{5,7},{6,4},{7,5},{8,10},{9,11},{10,... | collective-permute-start | bytes 423944 | tf_op jit(solution)/shard_map/ppermute | solution.py:611
  14.6 13.2 %collective-permute-start.2 = (bf16[24,2944]{1,0:T(8,128)(2,1)S(1)}, bf16[24,2944]{1,0:T(8,128)(2,1)S(1)}, u32[]{:S(2)}, u32[]{:S(2)}) collective-permute-start(bf16[24,2944]{1,0:T(8,128)(2,1)S(1)} %constant_dynamic-update-slice_fusion), channel_id=1, source_target_pairs={{0,3},{1,0},{2,1},{3,2},{4,7},{5,4},{6,5},{7,6},{8,11},{9,8},{10,9... | collective-permute-start | bytes 423944 | tf_op jit(solution)/shard_map/ppermute | solution.py:611
  28.6 94.5 %all-gather.6.cloned.1.call-start = ((), (), s32[]{:S(2)}) async-start(), calls=%async_computation.3 | async-start | bytes 6635520 | tf_op jit(solution)/shard_map/all_gather | solution.py:623
  30.4 5.8 %collective-permute-start.3 = (bf16[24,3840]{1,0:T(8,128)(2,1)S(1)}, bf16[24,3840]{1,0:T(8,128)(2,1)S(1)}, u32[]{:S(2)}, u32[]{:S(2)}) collective-permute-start(bf16[24,3840]{1,0:T(8,128)(2,1)S(1)} %constant_dynamic-update-slice_fusion.4), channel_id=1, source_target_pairs={{0,1},{1,2},{2,3},{3,0},{4,5},{5,6},{6,7},{7,4},{8,9},{9,10},{10,1... | collective-permute-start | bytes 552968 | tf_op jit(solution)/shard_map/ppermute | solution.py:611
  30.4 15.7 %collective-permute-start.4 = (bf16[24,3840]{1,0:T(8,128)(2,1)S(1)}, bf16[24,3840]{1,0:T(8,128)(2,1)S(1)}, u32[]{:S(2)}, u32[]{:S(2)}) collective-permute-start(bf16[24,3840]{1,0:T(8,128)(2,1)S(1)} %constant_dynamic-update-slice_fusion.4), channel_id=1, source_target_pairs={{0,2},{1,3},{2,0},{3,1},{4,6},{5,7},{6,4},{7,5},{8,10},{9,11},{10,... | collective-permute-start | bytes 552968 | tf_op jit(solution)/shard_map/ppermute | solution.py:611
  30.8 16.9 %collective-permute-start.5 = (bf16[24,3840]{1,0:T(8,128)(2,1)S(1)}, bf16[24,3840]{1,0:T(8,128)(2,1)S(1)}, u32[]{:S(2)}, u32[]{:S(2)}) collective-permute-start(bf16[24,3840]{1,0:T(8,128)(2,1)S(1)} %constant_dynamic-update-slice_fusion.4), channel_id=1, source_target_pairs={{0,3},{1,0},{2,1},{3,2},{4,7},{5,4},{6,5},{7,6},{8,11},{9,8},{10,9... | collective-permute-start | bytes 552968 | tf_op jit(solution)/shard_map/ppermute | solution.py:611
  48.6 105.9 %all-gather.8.cloned.1.call-start = ((), (), s32[]{:S(2)}) async-start(), calls=%async_computation.4 | async-start | bytes 5308416 | tf_op jit(solution)/shard_map/all_gather | solution.py:623
  48.7 5.0 %collective-permute-start.6 = (bf16[96,768]{1,0:T(8,128)(2,1)S(1)}, bf16[96,768]{1,0:T(8,128)(2,1)S(1)}, u32[]{:S(2)}, u32[]{:S(2)}) collective-permute-start(bf16[96,768]{1,0:T(8,128)(2,1)S(1)} %copy-done.30), channel_id=1, source_target_pairs={{0,1},{1,2},{2,3},{3,0},{4,5},{5,6},{6,7},{7,4},{8,9},{9,10},{10,1... | collective-permute-start | bytes 442376 | tf_op jit(solution)/shard_map/ppermute | solution.py:611
  48.8 12.5 %collective-permute-start.7 = (bf16[96,768]{1,0:T(8,128)(2,1)S(1)}, bf16[96,768]{1,0:T(8,128)(2,1)S(1)}, u32[]{:S(2)}, u32[]{:S(2)}) collective-permute-start(bf16[96,768]{1,0:T(8,128)(2,1)S(1)} %copy-done.30), channel_id=1, source_target_pairs={{0,2},{1,3},{2,0},{3,1},{4,6},{5,7},{6,4},{7,5},{8,10},{9,11},{10,... | collective-permute-start | bytes 442376 | tf_op jit(solution)/shard_map/ppermute | solution.py:611
  50.4 13.8 %collective-permute-start.8 = (bf16[96,768]{1,0:T(8,128)(2,1)S(1)}, bf16[96,768]{1,0:T(8,128)(2,1)S(1)}, u32[]{:S(2)}, u32[]{:S(2)}) collective-permute-start(bf16[96,768]{1,0:T(8,128)(2,1)S(1)} %copy-done.30), channel_id=1, source_target_pairs={{0,3},{1,0},{2,1},{3,2},{4,7},{5,4},{6,5},{7,6},{8,11},{9,8},{10,9... | collective-permute-start | bytes 442376 | tf_op jit(solution)/shard_map/ppermute | solution.py:611
  53.7 16.9 %copy-start.7 = (bf16[2,1,512,768]{3,2,1,0:T(8,128)(2,1)S(1)}, bf16[2,1,512,768]{3,2,1,0:T(8,128)(2,1)}, u32[]{:S(2)}) copy-start(bf16[2,1,512,768]{3,2,1,0:T(8,128)(2,1)} %param.21) | copy-start | bytes 4718596
  65.0 168.9 %reduce-scatter.3.cloned.1.call-start = ((), (), s32[]{:S(2)}) async-start(), calls=%async_computation.5 | async-start | bytes 5308416 | tf_op jit(solution)/shard_map/reduce_scatter | solution.py:627
  70.5 4.5 %slice-start = ((s8[4521984]{0:T(1024)(128)(4,1)}), s8[4194304]{0:T(1024)(128)(4,1)S(1)}, s32[]{:S(2)}) async-start(s8[4521984]{0:T(1024)(128)(4,1)} %bitcast.83), calls=%async_computation.7 | async-start | bytes 8388608
  75.1 4.3 %copy-start.1 = (bf16[512,1536]{1,0:T(8,128)(2,1)}, bf16[512,1536]{1,0:T(8,128)(2,1)S(1)}, u32[]{:S(2)}) copy-start(bf16[512,1536]{1,0:T(8,128)(2,1)S(1)} %fusion.23.pq_ref.pk_ref) | copy-start | bytes 4718596
  126.7 4.4 %copy-start.31 = (bf16[768,3840]{1,0:T(8,128)(2,1)S(1)}, bf16[768,3840]{1,0:T(8,128)(2,1)}, u32[]{:S(2)}) copy-start(bf16[768,3840]{1,0:T(8,128)(2,1)} %all-gather.6.cloned.1.call-done.up_ref) | copy-start | bytes 17694724
  175.3 109.5 %reduce-scatter.5.cloned.1.call-start = ((), (), s32[]{:S(2)}) async-start(), calls=%async_computation.6 | async-start | bytes 3686400 | tf_op jit(solution)/shard_map/reduce_scatter | solution.py:680
  175.4 22.4 %copy-start.5 = (f32[1024,768]{1,0:T(8,128)S(1)}, f32[1024,768]{1,0:T(8,128)}, u32[]{:S(2)}) copy-start(f32[1024,768]{1,0:T(8,128)} %copy-done.4) | copy-start | bytes 9437188
  205.1 5.0 %copy-start.12 = (f32[1024,768]{1,0:T(8,128)}, f32[1024,768]{1,0:T(8,128)S(1)}, u32[]{:S(2)}) copy-start(f32[1024,768]{1,0:T(8,128)S(1)} %get-tuple-element.175) | copy-start | bytes 9437188
  209.7 24.2 %collective-permute-start.9 = (bf16[2,2,96,3840]{3,2,1,0:T(8,128)(2,1)S(1)}, bf16[2,2,96,3840]{3,2,1,0:T(8,128)(2,1)}, u32[]{:S(2)}, u32[]{:S(2)}) collective-permute-start(bf16[2,2,96,3840]{3,2,1,0:T(8,128)(2,1)S(1)} %get-tuple-element.179), channel_id=1, source_target_pairs={{0,4},{4,0},{8,12},{12,8},{16,20},{20,16},{24,28},{28,24},{1,5},{5... | collective-permute-start | bytes 8847368 | tf_op jit(solution)/shard_map/ppermute | solution.py:648
  241.3 23.6 %collective-permute-start.10 = (bf16[96,768]{1,0:T(8,128)(2,1)S(1)}, bf16[96,768]{1,0:T(8,128)(2,1)S(1)}, u32[]{:S(2)}, u32[]{:S(2)}) collective-permute-start(bf16[96,768]{1,0:T(8,128)(2,1)S(1)} %get-tuple-element.188), channel_id=1, source_target_pairs={{0,1},{1,2},{2,3},{3,0},{4,5},{5,6},{6,7},{7,4},{8,9},{9,10},{10,1... | collective-permute-start | bytes 442376 | tf_op jit(solution)/shard_map/ppermute | solution.py:611
  242.5 22.4 %collective-permute-start.11 = (bf16[96,768]{1,0:T(8,128)(2,1)S(1)}, bf16[96,768]{1,0:T(8,128)(2,1)S(1)}, u32[]{:S(2)}, u32[]{:S(2)}) collective-permute-start(bf16[96,768]{1,0:T(8,128)(2,1)S(1)} %get-tuple-element.187), channel_id=1, source_target_pairs={{0,2},{1,3},{2,0},{3,1},{4,6},{5,7},{6,4},{7,5},{8,10},{9,11},{10,... | collective-permute-start | bytes 442376 | tf_op jit(solution)/shard_map/ppermute | solution.py:611
  243.4 21.5 %collective-permute-start.12 = (bf16[96,768]{1,0:T(8,128)(2,1)S(1)}, bf16[96,768]{1,0:T(8,128)(2,1)S(1)}, u32[]{:S(2)}, u32[]{:S(2)}) collective-permute-start(bf16[96,768]{1,0:T(8,128)(2,1)S(1)} %get-tuple-element.186), channel_id=1, source_target_pairs={{0,3},{1,0},{2,1},{3,2},{4,7},{5,4},{6,5},{7,6},{8,11},{9,8},{10,9... | collective-permute-start | bytes 442376 | tf_op jit(solution)/shard_map/ppermute | solution.py:611
  264.8 13.5 %copy-start.24 = (bf16[96,768]{1,0:T(8,128)(2,1)}, bf16[96,768]{1,0:T(8,128)(2,1)S(1)}, u32[]{:S(2)}) copy-start(bf16[96,768]{1,0:T(8,128)(2,1)S(1)} %collective-permute-done.10) | copy-start | bytes 442372
  264.8 13.5 %copy-start.26 = (bf16[96,768]{1,0:T(8,128)(2,1)}, bf16[96,768]{1,0:T(8,128)(2,1)S(1)}, u32[]{:S(2)}) copy-start(bf16[96,768]{1,0:T(8,128)(2,1)S(1)} %collective-permute-done.11) | copy-start | bytes 442372
  264.9 13.5 %copy-start.28 = (bf16[96,768]{1,0:T(8,128)(2,1)}, bf16[96,768]{1,0:T(8,128)(2,1)S(1)}, u32[]{:S(2)}) copy-start(bf16[96,768]{1,0:T(8,128)(2,1)S(1)} %collective-permute-done.12) | copy-start | bytes 442372
  278.4 6.5 %copy-start.19 = (bf16[4,96,1536]{2,1,0:T(8,128)(2,1)S(1)}, bf16[4,96,1536]{2,1,0:T(8,128)(2,1)}, u32[]{:S(2)}) copy-start(bf16[4,96,1536]{2,1,0:T(8,128)(2,1)} %get-tuple-element.90) | copy-start | bytes 3538948
  278.4 3.6 %collective-permute-start.14 = (bf16[4,96,1408]{2,1,0:T(8,128)(2,1)}, bf16[4,96,1408]{2,1,0:T(8,128)(2,1)S(1)}, u32[]{:S(2)}, u32[]{:S(2)}) collective-permute-start(bf16[4,96,1408]{2,1,0:T(8,128)(2,1)} %get-tuple-element.93), channel_id=1, source_target_pairs={{0,4},{4,0},{8,12},{12,8},{16,20},{20,16},{24,28},{28,24},{1,5},{5... | collective-permute-start | bytes 3244040 | tf_op jit(solution)/shard_map/ppermute | solution.py:648
  279.4 5.4 %collective-permute-start.13 = (bf16[4,96,1536]{2,1,0:T(8,128)(2,1)}, bf16[4,96,1536]{2,1,0:T(8,128)(2,1)S(1)}, u32[]{:S(2)}, u32[]{:S(2)}) collective-permute-start(bf16[4,96,1536]{2,1,0:T(8,128)(2,1)} %get-tuple-element.91), channel_id=1, source_target_pairs={{0,4},{4,0},{8,12},{12,8},{16,20},{20,16},{24,28},{28,24},{1,5},{5... | collective-permute-start | bytes 3538952 | tf_op jit(solution)/shard_map/ppermute | solution.py:648
  284.8 5.2 %copy-start.8 = (bf16[1024,768]{1,0:T(8,128)(2,1)S(1)}, bf16[1024,768]{1,0:T(8,128)(2,1)}, u32[]{:S(2)}) copy-start(bf16[1024,768]{1,0:T(8,128)(2,1)} %get-tuple-element.96.gq_ref) | copy-start | bytes 4718596
  284.8 5.2 %copy-start.9 = (bf16[1024,768]{1,0:T(8,128)(2,1)S(1)}, bf16[1024,768]{1,0:T(8,128)(2,1)}, u32[]{:S(2)}) copy-start(bf16[1024,768]{1,0:T(8,128)(2,1)} %get-tuple-element.97.gk_ref) | copy-start | bytes 4718596
  284.8 5.1 %copy-start.10 = (bf16[1024,768]{1,0:T(8,128)(2,1)S(1)}, bf16[1024,768]{1,0:T(8,128)(2,1)}, u32[]{:S(2)}) copy-start(bf16[1024,768]{1,0:T(8,128)(2,1)} %get-tuple-element.98.gv_ref) | copy-start | bytes 4718596
  285.2 13.6 %collective-permute-start.16 = (bf16[2,96,1408]{2,1,0:T(8,128)(2,1)S(1)}, bf16[2,96,1408]{2,1,0:T(8,128)(2,1)S(1)}, u32[]{:S(2)}, u32[]{:S(2)}) collective-permute-start(bf16[2,96,1408]{2,1,0:T(8,128)(2,1)S(1)} %dynamic-slice_bitcast_fusion.3), channel_id=1, source_target_pairs={{0,8},{4,12},{8,0},{12,4},{16,24},{20,28},{24,16},{28,20},{1,9},{5... | collective-permute-start | bytes 1622024 | tf_op jit(solution)/shard_map/ppermute | solution.py:648
  286.5 14.3 %collective-permute-start.15 = (bf16[2,96,1536]{2,1,0:T(8,128)(2,1)S(1)}, bf16[2,96,1536]{2,1,0:T(8,128)(2,1)S(1)}, u32[]{:S(2)}, u32[]{:S(2)}) collective-permute-start(bf16[2,96,1536]{2,1,0:T(8,128)(2,1)S(1)} %dynamic-slice_bitcast_fusion.2), channel_id=1, source_target_pairs={{0,16},{4,20},{8,24},{12,28},{16,0},{20,4},{24,8},{28,12},{1,17},{... | collective-permute-start | bytes 1769480 | tf_op jit(solution)/shard_map/ppermute | solution.py:648
  286.8 14.1 %collective-permute-start.17 = (bf16[24,3840]{1,0:T(8,128)(2,1)S(1)}, bf16[24,3840]{1,0:T(8,128)(2,1)S(1)}, u32[]{:S(2)}, u32[]{:S(2)}) collective-permute-start(bf16[24,3840]{1,0:T(8,128)(2,1)S(1)} %get-tuple-element.184), channel_id=1, source_target_pairs={{0,1},{1,2},{2,3},{3,0},{4,5},{5,6},{6,7},{7,4},{8,9},{9,10},{10,1... | collective-permute-start | bytes 552968 | tf_op jit(solution)/shard_map/ppermute | solution.py:611
  287.4 14.9 %collective-permute-start.18 = (bf16[24,3840]{1,0:T(8,128)(2,1)S(1)}, bf16[24,3840]{1,0:T(8,128)(2,1)S(1)}, u32[]{:S(2)}, u32[]{:S(2)}) collective-permute-start(bf16[24,3840]{1,0:T(8,128)(2,1)S(1)} %get-tuple-element.183), channel_id=1, source_target_pairs={{0,2},{1,3},{2,0},{3,1},{4,6},{5,7},{6,4},{7,5},{8,10},{9,11},{10,... | collective-permute-start | bytes 552968 | tf_op jit(solution)/shard_map/ppermute | solution.py:611
  290.0 15.9 %collective-permute-start.19 = (bf16[24,3840]{1,0:T(8,128)(2,1)S(1)}, bf16[24,3840]{1,0:T(8,128)(2,1)S(1)}, u32[]{:S(2)}, u32[]{:S(2)}) collective-permute-start(bf16[24,3840]{1,0:T(8,128)(2,1)S(1)} %get-tuple-element.182), channel_id=1, source_target_pairs={{0,3},{1,0},{2,1},{3,2},{4,7},{5,4},{6,5},{7,6},{8,11},{9,8},{10,9... | collective-permute-start | bytes 552968 | tf_op jit(solution)/shard_map/ppermute | solution.py:611
  297.7 9.5 %copy-start.22 = (bf16[96,768]{1,0:T(8,128)(2,1)S(1)}, bf16[96,768]{1,0:T(8,128)(2,1)}, u32[]{:S(2)}) copy-start(bf16[96,768]{1,0:T(8,128)(2,1)} %get-tuple-element.107) | copy-start | bytes 442372
  297.7 9.5 %copy-start.25 = (bf16[96,768]{1,0:T(8,128)(2,1)S(1)}, bf16[96,768]{1,0:T(8,128)(2,1)}, u32[]{:S(2)}) copy-start(bf16[96,768]{1,0:T(8,128)(2,1)} %copy-done.24) | copy-start | bytes 442372
  297.7 9.5 %copy-start.27 = (bf16[96,768]{1,0:T(8,128)(2,1)S(1)}, bf16[96,768]{1,0:T(8,128)(2,1)}, u32[]{:S(2)}) copy-start(bf16[96,768]{1,0:T(8,128)(2,1)} %copy-done.26) | copy-start | bytes 442372
  297.7 9.5 %copy-start.29 = (bf16[96,768]{1,0:T(8,128)(2,1)S(1)}, bf16[96,768]{1,0:T(8,128)(2,1)}, u32[]{:S(2)}) copy-start(bf16[96,768]{1,0:T(8,128)(2,1)} %copy-done.28) | copy-start | bytes 442372
  306.0 7.0 %collective-permute-start.21 = (bf16[96,1408]{1,0:T(8,128)(2,1)S(1)}, bf16[96,1408]{1,0:T(8,128)(2,1)S(1)}, u32[]{:S(2)}, u32[]{:S(2)}) collective-permute-start(bf16[96,1408]{1,0:T(8,128)(2,1)S(1)} %dynamic-slice_bitcast_fusion.5), channel_id=1, source_target_pairs={{0,16},{4,20},{8,24},{12,28},{16,0},{20,4},{24,8},{28,12},{1,17},{... | collective-permute-start | bytes 811016 | tf_op jit(solution)/shard_map/ppermute | solution.py:648
  308.0 7.1 %collective-permute-start.20 = (bf16[96,1536]{1,0:T(8,128)(2,1)S(1)}, bf16[96,1536]{1,0:T(8,128)(2,1)S(1)}, u32[]{:S(2)}, u32[]{:S(2)}) collective-permute-start(bf16[96,1536]{1,0:T(8,128)(2,1)S(1)} %dynamic-slice_bitcast_fusion.4), channel_id=1, source_target_pairs={{0,8},{4,12},{8,0},{12,4},{16,24},{20,28},{24,16},{28,20},{1,9},{5... | collective-permute-start | bytes 884744 | tf_op jit(solution)/shard_map/ppermute | solution.py:648
  315.3 4.0 %collective-permute-start.22 = (bf16[24,2944]{1,0:T(8,128)(2,1)S(1)}, bf16[24,2944]{1,0:T(8,128)(2,1)S(1)}, u32[]{:S(2)}, u32[]{:S(2)}) collective-permute-start(bf16[24,2944]{1,0:T(8,128)(2,1)S(1)} %get-tuple-element.190), channel_id=1, source_target_pairs={{0,1},{1,2},{2,3},{3,0},{4,5},{5,6},{6,7},{7,4},{8,9},{9,10},{10,1... | collective-permute-start | bytes 423944 | tf_op jit(solution)/shard_map/ppermute | solution.py:611
  315.4 6.7 %collective-permute-start.23 = (bf16[24,2944]{1,0:T(8,128)(2,1)S(1)}, bf16[24,2944]{1,0:T(8,128)(2,1)S(1)}, u32[]{:S(2)}, u32[]{:S(2)}) collective-permute-start(bf16[24,2944]{1,0:T(8,128)(2,1)S(1)} %get-tuple-element.191), channel_id=1, source_target_pairs={{0,2},{1,3},{2,0},{3,1},{4,6},{5,7},{6,4},{7,5},{8,10},{9,11},{10,... | collective-permute-start | bytes 423944 | tf_op jit(solution)/shard_map/ppermute | solution.py:611
  315.4 13.9 %collective-permute-start.24 = (bf16[24,2944]{1,0:T(8,128)(2,1)S(1)}, bf16[24,2944]{1,0:T(8,128)(2,1)S(1)}, u32[]{:S(2)}, u32[]{:S(2)}) collective-permute-start(bf16[24,2944]{1,0:T(8,128)(2,1)S(1)} %get-tuple-element.192), channel_id=1, source_target_pairs={{0,3},{1,0},{2,1},{3,2},{4,7},{5,4},{6,5},{7,6},{8,11},{9,8},{10,9... | collective-permute-start | bytes 423944 | tf_op jit(solution)/shard_map/ppermute | solution.py:611
  (18 other events, 41.1 us)
Sparse Core Ops, SparseCore 0:
  28.8 38.5 all-gather.3
  69.8 43.8 all-gather.5
  115.6 38.9 all-gather.7
  175.5 53.4 reduce-scatter.2
  238.2 41.7 reduce-scatter.4

commit v5 on v4

--- a/solution.py
+++ b/solution.py
@@ -606,6 +606,10 @@
     return grad_in, column_sums(grad * normed), column_sums(grad)
 
 
+def far_first(size):
+    return sorted(range(size), key=lambda shift: -min(shift, size - shift))
+
+
 def narrow_shifts(block, shift):
     size = lax.axis_size("narrow")
     return lax.ppermute(block, "narrow", [(i, (i + shift) % size) for i in range(size)])
@@ -616,7 +620,7 @@
     me = lax.axis_index("narrow")
     rows, cols = shard.shape
     together = jnp.zeros((size * rows, cols), shard.dtype)
-    for shift in range(size):
+    for shift in far_first(size):
         block = narrow_shifts(shard, shift) if shift else shard
         owner = lax.rem(me - shift + size, size)
         together = lax.dynamic_update_slice(together, block, (owner * rows, 0))
@@ -632,7 +636,7 @@
     me = lax.axis_index("narrow")
     rows = part.shape[-2] // size
     pieces = []
-    for shift in range(size):
+    for shift in far_first(size):
         target = lax.rem(me + shift, size)
         block = lax.dynamic_slice_in_dim(part, target * rows, rows, part.ndim - 2)
         pieces.append(narrow_shifts(block, shift) if shift else block)

time: 344 us -> 345 us (level)
  transfers between devices with their start and end apart: 30 -> 30, of which waited for: 21 -> 20; matrix products, arithmetic and copies ran while one was open for 18% -> 18% of each run, Pallas kernels for 34% -> 34%
where the time goes in v5:
time: 345 us; the launch traced here: 339 us
  Pallas kernels  116 us (34%)
  waiting for transfers between devices  79.4 us (23%)
  matrix products  54.2 us (16%)
  local copies, waits for them, and re-layouts  30.7 us (9%)
  starting transfers between devices  22.6 us (7%)
  other arithmetic  21.6 us (6%)
  between operations  14.9 us (4%)
    ppermute x18, waiting for transfers between devices, narrow_shifts(): lax.ppermute(block, 'narrow', [(i, (i + shift) % size) for i in range(siz...  53.2 us
    pallas_call x1, Pallas kernels, attend(): pl.pallas_call(attend_kernel, grid_spec=pltpu.PrefetchScalarGridSpec(num_...  39.9 us
    pallas_call x2, Pallas kernels, attend_back(): pl.pallas_call(functools.partial(attend_back_kernel, len(earlier)), grid=...  39.9 us
    dot_general x4, matrix products, dot_nn(): lax.dot_general(left, right, (((1,), (0,)), ((), ())), preferred_element_...  30.4 us
    pallas_call x1, Pallas kernels, feed_back(): pl.pallas_call(feed_back_kernel, grid=(blocks,), in_specs=[whole((tokens,...  22.4 us
    unnamed x83, local copies, waits for them, and re-layouts  18.4 us
    ppermute x18, starting transfers between devices, narrow_shifts(): lax.ppermute(block, 'narrow', [(i, (i + shift) % size) for i in range(siz...  17.7 us
    all_gather x3, waiting for transfers between devices, gather_rows(): return lax.all_gather(together, 'wide', axis=0, tiled=True)  13.9 us
  transfers between devices with their start and end apart: 30, of which 20 were waited for; matrix products, arithmetic and copies ran while one was open for 18% of the time, Pallas kernels for 34%

profile of v5, /device:TPU:9, one launch (start us, length us, event | category | flops | bytes accessed | tf_op | source)
XLA Modules:
  0.0 339.1 jit_solution(12725217498552506846)
XLA Ops:
  12.2 2.4 collective-permute-start
  14.5 1.5 collective-permute-start.2
  16.0 5.4 %collective-permute-done = bf16[24,2944]{1,0:T(8,128)(2,1)S(1)} collective-permute-done((bf16[24,2944]{1,0:T(8,128)(2,1)S(1)}, bf16[24,2944]{1,0:T(8,128)(2,1)S(1)}, u32[]{:S(2)}, u32[]{:S(2)}) %collective-permute-start) | collective-permute-done | bytes 141344 | tf_op jit(solution)/shard_map/ppermute | solution.py:615
  21.5 5.5 %collective-permute-done.1 = bf16[24,2944]{1,0:T(8,128)(2,1)S(1)} collective-permute-done((bf16[24,2944]{1,0:T(8,128)(2,1)S(1)}, bf16[24,2944]{1,0:T(8,128)(2,1)S(1)}, u32[]{:S(2)}, u32[]{:S(2)}) %collective-permute-start.1) | collective-permute-done | bytes 141344 | tf_op jit(solution)/shard_map/ppermute | solution.py:615
  29.7 2.3 collective-permute-start.4
  33.1 3.3 collective-permute-done.3
  36.4 5.0 %collective-permute-done.4 = bf16[24,3840]{1,0:T(8,128)(2,1)S(1)} collective-permute-done((bf16[24,3840]{1,0:T(8,128)(2,1)S(1)}, bf16[24,3840]{1,0:T(8,128)(2,1)S(1)}, u32[]{:S(2)}, u32[]{:S(2)}) %collective-permute-start.4) | collective-permute-done | bytes 184352 | tf_op jit(solution)/shard_map/ppermute | solution.py:615
  41.4 7.3 %collective-permute-done.5 = bf16[24,3840]{1,0:T(8,128)(2,1)S(1)} collective-permute-done((bf16[24,3840]{1,0:T(8,128)(2,1)S(1)}, bf16[24,3840]{1,0:T(8,128)(2,1)S(1)}, u32[]{:S(2)}, u32[]{:S(2)}) %collective-permute-start.5) | collective-permute-done | bytes 184352 | tf_op jit(solution)/shard_map/ppermute | solution.py:615
  49.9 1.5 collective-permute-start.8
  51.3 5.3 %collective-permute-done.6 = bf16[96,768]{1,0:T(8,128)(2,1)S(1)} collective-permute-done((bf16[96,768]{1,0:T(8,128)(2,1)S(1)}, bf16[96,768]{1,0:T(8,128)(2,1)S(1)}, u32[]{:S(2)}, u32[]{:S(2)}) %collective-permute-start.6) | collective-permute-done | bytes 147488 | tf_op jit(solution)/shard_map/ppermute | solution.py:615
  56.6 6.1 %collective-permute-done.7 = bf16[96,768]{1,0:T(8,128)(2,1)S(1)} collective-permute-done((bf16[96,768]{1,0:T(8,128)(2,1)S(1)}, bf16[96,768]{1,0:T(8,128)(2,1)S(1)}, u32[]{:S(2)}, u32[]{:S(2)}) %collective-permute-start.7) | collective-permute-done | bytes 147488 | tf_op jit(solution)/shard_map/ppermute | solution.py:615
  63.9 3.5 %all-gather.4.cloned.1.call-done.rel_ref.wq_ref.wk_ref = bf16[768,2944]{1,0:T(8,128)(2,1)} async-done(((bf16[96,2944]{1,0:T(8,128)(2,1)}), bf16[768,2944]{1,0:T(8,128)(2,1)}) %all-gather.4.cloned.1.call-update) | async-done | bytes 4522000 | tf_op jit(solution)/shard_map/all_gather | solution.py:627
  69.3 1.3 slice_reduce_fusion.1
  71.4 3.7 %fusion.23.pq_ref.pk_ref = bf16[512,1536]{1,0:T(8,128)(2,1)S(1)} fusion(bf16[768,2944]{1,0:T(8,128)(2,1)} %all-gather.4.cloned.1.call-done.rel_ref.wq_ref.wk_ref, f32[1536]{0:T(1024)S(1)} %add.286), kind=kOutput, calls=%fused_computation.45 | convolution fusion | flops 1209532416 | bytes 4724736 | tf_op jit(solution)/shard_map/dot_general | solution.py:40
  75.2 4.3 %fusion.5.q_ref.k_ref.v_ref = bf16[1024,2304]{1,0:T(8,128)(2,1)S(1)} fusion(bf16[1024,768]{1,0:T(8,128)(2,1)S(1)} %bitcast.97, f32[2304]{0:T(1024)S(1)} %add.283, bf16[768,2944]{1,0:T(8,128)(2,1)S(1)} %bitcast.84), kind=kOutput, calls=%fused_computation.11 | convolution fusion | flops 3628597248 | bytes 9842688 | tf_op jit(solution)/shard_map/dot_general | solution.py:36
  79.4 39.9 %attend.1 = (bf16[1024,768]{1,0:T(8,128)(2,1)S(1)}, f32[1024,768]{1,0:T(8,128)S(1)}, bf16[2,12,512,512]{3,2,1,0:T(8,128)(2,1)}, f32[2,12,512,128]{3,2,1,0:T(8,128)}) custom-call(s32[2]{0:T(128)S(1)} %bitcast.82, bf16[1024,2304]{1,0:T(8,128)(2,1)S(1)} %fusion.5.q_ref.k_ref.v_ref, bf16[1024,2304]{1,0:T(8,128)(2,1)S(1)} %fusion.5.q_ref.k_ref.v_ref, ...), custom_call_target="tpu_custom_call" | custom-call | flops 12884901888 | bytes 20971520 | tf_op jit(solution)/shard_map/attend/pallas_call | solution.py:251
  119.4 2.1 copy-done
  121.5 1.7 copy-done.2
  123.2 3.5 %fusion.52 = (f32[1024]{0:T(1024)S(1)}, f32[1024,768]{1,0:T(8,128)S(1)}) fusion(f32[768]{0:T(1024)S(1)} %get-tuple-element.162, bf16[1024,768]{1,0:T(8,128)(2,1)S(1)} %get-tuple-element.65, bf16[768,3840]{1,0:T(8,128)(2,1)} %all-gather.6.cloned.1.call-done.up_ref, bf16[1024,768]{1,0:T(8,128)(2,1)} %bitcast.95), kind=kOutput, calls=%fused_computation.168 | convolution fusion | flops 1211104256 | bytes 7478272 | tf_op jit(solution)/shard_map/dot_general | solution.py:36
  131.1 13.1 %fusion.4 = (bf16[1024,3072]{1,0:T(8,128)(2,1)}, bf16[1024,3072]{1,0:T(8,128)(2,1)}) fusion(f32[3072]{0:T(1024)S(1)} %add.297, bf16[1024,768]{1,0:T(8,128)(2,1)S(1)} %fusion.24.hidden_ref, bf16[768,3840]{1,0:T(8,128)(2,1)S(1)} %copy-done.31), kind=kOutput, calls=%fused_computation.5 | convolution fusion | flops 4869586944 | bytes 18886656 | tf_op jit(solution)/shard_map/dot_general | solution.py:36
  144.2 10.4 %all-gather.8.cloned.1.call-done.down_ref = bf16[3072,768]{1,0:T(8,128)(2,1)} async-done(((bf16[384,768]{1,0:T(8,128)(2,1)}), bf16[3072,768]{1,0:T(8,128)(2,1)}) %all-gather.8.cloned.1.call-update) | async-done | bytes 4718608 | tf_op jit(solution)/shard_map/all_gather | solution.py:627
  154.6 9.5 %fusion.53 = (f32[1024]{0:T(1024)S(1)}, f32[1024,768]{1,0:T(8,128)S(1)}) fusion(f32[768]{0:T(1024)S(1)} %get-tuple-element.159, bf16[1024,3072]{1,0:T(8,128)(2,1)} %get-tuple-element.178, bf16[3072,768]{1,0:T(8,128)(2,1)} %all-gather.8.cloned.1.call-done.down_ref, f32[768]{0:T(1024)S(1)} %get-tuple-element.160, f32[768]{0:T(1024)S(1)} %get-tuple-element.161, ...), kind=kOutput, calls=%fused_computation.169 | convolution fusion | flops 4837342208 | bytes 17323008 | tf_op jit(solution)/shard_map/dot_general | solution.py:36
  168.4 7.0 %convolution_convert_fusion = bf16[3072,768]{1,0:T(8,128)(2,1)} fusion(bf16[1024,3072]{1,0:T(8,128)(2,1)S(1)} %bitcast.104, bf16[1024,768]{1,0:T(8,128)(2,1)S(1)} %get-tuple-element.173.grad_ref), kind=kOutput, calls=%fused_computation.10 | convolution fusion | flops 4834197504 | bytes 12582912 | tf_op jit(solution)/shard_map/dot_general | solution.py:40
  175.5 22.4 %feed_back.1 = (f32[1024,768]{1,0:T(8,128)}, bf16[768,3840]{1,0:T(8,128)(2,1)}, f32[8,3072]{1,0:T(8,128)}) custom-call(bf16[1024,768]{1,0:T(8,128)(2,1)} %copy-done.17, bf16[1024,768]{1,0:T(8,128)(2,1)} %copy-done.16, bf16[1024,3072]{1,0:T(8,128)(2,1)} %get-tuple-element.177.slope_ref, bf16[3072,768]{1,0:T(8,128)(2,1)} %all-gather.8.cloned.1.call-done.down_ref, ...), custom_call_target="tpu_custom_call" | custom-call | flops 14495514624 | bytes 31457280 | tf_op jit(solution)/shard_map/feed_back/pallas_call | solution.py:559
  197.9 6.2 %multiply_reduce_fusion = (f32[768]{0:T(1024)S(1)}, f32[1024]{0:T(1024)S(1)}, f32[1024]{0:T(1024)S(1)}, f32[768]{0:T(1024)S(1)}, f32[1024,768]{1,0:T(8,128)S(1)}, /*index=5*/bf16[1024,768]{1,0:T(8,128)(2,1)}) fusion(f32[1024,768]{1,0:T(8,128)S(1)} %copy-done.5, f32[1024]{0:T(1024)S(1)} %add_rsqrt_fusion.1, f32[1024]{0:T(1024)S(1)} %broadcast_multiply_fusion.4, ...), kind=kLoop, calls=%fused_computation.33 | loop fusion | flops 16511488 | bytes 15776768 | tf_op jit(solution)/shard_map/reduce_sum | solution.py:596
  205.1 2.8 copy-done.11
  207.9 1.4 fusion.31
  210.2 3.9 %convolution_convert_fusion.1.gc_ref = bf16[1024,768]{1,0:T(8,128)(2,1)} fusion(bf16[768,3840]{1,0:T(8,128)(2,1)} %all-gather.6.cloned.1.call-done.up_ref, f32[1024,768]{1,0:T(8,128)S(1)} %get-tuple-element.175), kind=kOutput, calls=%fused_computation.56 | convolution fusion | flops 1209532416 | bytes 5898240 | tf_op jit(solution)/shard_map/dot_general | solution.py:32
  214.0 19.9 %attend_back.2 = (bf16[1024,768]{1,0:T(8,128)(2,1)}, bf16[1024,768]{1,0:T(8,128)(2,1)}, bf16[1024,768]{1,0:T(8,128)(2,1)}, f32[768,512]{1,0:T(8,128)}, f32[768,512]{1,0:T(8,128)}) custom-call(bf16[1024,2304]{1,0:T(8,128)(2,1)} %copy-done, bf16[1024,2304]{1,0:T(8,128)(2,1)} %copy-done, bf16[1024,2304]{1,0:T(8,128)(2,1)} %copy-done, ...), custom_call_target="tpu_custom_call" | custom-call | flops 12884901888 | bytes 12582912 | tf_op jit(solution)/shard_map/attend_back/pallas_call | solution.py:423
  234.0 4.1 %add_convert_fusion.1 = bf16[2,2,96,3840]{3,2,1,0:T(8,128)(2,1)} fusion(bf16[2,2,96,3840]{3,2,1,0:T(8,128)(2,1)} %collective-permute-done.9, bf16[2,2,96,3840]{3,2,1,0:T(8,128)(2,1)S(1)} %get-tuple-element.88), kind=kLoop, calls=%fused_computation.9 | loop fusion | flops 5898240 | bytes 8847360 | tf_op jit(solution)/shard_map/convert_element_type | solution.py:669
  241.3 2.1 collective-permute-start.10
  243.4 1.5 collective-permute-start.12
  244.9 20.0 %attend_back.3 = (bf16[1024,768]{1,0:T(8,128)(2,1)}, bf16[1024,768]{1,0:T(8,128)(2,1)}, bf16[1024,768]{1,0:T(8,128)(2,1)}, f32[768,512]{1,0:T(8,128)}, f32[768,512]{1,0:T(8,128)}) custom-call(bf16[1024,2304]{1,0:T(8,128)(2,1)} %copy-done, bf16[1024,2304]{1,0:T(8,128)(2,1)} %copy-done, ...), custom_call_target="tpu_custom_call", output_to_operand_aliasing={{0}: (9, {}), {1}: (10, {}), {2}: (11, {}), {3}: (12, {}), ... | custom-call | flops 12884901888 | bytes 12582912 | tf_op jit(solution)/shard_map/attend_back/pallas_call | solution.py:423
  264.9 13.5 %weigh.1 = (bf16[4,96,1536]{2,1,0:T(8,128)(2,1)}, bf16[4,96,1536]{2,1,0:T(8,128)(2,1)}, bf16[4,96,1408]{2,1,0:T(8,128)(2,1)}, bf16[4,96,1408]{2,1,0:T(8,128)(2,1)}) custom-call(s32[1]{0:T(128)} %bitcast.9.low_ref, bf16[1024,768]{1,0:T(8,128)(2,1)} %bitcast.96, bf16[1024,768]{1,0:T(8,128)(2,1)} %get-tuple-element.96.gq_ref, ...), custom_call_target="tpu_custom_call" | custom-call | flops 6039797760 | bytes 20971520 | tf_op jit(solution)/shard_map/weigh/pallas_call | solution.py:506
  279.6 2.5 collective-permute-done.14
  283.0 1.8 add_convert_fusion.4
  287.9 2.6 collective-permute-start.18
  290.5 7.7 %fusion.26 = f32[1024,768]{1,0:T(8,128)} fusion(f32[1024,768]{1,0:T(8,128)} %copy-done.12, bf16[768,2944]{1,0:T(8,128)(2,1)} %all-gather.4.cloned.1.call-done.rel_ref.wq_ref.wk_ref, bf16[1024,768]{1,0:T(8,128)(2,1)S(1)} %copy-done.10, bf16[1024,768]{1,0:T(8,128)(2,1)S(1)} %copy-done.9, bf16[1024,768]{1,0:T(8,128)(2,1)S(1)} %copy-done.8), kind=kOutput, calls=%fused_computation.55 | convolution fusion | flops 3638820864 | bytes 14548992 | tf_op jit(solution)/shard_map/dot_general | solution.py:32
  299.0 1.9 collective-permute-done.15
  301.0 1.9 collective-permute-done.18
  302.9 3.4 %collective-permute-done.19 = bf16[24,3840]{1,0:T(8,128)(2,1)S(1)} collective-permute-done((bf16[24,3840]{1,0:T(8,128)(2,1)S(1)}, bf16[24,3840]{1,0:T(8,128)(2,1)S(1)}, u32[]{:S(2)}, u32[]{:S(2)}) %collective-permute-start.19) | collective-permute-done | bytes 184352 | tf_op jit(solution)/shard_map/ppermute | solution.py:615
  306.3 1.4 collective-permute-start.21
  308.8 5.1 %collective-permute-done.21 = bf16[96,1408]{1,0:T(8,128)(2,1)S(1)} collective-permute-done((bf16[96,1408]{1,0:T(8,128)(2,1)S(1)}, bf16[96,1408]{1,0:T(8,128)(2,1)S(1)}, u32[]{:S(2)}, u32[]{:S(2)}) %collective-permute-start.21) | collective-permute-done | bytes 270368 | tf_op jit(solution)/shard_map/ppermute | solution.py:652
  314.0 2.3 collective-permute-done.20
  316.6 1.5 collective-permute-start.24
  319.5 1.9 collective-permute-done.22
  321.4 6.0 %collective-permute-done.23 = bf16[24,2944]{1,0:T(8,128)(2,1)S(1)} collective-permute-done((bf16[24,2944]{1,0:T(8,128)(2,1)S(1)}, bf16[24,2944]{1,0:T(8,128)(2,1)S(1)}, u32[]{:S(2)}, u32[]{:S(2)}) %collective-permute-start.23) | collective-permute-done | bytes 141344 | tf_op jit(solution)/shard_map/ppermute | solution.py:615
  327.4 1.9 collective-permute-done.24
  (200 shorter events, 39.3 us)
Async XLA Ops:
  7.2 42.5 %copy-start.30 = (bf16[96,768]{1,0:T(8,128)(2,1)S(1)}, bf16[96,768]{1,0:T(8,128)(2,1)}, u32[]{:S(2)}) copy-start(bf16[96,768]{1,0:T(8,128)(2,1)} %param.35) | copy-start | bytes 442372
  7.2 60.2 %all-gather.4.cloned.1.call-start = ((), (), s32[]{:S(2)}) async-start(), calls=%async_computation.2 | async-start | bytes 5087232 | tf_op jit(solution)/shard_map/all_gather | solution.py:627
  12.2 9.2 %collective-permute-start = (bf16[24,2944]{1,0:T(8,128)(2,1)S(1)}, bf16[24,2944]{1,0:T(8,128)(2,1)S(1)}, u32[]{:S(2)}, u32[]{:S(2)}) collective-permute-start(bf16[24,2944]{1,0:T(8,128)(2,1)S(1)} %constant_dynamic-update-slice_fusion), channel_id=1, source_target_pairs={{0,2},{1,3},{2,0},{3,1},{4,6},{5,7},{6,4},{7,5},{8,10},{9,11},{10,... | collective-permute-start | bytes 423944 | tf_op jit(solution)/shard_map/ppermute | solution.py:615
  14.5 12.4 %collective-permute-start.1 = (bf16[24,2944]{1,0:T(8,128)(2,1)S(1)}, bf16[24,2944]{1,0:T(8,128)(2,1)S(1)}, u32[]{:S(2)}, u32[]{:S(2)}) collective-permute-start(bf16[24,2944]{1,0:T(8,128)(2,1)S(1)} %constant_dynamic-update-slice_fusion), channel_id=1, source_target_pairs={{0,1},{1,2},{2,3},{3,0},{4,5},{5,6},{6,7},{7,4},{8,9},{9,10},{10,1... | collective-permute-start | bytes 423944 | tf_op jit(solution)/shard_map/ppermute | solution.py:615
  14.5 12.4 %collective-permute-start.2 = (bf16[24,2944]{1,0:T(8,128)(2,1)S(1)}, bf16[24,2944]{1,0:T(8,128)(2,1)S(1)}, u32[]{:S(2)}, u32[]{:S(2)}) collective-permute-start(bf16[24,2944]{1,0:T(8,128)(2,1)S(1)} %constant_dynamic-update-slice_fusion), channel_id=1, source_target_pairs={{0,3},{1,0},{2,1},{3,2},{4,7},{5,4},{6,5},{7,6},{8,11},{9,8},{10,9... | collective-permute-start | bytes 423944 | tf_op jit(solution)/shard_map/ppermute | solution.py:615
  27.9 95.3 %all-gather.6.cloned.1.call-start = ((), (), s32[]{:S(2)}) async-start(), calls=%async_computation.3 | async-start | bytes 6635520 | tf_op jit(solution)/shard_map/all_gather | solution.py:627
  29.6 6.7 %collective-permute-start.3 = (bf16[24,3840]{1,0:T(8,128)(2,1)S(1)}, bf16[24,3840]{1,0:T(8,128)(2,1)S(1)}, u32[]{:S(2)}, u32[]{:S(2)}) collective-permute-start(bf16[24,3840]{1,0:T(8,128)(2,1)S(1)} %constant_dynamic-update-slice_fusion.4), channel_id=1, source_target_pairs={{0,2},{1,3},{2,0},{3,1},{4,6},{5,7},{6,4},{7,5},{8,10},{9,11},{10,... | collective-permute-start | bytes 552968 | tf_op jit(solution)/shard_map/ppermute | solution.py:615
  29.7 11.7 %collective-permute-start.4 = (bf16[24,3840]{1,0:T(8,128)(2,1)S(1)}, bf16[24,3840]{1,0:T(8,128)(2,1)S(1)}, u32[]{:S(2)}, u32[]{:S(2)}) collective-permute-start(bf16[24,3840]{1,0:T(8,128)(2,1)S(1)} %constant_dynamic-update-slice_fusion.4), channel_id=1, source_target_pairs={{0,1},{1,2},{2,3},{3,0},{4,5},{5,6},{6,7},{7,4},{8,9},{9,10},{10,1... | collective-permute-start | bytes 552968 | tf_op jit(solution)/shard_map/ppermute | solution.py:615
  31.9 16.8 %collective-permute-start.5 = (bf16[24,3840]{1,0:T(8,128)(2,1)S(1)}, bf16[24,3840]{1,0:T(8,128)(2,1)S(1)}, u32[]{:S(2)}, u32[]{:S(2)}) collective-permute-start(bf16[24,3840]{1,0:T(8,128)(2,1)S(1)} %constant_dynamic-update-slice_fusion.4), channel_id=1, source_target_pairs={{0,3},{1,0},{2,1},{3,2},{4,7},{5,4},{6,5},{7,6},{8,11},{9,8},{10,9... | collective-permute-start | bytes 552968 | tf_op jit(solution)/shard_map/ppermute | solution.py:615
  49.6 105.0 %all-gather.8.cloned.1.call-start = ((), (), s32[]{:S(2)}) async-start(), calls=%async_computation.4 | async-start | bytes 5308416 | tf_op jit(solution)/shard_map/all_gather | solution.py:627
  49.7 6.9 %collective-permute-start.6 = (bf16[96,768]{1,0:T(8,128)(2,1)S(1)}, bf16[96,768]{1,0:T(8,128)(2,1)S(1)}, u32[]{:S(2)}, u32[]{:S(2)}) collective-permute-start(bf16[96,768]{1,0:T(8,128)(2,1)S(1)} %copy-done.30), channel_id=1, source_target_pairs={{0,2},{1,3},{2,0},{3,1},{4,6},{5,7},{6,4},{7,5},{8,10},{9,11},{10,... | collective-permute-start | bytes 442376 | tf_op jit(solution)/shard_map/ppermute | solution.py:615
  49.8 12.9 %collective-permute-start.7 = (bf16[96,768]{1,0:T(8,128)(2,1)S(1)}, bf16[96,768]{1,0:T(8,128)(2,1)S(1)}, u32[]{:S(2)}, u32[]{:S(2)}) collective-permute-start(bf16[96,768]{1,0:T(8,128)(2,1)S(1)} %copy-done.30), channel_id=1, source_target_pairs={{0,1},{1,2},{2,3},{3,0},{4,5},{5,6},{6,7},{7,4},{8,9},{9,10},{10,1... | collective-permute-start | bytes 442376 | tf_op jit(solution)/shard_map/ppermute | solution.py:615
  49.9 13.1 %collective-permute-start.8 = (bf16[96,768]{1,0:T(8,128)(2,1)S(1)}, bf16[96,768]{1,0:T(8,128)(2,1)S(1)}, u32[]{:S(2)}, u32[]{:S(2)}) collective-permute-start(bf16[96,768]{1,0:T(8,128)(2,1)S(1)} %copy-done.30), channel_id=1, source_target_pairs={{0,3},{1,0},{2,1},{3,2},{4,7},{5,4},{6,5},{7,6},{8,11},{9,8},{10,9... | collective-permute-start | bytes 442376 | tf_op jit(solution)/shard_map/ppermute | solution.py:615
  62.7 7.8 %copy-start.7 = (bf16[2,1,512,768]{3,2,1,0:T(8,128)(2,1)S(1)}, bf16[2,1,512,768]{3,2,1,0:T(8,128)(2,1)}, u32[]{:S(2)}) copy-start(bf16[2,1,512,768]{3,2,1,0:T(8,128)(2,1)} %param.21) | copy-start | bytes 4718596
  63.9 170.1 %reduce-scatter.3.cloned.1.call-start = ((), (), s32[]{:S(2)}) async-start(), calls=%async_computation.5 | async-start | bytes 5308416 | tf_op jit(solution)/shard_map/reduce_scatter | solution.py:631
  70.6 4.5 %slice-start = ((s8[4521984]{0:T(1024)(128)(4,1)}), s8[4194304]{0:T(1024)(128)(4,1)S(1)}, s32[]{:S(2)}) async-start(s8[4521984]{0:T(1024)(128)(4,1)} %bitcast.83), calls=%async_computation.7 | async-start | bytes 8388608
  75.1 4.3 %copy-start.1 = (bf16[512,1536]{1,0:T(8,128)(2,1)}, bf16[512,1536]{1,0:T(8,128)(2,1)S(1)}, u32[]{:S(2)}) copy-start(bf16[512,1536]{1,0:T(8,128)(2,1)S(1)} %fusion.23.pq_ref.pk_ref) | copy-start | bytes 4718596
  126.7 4.4 %copy-start.31 = (bf16[768,3840]{1,0:T(8,128)(2,1)S(1)}, bf16[768,3840]{1,0:T(8,128)(2,1)}, u32[]{:S(2)}) copy-start(bf16[768,3840]{1,0:T(8,128)(2,1)} %all-gather.6.cloned.1.call-done.up_ref) | copy-start | bytes 17694724
  175.4 109.5 %reduce-scatter.5.cloned.1.call-start = ((), (), s32[]{:S(2)}) async-start(), calls=%async_computation.6 | async-start | bytes 3686400 | tf_op jit(solution)/shard_map/reduce_scatter | solution.py:684
  175.5 22.4 %copy-start.5 = (f32[1024,768]{1,0:T(8,128)S(1)}, f32[1024,768]{1,0:T(8,128)}, u32[]{:S(2)}) copy-start(f32[1024,768]{1,0:T(8,128)} %copy-done.4) | copy-start | bytes 9437188
  205.1 5.0 %copy-start.12 = (f32[1024,768]{1,0:T(8,128)}, f32[1024,768]{1,0:T(8,128)S(1)}, u32[]{:S(2)}) copy-start(f32[1024,768]{1,0:T(8,128)S(1)} %get-tuple-element.175) | copy-start | bytes 9437188
  209.7 24.2 %collective-permute-start.9 = (bf16[2,2,96,3840]{3,2,1,0:T(8,128)(2,1)S(1)}, bf16[2,2,96,3840]{3,2,1,0:T(8,128)(2,1)}, u32[]{:S(2)}, u32[]{:S(2)}) collective-permute-start(bf16[2,2,96,3840]{3,2,1,0:T(8,128)(2,1)S(1)} %get-tuple-element.179), channel_id=1, source_target_pairs={{0,4},{4,0},{8,12},{12,8},{16,20},{20,16},{24,28},{28,24},{1,5},{5... | collective-permute-start | bytes 8847368 | tf_op jit(solution)/shard_map/ppermute | solution.py:652
  241.3 23.6 %collective-permute-start.10 = (bf16[96,768]{1,0:T(8,128)(2,1)S(1)}, bf16[96,768]{1,0:T(8,128)(2,1)S(1)}, u32[]{:S(2)}, u32[]{:S(2)}) collective-permute-start(bf16[96,768]{1,0:T(8,128)(2,1)S(1)} %get-tuple-element.189), channel_id=1, source_target_pairs={{0,2},{1,3},{2,0},{3,1},{4,6},{5,7},{6,4},{7,5},{8,10},{9,11},{10,... | collective-permute-start | bytes 442376 | tf_op jit(solution)/shard_map/ppermute | solution.py:615
  243.4 21.4 %collective-permute-start.11 = (bf16[96,768]{1,0:T(8,128)(2,1)S(1)}, bf16[96,768]{1,0:T(8,128)(2,1)S(1)}, u32[]{:S(2)}, u32[]{:S(2)}) collective-permute-start(bf16[96,768]{1,0:T(8,128)(2,1)S(1)} %get-tuple-element.188), channel_id=1, source_target_pairs={{0,1},{1,2},{2,3},{3,0},{4,5},{5,6},{6,7},{7,4},{8,9},{9,10},{10,1... | collective-permute-start | bytes 442376 | tf_op jit(solution)/shard_map/ppermute | solution.py:615
  243.4 21.5 %collective-permute-start.12 = (bf16[96,768]{1,0:T(8,128)(2,1)S(1)}, bf16[96,768]{1,0:T(8,128)(2,1)S(1)}, u32[]{:S(2)}, u32[]{:S(2)}) collective-permute-start(bf16[96,768]{1,0:T(8,128)(2,1)S(1)} %get-tuple-element.187), channel_id=1, source_target_pairs={{0,3},{1,0},{2,1},{3,2},{4,7},{5,4},{6,5},{7,6},{8,11},{9,8},{10,9... | collective-permute-start | bytes 442376 | tf_op jit(solution)/shard_map/ppermute | solution.py:615
  264.9 13.5 %copy-start.24 = (bf16[96,768]{1,0:T(8,128)(2,1)}, bf16[96,768]{1,0:T(8,128)(2,1)S(1)}, u32[]{:S(2)}) copy-start(bf16[96,768]{1,0:T(8,128)(2,1)S(1)} %collective-permute-done.10) | copy-start | bytes 442372
  264.9 13.5 %copy-start.26 = (bf16[96,768]{1,0:T(8,128)(2,1)}, bf16[96,768]{1,0:T(8,128)(2,1)S(1)}, u32[]{:S(2)}) copy-start(bf16[96,768]{1,0:T(8,128)(2,1)S(1)} %collective-permute-done.11) | copy-start | bytes 442372
  264.9 13.5 %copy-start.28 = (bf16[96,768]{1,0:T(8,128)(2,1)}, bf16[96,768]{1,0:T(8,128)(2,1)S(1)}, u32[]{:S(2)}) copy-start(bf16[96,768]{1,0:T(8,128)(2,1)S(1)} %collective-permute-done.12) | copy-start | bytes 442372
  278.4 6.5 %copy-start.19 = (bf16[4,96,1536]{2,1,0:T(8,128)(2,1)S(1)}, bf16[4,96,1536]{2,1,0:T(8,128)(2,1)}, u32[]{:S(2)}) copy-start(bf16[4,96,1536]{2,1,0:T(8,128)(2,1)} %get-tuple-element.90) | copy-start | bytes 3538948
  278.4 3.6 %collective-permute-start.14 = (bf16[4,96,1408]{2,1,0:T(8,128)(2,1)}, bf16[4,96,1408]{2,1,0:T(8,128)(2,1)S(1)}, u32[]{:S(2)}, u32[]{:S(2)}) collective-permute-start(bf16[4,96,1408]{2,1,0:T(8,128)(2,1)} %get-tuple-element.93), channel_id=1, source_target_pairs={{0,4},{4,0},{8,12},{12,8},{16,20},{20,16},{24,28},{28,24},{1,5},{5... | collective-permute-start | bytes 3244040 | tf_op jit(solution)/shard_map/ppermute | solution.py:652
  279.5 5.4 %collective-permute-start.13 = (bf16[4,96,1536]{2,1,0:T(8,128)(2,1)}, bf16[4,96,1536]{2,1,0:T(8,128)(2,1)S(1)}, u32[]{:S(2)}, u32[]{:S(2)}) collective-permute-start(bf16[4,96,1536]{2,1,0:T(8,128)(2,1)} %get-tuple-element.91), channel_id=1, source_target_pairs={{0,4},{4,0},{8,12},{12,8},{16,20},{20,16},{24,28},{28,24},{1,5},{5... | collective-permute-start | bytes 3538952 | tf_op jit(solution)/shard_map/ppermute | solution.py:652
  284.9 5.6 %copy-start.8 = (bf16[1024,768]{1,0:T(8,128)(2,1)S(1)}, bf16[1024,768]{1,0:T(8,128)(2,1)}, u32[]{:S(2)}) copy-start(bf16[1024,768]{1,0:T(8,128)(2,1)} %get-tuple-element.96.gq_ref) | copy-start | bytes 4718596
  284.9 5.6 %copy-start.9 = (bf16[1024,768]{1,0:T(8,128)(2,1)S(1)}, bf16[1024,768]{1,0:T(8,128)(2,1)}, u32[]{:S(2)}) copy-start(bf16[1024,768]{1,0:T(8,128)(2,1)} %get-tuple-element.97.gk_ref) | copy-start | bytes 4718596
  284.9 5.6 %copy-start.10 = (bf16[1024,768]{1,0:T(8,128)(2,1)S(1)}, bf16[1024,768]{1,0:T(8,128)(2,1)}, u32[]{:S(2)}) copy-start(bf16[1024,768]{1,0:T(8,128)(2,1)} %get-tuple-element.98.gv_ref) | copy-start | bytes 4718596
  285.3 13.6 %collective-permute-start.16 = (bf16[2,96,1408]{2,1,0:T(8,128)(2,1)S(1)}, bf16[2,96,1408]{2,1,0:T(8,128)(2,1)S(1)}, u32[]{:S(2)}, u32[]{:S(2)}) collective-permute-start(bf16[2,96,1408]{2,1,0:T(8,128)(2,1)S(1)} %dynamic-slice_bitcast_fusion.3), channel_id=1, source_target_pairs={{0,8},{4,12},{8,0},{12,4},{16,24},{20,28},{24,16},{28,20},{1,9},{5... | collective-permute-start | bytes 1622024 | tf_op jit(solution)/shard_map/ppermute | solution.py:652
  286.5 14.3 %collective-permute-start.15 = (bf16[2,96,1536]{2,1,0:T(8,128)(2,1)S(1)}, bf16[2,96,1536]{2,1,0:T(8,128)(2,1)S(1)}, u32[]{:S(2)}, u32[]{:S(2)}) collective-permute-start(bf16[2,96,1536]{2,1,0:T(8,128)(2,1)S(1)} %dynamic-slice_bitcast_fusion.2), channel_id=1, source_target_pairs={{0,16},{4,20},{8,24},{12,28},{16,0},{20,4},{24,8},{28,12},{1,17},{... | collective-permute-start | bytes 1769480 | tf_op jit(solution)/shard_map/ppermute | solution.py:652
  286.9 14.1 %collective-permute-start.17 = (bf16[24,3840]{1,0:T(8,128)(2,1)S(1)}, bf16[24,3840]{1,0:T(8,128)(2,1)S(1)}, u32[]{:S(2)}, u32[]{:S(2)}) collective-permute-start(bf16[24,3840]{1,0:T(8,128)(2,1)S(1)} %get-tuple-element.185), channel_id=1, source_target_pairs={{0,2},{1,3},{2,0},{3,1},{4,6},{5,7},{6,4},{7,5},{8,10},{9,11},{10,... | collective-permute-start | bytes 552968 | tf_op jit(solution)/shard_map/ppermute | solution.py:615
  287.9 15.0 %collective-permute-start.18 = (bf16[24,3840]{1,0:T(8,128)(2,1)S(1)}, bf16[24,3840]{1,0:T(8,128)(2,1)S(1)}, u32[]{:S(2)}, u32[]{:S(2)}) collective-permute-start(bf16[24,3840]{1,0:T(8,128)(2,1)S(1)} %get-tuple-element.184), channel_id=1, source_target_pairs={{0,1},{1,2},{2,3},{3,0},{4,5},{5,6},{6,7},{7,4},{8,9},{9,10},{10,1... | collective-permute-start | bytes 552968 | tf_op jit(solution)/shard_map/ppermute | solution.py:615
  290.5 15.8 %collective-permute-start.19 = (bf16[24,3840]{1,0:T(8,128)(2,1)S(1)}, bf16[24,3840]{1,0:T(8,128)(2,1)S(1)}, u32[]{:S(2)}, u32[]{:S(2)}) collective-permute-start(bf16[24,3840]{1,0:T(8,128)(2,1)S(1)} %get-tuple-element.183), channel_id=1, source_target_pairs={{0,3},{1,0},{2,1},{3,2},{4,7},{5,4},{6,5},{7,6},{8,11},{9,8},{10,9... | collective-permute-start | bytes 552968 | tf_op jit(solution)/shard_map/ppermute | solution.py:615
  298.2 9.4 %copy-start.22 = (bf16[96,768]{1,0:T(8,128)(2,1)S(1)}, bf16[96,768]{1,0:T(8,128)(2,1)}, u32[]{:S(2)}) copy-start(bf16[96,768]{1,0:T(8,128)(2,1)} %get-tuple-element.110) | copy-start | bytes 442372
  298.2 9.4 %copy-start.25 = (bf16[96,768]{1,0:T(8,128)(2,1)S(1)}, bf16[96,768]{1,0:T(8,128)(2,1)}, u32[]{:S(2)}) copy-start(bf16[96,768]{1,0:T(8,128)(2,1)} %copy-done.24) | copy-start | bytes 442372
  298.2 9.4 %copy-start.27 = (bf16[96,768]{1,0:T(8,128)(2,1)S(1)}, bf16[96,768]{1,0:T(8,128)(2,1)}, u32[]{:S(2)}) copy-start(bf16[96,768]{1,0:T(8,128)(2,1)} %copy-done.26) | copy-start | bytes 442372
  298.3 9.4 %copy-start.29 = (bf16[96,768]{1,0:T(8,128)(2,1)S(1)}, bf16[96,768]{1,0:T(8,128)(2,1)}, u32[]{:S(2)}) copy-start(bf16[96,768]{1,0:T(8,128)(2,1)} %copy-done.28) | copy-start | bytes 442372
  306.3 7.6 %collective-permute-start.21 = (bf16[96,1408]{1,0:T(8,128)(2,1)S(1)}, bf16[96,1408]{1,0:T(8,128)(2,1)S(1)}, u32[]{:S(2)}, u32[]{:S(2)}) collective-permute-start(bf16[96,1408]{1,0:T(8,128)(2,1)S(1)} %dynamic-slice_bitcast_fusion.5), channel_id=1, source_target_pairs={{0,16},{4,20},{8,24},{12,28},{16,0},{20,4},{24,8},{28,12},{1,17},{... | collective-permute-start | bytes 811016 | tf_op jit(solution)/shard_map/ppermute | solution.py:652
  308.5 7.8 %collective-permute-start.20 = (bf16[96,1536]{1,0:T(8,128)(2,1)S(1)}, bf16[96,1536]{1,0:T(8,128)(2,1)S(1)}, u32[]{:S(2)}, u32[]{:S(2)}) collective-permute-start(bf16[96,1536]{1,0:T(8,128)(2,1)S(1)} %dynamic-slice_bitcast_fusion.4), channel_id=1, source_target_pairs={{0,8},{4,12},{8,0},{12,4},{16,24},{20,28},{24,16},{28,20},{1,9},{5... | collective-permute-start | bytes 884744 | tf_op jit(solution)/shard_map/ppermute | solution.py:652
  316.4 5.0 %collective-permute-start.22 = (bf16[24,2944]{1,0:T(8,128)(2,1)S(1)}, bf16[24,2944]{1,0:T(8,128)(2,1)S(1)}, u32[]{:S(2)}, u32[]{:S(2)}) collective-permute-start(bf16[24,2944]{1,0:T(8,128)(2,1)S(1)} %get-tuple-element.190), channel_id=1, source_target_pairs={{0,2},{1,3},{2,0},{3,1},{4,6},{5,7},{6,4},{7,5},{8,10},{9,11},{10,... | collective-permute-start | bytes 423944 | tf_op jit(solution)/shard_map/ppermute | solution.py:615
  316.5 10.9 %collective-permute-start.23 = (bf16[24,2944]{1,0:T(8,128)(2,1)S(1)}, bf16[24,2944]{1,0:T(8,128)(2,1)S(1)}, u32[]{:S(2)}, u32[]{:S(2)}) collective-permute-start(bf16[24,2944]{1,0:T(8,128)(2,1)S(1)} %get-tuple-element.191), channel_id=1, source_target_pairs={{0,1},{1,2},{2,3},{3,0},{4,5},{5,6},{6,7},{7,4},{8,9},{9,10},{10,1... | collective-permute-start | bytes 423944 | tf_op jit(solution)/shard_map/ppermute | solution.py:615
  316.6 12.8 %collective-permute-start.24 = (bf16[24,2944]{1,0:T(8,128)(2,1)S(1)}, bf16[24,2944]{1,0:T(8,128)(2,1)S(1)}, u32[]{:S(2)}, u32[]{:S(2)}) collective-permute-start(bf16[24,2944]{1,0:T(8,128)(2,1)S(1)} %get-tuple-element.192), channel_id=1, source_target_pairs={{0,3},{1,0},{2,1},{3,2},{4,7},{5,4},{6,5},{7,6},{8,11},{9,8},{10,9... | collective-permute-start | bytes 423944 | tf_op jit(solution)/shard_map/ppermute | solution.py:615
  (18 other events, 41.1 us)
Sparse Core Ops, SparseCore 0:
  28.0 39.3 all-gather.3
  69.9 43.8 all-gather.5
  115.7 38.9 all-gather.7
  175.5 53.4 reduce-scatter.2
  238.2 41.7 reduce-scatter.4
